TPU v7x, 32 devices: a whole 2x2x4 slice. The times are simulated.
32 devices in a mesh: pipe: 4 (over y, core), fsdp: 4 (over z), tensor: 2 (over x).
Axes of the slice: x: 2, y: 2, z: 4, core: 2. Of those that a mesh axis runs over, the one named last changes fastest.
Arguments:
- tokens: bfloat16 [768, 4096], P('fsdp', 'tensor'), may hold values from -8 to 8
- norm_gains: float32 [4, 4096], P('pipe'), may hold values from 0.1 to 1.9
- q_blocks: bfloat16 [4, 4, 16, 256, 256], P('pipe', None, 'tensor', 'fsdp'), may hold values from -1 to 1
- k_blocks: bfloat16 [4, 4, 16, 256, 256], P('pipe', None, 'tensor', 'fsdp'), may hold values from -1 to 1
- v_blocks: bfloat16 [4, 4, 16, 256, 256], P('pipe', None, 'tensor', 'fsdp'), may hold values from -0.1875 to 0.1875
- o_blocks: bfloat16 [4, 4, 16, 256, 256], P('pipe', 'tensor', None, 'fsdp'), may hold values from -0.1875 to 0.1875
- q_rows: int32 [4, 4, 16], P('pipe', None, 'tensor'), may hold values from 0 to 15, as said below
- k_rows: int32 [4, 4, 16], P('pipe', None, 'tensor'), may hold values from 0 to 15, as said below
- v_rows: int32 [4, 4, 16], P('pipe', None, 'tensor'), may hold values from 0 to 15, as said below
- o_rows: int32 [4, 4, 16], P('pipe', 'tensor'), may hold values from 0 to 7, as said below
- mask_blocks: int32 [12, 4, 4], P('fsdp'), may hold values from 0 to 1, as said below
Outputs:
- activations: bfloat16 [4, 768, 4096], P('pipe', 'fsdp', 'tensor')
Inputs may be any that keep to these rules, and one draw needn't show every extreme that they name: `q_rows`: for each section and column block the 4 listed input blocks are distinct. `k_rows`: for each section and column block the 4 listed input blocks are distinct. `v_rows`: for each section and column block the 4 listed input blocks are distinct. `o_rows`: entries k and k2 with k // 2 == k2 // 2 name distinct head blocks of one column block. Every diagonal block mask_blocks[n, i, i] is 1.
All inputs are finite; a program needn't handle non-finite values.
Results may differ from a plain program's by a relative error of at most 0.017.
Values may be sent and summed in bfloat16 or wider, within the bound.
No kernel may reach another device: no remote copies, remote signals or barrier semaphores. Data moves between devices by JAX's collectives and lax.ppermute only.
A program may use at most 64 MiB of HBM per device.

v0:
```python
import functools

import jax
import jax.numpy as jnp
from jax import lax
from jax.experimental import pallas as pl
from jax.experimental.pallas import tpu as pltpu
from jax.sharding import PartitionSpec as P

HD = 128
MBLK = 16
ATTEND_US = 1
PROJECT_US = 1
AXES = ("pipe", "fsdp", "tensor")
VMEM_LIMIT = 24 * 1024 * 1024


def hop(value, sizes, target):
    pipe, fsdp, tensor = sizes
    pairs = []
    for p in range(pipe):
        for z in range(fsdp):
            for x in range(tensor):
                to = target(p, z, x)
                if to is not None:
                    pairs.append(((p * fsdp + z) * tensor + x, (to[0] * fsdp + to[1]) * tensor + to[2]))
    return lax.ppermute(value, AXES, pairs)


def after(value, *earlier):
    return lax.optimization_barrier((value, *earlier))[0]


def gather_weights(parts, firsts, total, sems, pos_ref):
    copies = []
    planes = len(parts) // 2
    for i, (part, first) in enumerate(zip(parts, firsts)):
        rows = part.shape[1]
        start = pl.multiple_of(pos_ref[i % planes] * rows, rows)
        copy = pltpu.make_async_copy(
            part.at[pl.ds(first, total.shape[1])], total.at[i // planes, :, pl.ds(start, rows), :], sems.at[i]
        )
        copy.start()
        copies.append(copy)
    return copies


def slot_of(block, me_ref, cols, blocks):
    half = blocks // 2
    dx = (block // half) ^ me_ref[1]
    d = ((block % half) // cols) ^ me_ref[0]
    piece = jnp.where((me_ref[0] & 1) == 1, 2 * dx + (d >> 1), (d & 2) + dx)
    return (piece * 2 + (d & 1)) * cols + block % cols


def attend_kernel(section, firsts, me_ref, list_ref, pos_ref, *rest):
    pieces, (gain_ref, allow_ref), parts = rest[:4], rest[4:6], rest[6 : 6 + len(firsts)]
    outs, (weights, normed, proj, sems) = rest[6 + len(firsts) : -4], rest[-4:]
    out_ref = outs[0]
    copies = gather_weights(parts, firsts, weights, sems, pos_ref)
    cols, (per_piece, rows, width) = out_ref.shape[0] // 2, pieces[0].shape
    blocks = 4 * per_piece
    row = me_ref[0] ^ section
    square = jnp.zeros((rows, width), jnp.float32)
    for piece in pieces:
        for t in range(per_piece):
            block = piece[t].astype(jnp.float32)
            square += block * block
    mean = jnp.sum(square, axis=-1, keepdims=True) / (blocks * width)
    inv_rms = lax.rsqrt(mean + 1e-05)
    for i, piece in enumerate(pieces):
        for t in range(per_piece):
            odd = me_ref[0] & 1
            dx = jnp.where(odd == 1, i // 2, i % 2)
            dy = jnp.where(odd == 1, i % 2, i // 2)
            place = ((me_ref[1] ^ dx) * (blocks // 2) + (me_ref[0] ^ (2 * dy + t // cols)) * cols + t % cols) * width
            gain = gain_ref[pl.ds(row, 1), pl.ds(pl.multiple_of(place, width), width)]
            normed[i * per_piece + t] = (piece[t].astype(jnp.float32) * inv_rms * gain).astype(jnp.bfloat16)
    if len(outs) > 1:
        keeper_y = (section - 1) // 2
        odd = me_ref[0] & 1
        for dy in range(2):
            for t in range(per_piece):
                place = ((keeper_y ^ dy) * per_piece + (odd ^ (t // cols)) * cols + t % cols) * width
                value = jnp.where(odd == 1, pieces[dy][t], pieces[2 * dy][t])
                outs[1][:, pl.ds(pl.multiple_of(place, width), width)] = value
    for copy in copies:
        copy.wait()
    count = weights.shape[1]
    per = count // (3 * cols)
    wide = blocks // 2
    for core in range(2):
        for kind in range(3):
            for c in range(cols):
                total = None
                for i in range(per):
                    n = (kind * per + i) * cols + c
                    where = (kind * per + i) * wide + (me_ref[0] ^ core) * cols + c
                    slot = slot_of(list_ref[row, where], me_ref, cols, blocks)
                    term = jnp.dot(normed[slot], weights[core, n], preferred_element_type=jnp.float32)
                    total = term if total is None else total + term
                proj[kind, core * cols + c] = total.astype(jnp.bfloat16)
    seq_len = allow_ref.shape[1]
    heads = [(c, pl.ds(h * HD, HD)) for c in range(2 * cols) for h in range(width // HD)]
    for n in range(allow_ref.shape[0]):
        span = pl.ds(n * seq_len, seq_len)
        scores = [
            lax.dot_general(
                proj[0, c, span, lanes],
                proj[1, c, span, lanes],
                (((1,), (1,)), ((), ())),
                preferred_element_type=jnp.float32,
            )
            for c, lanes in heads
        ]
        scores = jnp.stack(scores) * HD ** (-0.5)
        scores = jnp.where(allow_ref[n][None] > 0, scores, jnp.float32(-1e30))
        exp_scores = jnp.exp(scores - jnp.max(scores, axis=-1, keepdims=True))
        probs = (exp_scores / jnp.sum(exp_scores, axis=-1, keepdims=True)).astype(jnp.bfloat16)
        for i, (c, lanes) in enumerate(heads):
            attended = jnp.dot(probs[i], proj[2, c, span, lanes], preferred_element_type=jnp.float32)
            out_ref[c, span, lanes] = attended.astype(jnp.bfloat16)


def output_kernel(section, firsts, me_ref, list_ref, pos_ref, *rest):
    pieces, u_ref, parts = rest[:4], rest[4], rest[5 : 5 + len(firsts)]
    out_ref, weights, heads, sems, head_sems = rest[5 + len(firsts) :]
    copies = gather_weights(parts, firsts, weights, sems, pos_ref)
    per_piece = pieces[0].shape[0]
    for i, piece in enumerate(pieces):
        copy = pltpu.make_async_copy(piece, heads.at[pl.ds(i * per_piece, per_piece)], head_sems.at[i])
        copy.start()
        copies.append(copy)
    for copy in copies:
        copy.wait()
    blocks = 4 * per_piece
    cols = out_ref.shape[0] // 2
    count = weights.shape[1]
    per = count // cols
    wide = blocks // 2
    row = me_ref[0] ^ section
    for core in range(2):
        for c in range(cols):
            total = None
            for i in range(per):
                half = i // (per // 2)
                where = (i * 2 + me_ref[1]) * wide + (me_ref[0] ^ core) * cols + c
                block = list_ref[row, where] + (me_ref[1] ^ half) * wide
                slot = slot_of(block, me_ref, cols, blocks)
                term = jnp.dot(heads[slot], weights[core, i * cols + c], preferred_element_type=jnp.float32)
                total = term if total is None else total + term
            to = core * cols + c
            out_ref[to] = (u_ref[to].astype(jnp.float32) + total).astype(jnp.bfloat16)


SMEM = pl.BlockSpec(memory_space=pltpu.SMEM)
VMEM = pl.BlockSpec(memory_space=pltpu.VMEM)
ANY = pl.BlockSpec(memory_space=pl.ANY)


def hint(us):
    return pl.CostEstimate(flops=int(us * 1e9), bytes_accessed=0, transcendentals=0)


def attend(section, me, lists, pos, pieces, gains, allow, count, parts):
    cols, rows, width = pieces[0].shape
    depth = sum(part.shape[1] for part, _ in parts) // 2
    outs = [jax.ShapeDtypeStruct((cols, rows, width), jnp.bfloat16)]
    if section > 0:
        outs.append(jax.ShapeDtypeStruct((rows, 2 * cols * width), jnp.bfloat16))
    return pl.pallas_call(
        functools.partial(attend_kernel, section, tuple(first for _, first in parts)),
        out_shape=outs,
        in_specs=[SMEM] * 3 + [VMEM] * 6 + [ANY] * len(parts),
        out_specs=[VMEM] * len(outs),
        scratch_shapes=[
            pltpu.VMEM((2, count, depth, width), jnp.bfloat16),
            pltpu.VMEM((4 * cols, rows, width), jnp.bfloat16),
            pltpu.VMEM((3, cols, rows, width), jnp.bfloat16),
            pltpu.SemaphoreType.DMA((len(parts),)),
        ],
        compiler_params=pltpu.CompilerParams(vmem_limit_bytes=VMEM_LIMIT),
        cost_estimate=hint(ATTEND_US),
        name="attend",
    )(me, lists, pos, *pieces, gains, allow, *(part for part, _ in parts))


def project_out(section, me, lists, pos, pieces, u_piece, count, parts):
    cols, rows, width = u_piece.shape
    depth = sum(part.shape[1] for part, _ in parts) // 2
    return pl.pallas_call(
        functools.partial(output_kernel, section, tuple(first for _, first in parts)),
        out_shape=jax.ShapeDtypeStruct(u_piece.shape, jnp.bfloat16),
        in_specs=[SMEM] * 3 + [ANY] * 4 + [VMEM] + [ANY] * len(parts),
        out_specs=VMEM,
        scratch_shapes=[
            pltpu.VMEM((2, count, depth, width), jnp.bfloat16),
            pltpu.VMEM((4 * cols, rows, width), jnp.bfloat16),
            pltpu.SemaphoreType.DMA((len(parts),)),
            pltpu.SemaphoreType.DMA((4,)),
        ],
        compiler_params=pltpu.CompilerParams(vmem_limit_bytes=VMEM_LIMIT),
        cost_estimate=hint(PROJECT_US),
        name="project_out",
    )(me, lists, pos, *pieces, u_piece, *(part for part, _ in parts))


def body(sizes, tokens, norm_gains, q_blocks, k_blocks, v_blocks, o_blocks, q_rows, k_rows, v_rows, o_rows, mask_blocks):
    sections, fsdp, tensor = sizes
    assert sections == 4 and tensor == 2
    send = lambda value, target: hop(value, sizes, target)
    p = lax.axis_index("pipe")
    z = lax.axis_index("fsdp")
    x = lax.axis_index("tensor")
    per, cols_half, shard, width = q_blocks.shape[1:]
    oper_t, cols_all = o_blocks.shape[1:3]
    cols = cols_half // sections
    rows = tokens.shape[0]
    feats = cols_all * width

    to_x = lambda p, z, x: (p, z, 1 - x)
    to_core = lambda p, z, x: (p ^ 1, z, x)
    as_float = lambda r: r.reshape(-1).astype(jnp.float32)
    o_list = as_float(o_rows)
    packed = jnp.concatenate(
        [as_float(q_rows), as_float(k_rows), as_float(v_rows), o_list, send(o_list, to_x), norm_gains.reshape(-1)]
    )[None]
    packed = jnp.concatenate([packed, send(packed, lambda p, z, x: (p ^ 1, z, x))])
    packed = jnp.concatenate([packed, send(packed, lambda p, z, x: (p ^ 2, z, x))])
    in_end = 3 * per * cols_half
    list_end = in_end + tensor * oper_t * cols_all
    in_lists = packed[:, :in_end].astype(jnp.int32)
    out_lists = packed[:, in_end:list_end].astype(jnp.int32)
    gains = packed[:, list_end:]
    me = jnp.stack([p, x]).astype(jnp.int32)

    pair_up = fsdp == 4
    if pair_up:
        near_z = {0: 1, 3: 2}
        far_z = {0: 2, 3: 1}
        swap_z = {1: 2, 2: 1}
        back_z = {1: 0, 2: 3}
        step = lambda where: (lambda p, z, x: (p, where[z], x) if z in where else None)
        inner = (z == 1) | (z == 2)

    piece = tokens.reshape(rows, sections // 2, 2, cols, width)
    piece = lax.dynamic_index_in_dim(piece, p >> 1, 1, keepdims=False)
    piece = jnp.stack([lax.dynamic_index_in_dim(piece, (p & 1) ^ dc, 1, keepdims=False) for dc in range(2)])
    piece = jnp.transpose(piece, (0, 2, 1, 3)).reshape(2 * cols, rows, width)
    mask = mask_blocks
    if pair_up:
        odd_near = lambda p, z, x: (p, near_z[z], x) if p & 1 and z in near_z else None
        piece = jnp.where((p & 1) == 1, send(piece, odd_near), piece)
        mask = jnp.where((p & 1) == 1, send(mask, odd_near), mask)
    allow = jnp.repeat(jnp.repeat(mask, MBLK, axis=1), MBLK, axis=2).astype(jnp.float32)
    by_first = lambda p, z, x: (p ^ 2, z, x) if p & 1 else (p, z, 1 - x)
    by_second = lambda p, z, x: (p, z, 1 - x) if p & 1 else (p ^ 2, z, x)

    def share(value):
        first = send(value, by_first)
        return [value, first, send(value, by_second), send(first, by_second)]

    def in_piece(d):
        pieces = [
            lax.dynamic_slice_in_dim(w[0], (p ^ d) * cols, cols, 1).reshape(-1, shard, width)
            for w in (q_blocks, k_blocks, v_blocks)
        ]
        return jnp.concatenate(pieces, axis=0)

    own_in = in_piece(0)
    in_pieces = [None] * sections

    def exchange(group, *tie):
        moved = [
            send(after(in_piece(d), *tie) if tie else in_piece(d), lambda p, z, x: (p ^ d, z, x) if p in group else None)
            for d in (1, 2, 3)
        ]
        for s in group:
            in_pieces[s] = lax.select_n(p ^ s, own_in, *moved)
        return moved

    moved = exchange((0, 2))
    u = after(piece, *moved)
    pieces = share(u)
    o_split = o_blocks[0].reshape(oper_t, tensor, sections, cols, shard, width)
    o_own = lax.dynamic_index_in_dim(o_split, x, 1, keepdims=False)
    o_other = lax.dynamic_index_in_dim(o_split, 1 - x, 1, keepdims=False)
    o_other = send(o_other, to_x)
    o_all = after(jnp.stack([o_own, o_other]), *moved)

    def out_piece(d):
        return lax.dynamic_index_in_dim(o_all, p ^ d, 2, keepdims=False).reshape(-1, shard, width)

    o_moved = [out_piece(0)] + [send(out_piece(d), lambda p, z, x: (p ^ d, z, x)) for d in (1, 2, 3)]
    moved = exchange((1, 3), *o_moved[1:], *pieces[1:])
    out_pieces = [lax.select_n(p ^ s, *o_moved) for s in range(sections)]

    if pair_up:
        low = z < 2
        pos = jnp.where(low, jnp.array([1, 0, 2, 3]), jnp.array([2, 3, 1, 0])).astype(jnp.int32)

        def first_leg(piece, *tie):
            piece = after(piece, *tie)
            return [piece, send(piece, step(near_z)), send(piece, step(swap_z))]

        def second_leg(leg, late, *tie):
            far = send(after(leg[0], *leg[1:], *tie), step(far_z))
            return with_core(leg + [after(far, *late)]), far

        def all_legs(piece, *tie):
            leg = first_leg(piece, *tie)
            leg.append(send(leg[0], step(far_z)))
            return with_core(leg), leg[-1]
    else:
        pos = jnp.zeros((1,), jnp.int32)

        def first_leg(piece, *tie):
            return [lax.all_gather(piece, "fsdp", axis=1, tiled=True)]

        def second_leg(leg, late, *tie):
            return with_core(leg), leg[0]

        def all_legs(piece, *tie):
            leg = first_leg(piece)
            return with_core(leg), leg[0]

    def with_core(parts):
        return [(part, 0) for part in parts + [send(part, to_core) for part in parts]]

    in_count, out_count = in_pieces[0].shape[0], out_pieces[0].shape[0]

    def deliver(core):
        if not pair_up:
            return kept[core]
        return send(
            kept[core],
            lambda p, z, x: (p - (p & 1) + core, back_z[z] if p & 1 else z, x) if z in back_z else None,
        )

    kept = [None, None]
    results = [None, None]
    leg = first_leg(in_pieces[0])
    ready = after(out_pieces[0], *leg[1:])
    in_weights, last_far = second_leg(leg, moved, gains, allow, *pieces[1:])
    out_weights, out_far = all_legs(ready, *pieces[1:])
    pieces[0] = after(pieces[0], *(part for part, _ in out_weights))
    last_far = after(last_far, out_far)
    for s in range(sections):
        if s + 1 < sections:
            leg = first_leg(jnp.concatenate([in_pieces[s + 1], out_pieces[s + 1]]), last_far, u)
        if s > 0:
            pieces = share(u)
        heads, *before = attend(s, me, in_lists, pos, pieces, gains, allow, in_count, in_weights)
        if s + 1 < sections:
            parts, last_far = second_leg(leg, [], heads)
        if s > 0:
            core = (s - 1) & 1
            kept[core] = before[0] if kept[core] is None else jnp.where((p >> 1) == 0, kept[core], before[0])
        if s == sections - 1:
            results = [deliver(core) for core in range(2)]
        pieces = share(heads)
        if s == sections - 1:
            pieces[0] = after(pieces[0], *results)
        u = project_out(s, me, out_lists, pos, pieces, u, out_count, out_weights)
        if s + 1 < sections:
            in_weights, out_weights = parts, [(part, first + in_count) for part, first in parts]

    final = u
    last_core = (sections - 1) & 1
    if pair_up:
        home = lambda z, core: back_z[z] if core else z
    else:
        home = lambda z, core: z if core == last_core else None
    halves = []
    for y in range(2):

        def to_last(p, z, x, y=y):
            to = home(z, p & 1) if (p >> 1) == y and (not pair_up or z in back_z) else None
            return None if to is None else (sections - 1, to, x)

        halves.append(send(final, to_last))
    made_by = jnp.where(inner, 0, 1) if pair_up else last_core
    blocks = jnp.stack(halves).reshape(2, 2, cols, rows, width)
    blocks = jnp.where(made_by == 1, blocks[:, ::-1], blocks)
    last = jnp.transpose(blocks, (3, 0, 1, 2, 4)).reshape(rows, -1)
    result = jnp.where((p & 1) == 1, results[1], results[0])
    return jnp.where(p == sections - 1, last, result)[None]


def solution(mesh):
    placed = (
        P("fsdp", "tensor"),
        P("pipe", None),
        P("pipe", None, "tensor", "fsdp", None),
        P("pipe", None, "tensor", "fsdp", None),
        P("pipe", None, "tensor", "fsdp", None),
        P("pipe", "tensor", None, "fsdp", None),
        P("pipe", None, "tensor"),
        P("pipe", None, "tensor"),
        P("pipe", None, "tensor"),
        P("pipe", "tensor", None),
        P("fsdp", None, None),
    )
    sizes = tuple(mesh.shape[axis] for axis in AXES)
    return jax.shard_map(
        functools.partial(body, sizes),
        mesh=mesh,
        in_specs=placed,
        out_specs=P("pipe", "fsdp", "tensor"),
        check_vma=False,
    )
```

profile of v0, /device:TPU:5, one launch (start us, length us, event | category | flops | bytes accessed | tf_op | source)
XLA Modules:
  0.0 351.9 jit_solution(794675449915258194)
XLA Ops:
  2.0 2.6 reshape.122
  5.0 3.9 %collective-permute-start.3 = (bf16[4,192,256]{2,1,0:T(8,128)(2,1)S(1)}, bf16[4,192,256]{2,1,0:T(8,128)(2,1)}, u32[]{:S(2)}, u32[]{:S(2)}) collective-permute-start(bf16[4,192,256]{2,1,0:T(8,128)(2,1)S(1)} %bitcast.63), channel_id=1, source_target_pairs={{8,10},{9,11},{14,12},{15,13},{24,26},{25,27},{30,28},{31,29}} | collective-permute-start | bytes 1179656 | tf_op jit(solution)/shard_map/ppermute | solution.py:27
  13.9 1.7 collective-permute-start.5
  24.4 3.5 %collective-permute-done.7 = bf16[2,4,2,64,256]{4,3,2,0,1:T(8,128)(2,1)} collective-permute-done((bf16[2,4,2,64,256]{4,3,2,0,1:T(8,128)(2,1)S(1)}, bf16[2,4,2,64,256]{4,3,2,0,1:T(8,128)(2,1)}, u32[]{:S(2)}, u32[]{:S(2)}) %collective-permute-start.7) | collective-permute-done | bytes 524320 | tf_op jit(solution)/shard_map/ppermute | solution.py:27
  27.9 4.7 %collective-permute-start.1 = (f32[1,4256]{1,0:T(1,128)S(1)}, f32[1,4256]{1,0:T(1,128)S(1)}, u32[]{:S(2)}, u32[]{:S(2)}) collective-permute-start(f32[1,4256]{1,0:T(1,128)S(1)} %broadcast_in_dim.12), channel_id=1, source_target_pairs={{0,8},{1,9},{2,10},{3,11},{4,12},{5,13},{6,14},{7,15},{8,0},{9,1},... | collective-permute-start | bytes 51080 | tf_op jit(solution)/shard_map/ppermute | solution.py:27
  33.7 4.2 %collective-permute-done.6 = bf16[24,64,256]{2,1,0:T(8,128)(2,1)} collective-permute-done((bf16[24,64,256]{2,1,0:T(8,128)(2,1)}, bf16[24,64,256]{2,1,0:T(8,128)(2,1)}, u32[]{:S(2)}, u32[]{:S(2)}) %collective-permute-start.6) | collective-permute-done | bytes 786464 | tf_op jit(solution)/shard_map/ppermute | solution.py:27
  39.1 1.9 collective-permute-start.10
  41.2 2.7 select_select_fusion.1
  43.9 2.2 collective-permute-start.11
  46.1 1.6 collective-permute-start.12
  48.7 5.1 %collective-permute-done.10 = bf16[8,64,256]{2,1,0:T(8,128)(2,1)} collective-permute-done((bf16[8,64,256]{2,1,0:T(8,128)(2,1)S(1)}, bf16[8,64,256]{2,1,0:T(8,128)(2,1)}, u32[]{:S(2)}, u32[]{:S(2)}) %collective-permute-start.10) | collective-permute-done | bytes 262176 | tf_op jit(solution)/shard_map/ppermute | solution.py:27
  53.8 6.7 %collective-permute-done.13.rest_1_ = bf16[4,192,256]{2,1,0:T(8,128)(2,1)S(1)} collective-permute-done((bf16[4,192,256]{2,1,0:T(8,128)(2,1)S(1)}, bf16[4,192,256]{2,1,0:T(8,128)(2,1)S(1)}, u32[]{:S(2)}, u32[]{:S(2)}) %collective-permute-start.13) | collective-permute-done | bytes 393248 | tf_op jit(solution)/shard_map/ppermute | solution.py:27
  61.8 5.3 %collective-permute-done.15.rest_3_ = bf16[4,192,256]{2,1,0:T(8,128)(2,1)S(1)} collective-permute-done((bf16[4,192,256]{2,1,0:T(8,128)(2,1)S(1)}, bf16[4,192,256]{2,1,0:T(8,128)(2,1)S(1)}, u32[]{:S(2)}, u32[]{:S(2)}) %collective-permute-start.15) | collective-permute-done | bytes 393248 | tf_op jit(solution)/shard_map/ppermute | solution.py:27
  67.9 1.3 collective-permute-start.25
  69.2 2.1 collective-permute-start.26
  71.4 1.3 collective-permute-start.27
  72.7 2.1 fusion.4
  74.9 1.3 collective-permute-start.16
  78.4 1.9 collective-permute-done.16.rest_6_
  80.3 6.0 %collective-permute-start.24 = (bf16[24,64,256]{2,1,0:T(8,128)(2,1)S(1)}, bf16[24,64,256]{2,1,0:T(8,128)(2,1)}, u32[]{:S(2)}, u32[]{:S(2)}) collective-permute-start(bf16[24,64,256]{2,1,0:T(8,128)(2,1)S(1)} %get-tuple-element.33.rest_6_), channel_id=1, source_target_pairs={{0,4},{1,5},{6,2},{7,3},{8,12},{9,13},{14,10},{15,11},{16,20},{17,... | collective-permute-start | bytes 2359304 | tf_op jit(solution)/shard_map/ppermute | solution.py:27
  86.3 1.3 collective-permute-start.18
  87.6 19.5 %collective-permute-done.18.rest_8_ = bf16[8,64,256]{2,1,0:T(8,128)(2,1)S(1)} collective-permute-done((bf16[8,64,256]{2,1,0:T(8,128)(2,1)S(1)}, bf16[8,64,256]{2,1,0:T(8,128)(2,1)S(1)}, u32[]{:S(2)}, u32[]{:S(2)}) %collective-permute-start.18) | collective-permute-done | bytes 262176 | tf_op jit(solution)/shard_map/ppermute | solution.py:27
  110.1 3.8 %collective-permute-start.38 = (bf16[32,64,256]{2,1,0:T(8,128)(2,1)S(1)}, bf16[32,64,256]{2,1,0:T(8,128)(2,1)S(1)}, u32[]{:S(2)}, u32[]{:S(2)}) collective-permute-start(bf16[32,64,256]{2,1,0:T(8,128)(2,1)S(1)} %pad_maximum_fusion.1.rest_6_.rest_5_), channel_id=1, source_target_pairs={{0,2},{1,3},{6,4},{7,5},{8,10},{9,11},{14,12},{15,13},{16,18},{17,... | collective-permute-start | bytes 3145736 | tf_op jit(solution)/shard_map/ppermute | solution.py:27
  118.3 1.6 copy.24.rest_5_
  127.0 5.6 %attend.4.rest_0_ = bf16[4,192,256]{2,1,0:T(8,128)(2,1)S(1)} custom-call(s32[2]{0:T(128)S(1)} %pad_add_fusion.me_ref, s32[4,96]{1,0:T(4,128)S(1)} %maximum_convert_fusion.list_ref, s32[4]{0:T(128)S(1)} %broadcast_select_fusion.2.pos_ref, bf16[4,192,256]{2,1,0:T(8,128)(2,1)S(1)} %broadcast_select_fusion.1.rest_0_.rest_4_, ...), custom_call_target="tpu_custom_call" | custom-call | flops 1000000000 | tf_op jit(solution)/shard_map/attend/pallas_call | solution.py:171
  132.7 3.6 %collective-permute-done.38.rest_7_.rest_6_ = bf16[32,64,256]{2,1,0:T(8,128)(2,1)S(1)} collective-permute-done((bf16[32,64,256]{2,1,0:T(8,128)(2,1)S(1)}, bf16[32,64,256]{2,1,0:T(8,128)(2,1)S(1)}, u32[]{:S(2)}, u32[]{:S(2)}) %collective-permute-start.38) | collective-permute-done | bytes 1048608 | tf_op jit(solution)/shard_map/ppermute | solution.py:27
  136.3 6.7 %collective-permute-start.40 = (bf16[32,64,256]{2,1,0:T(8,128)(2,1)S(1)}, bf16[32,64,256]{2,1,0:T(8,128)(2,1)S(1)}, u32[]{:S(2)}, u32[]{:S(2)}) collective-permute-start(bf16[32,64,256]{2,1,0:T(8,128)(2,1)S(1)} %pad_maximum_fusion.1.rest_6_.rest_5_), channel_id=1, source_target_pairs={{0,4},{1,5},{6,2},{7,3},{8,12},{9,13},{14,10},{15,11},{16,20},{17,... | collective-permute-start | bytes 3145736 | tf_op jit(solution)/shard_map/ppermute | solution.py:27
  146.4 4.7 %collective-permute-done.33.rest_2_ = bf16[4,192,256]{2,1,0:T(8,128)(2,1)S(1)} collective-permute-done((bf16[4,192,256]{2,1,0:T(8,128)(2,1)S(1)}, bf16[4,192,256]{2,1,0:T(8,128)(2,1)S(1)}, u32[]{:S(2)}, u32[]{:S(2)}) %collective-permute-start.33) | collective-permute-done | bytes 393248 | tf_op jit(solution)/shard_map/ppermute | solution.py:27
  151.1 4.2 %collective-permute-done.34.rest_3_ = bf16[4,192,256]{2,1,0:T(8,128)(2,1)S(1)} collective-permute-done((bf16[4,192,256]{2,1,0:T(8,128)(2,1)S(1)}, bf16[4,192,256]{2,1,0:T(8,128)(2,1)S(1)}, u32[]{:S(2)}, u32[]{:S(2)}) %collective-permute-start.34) | collective-permute-done | bytes 393248 | tf_op jit(solution)/shard_map/ppermute | solution.py:27
  155.4 2.2 project_out.4.rest_0_.rest_4_
  158.0 6.4 %collective-permute-done.40.rest_9_.rest_8_ = bf16[32,64,256]{2,1,0:T(8,128)(2,1)S(1)} collective-permute-done((bf16[32,64,256]{2,1,0:T(8,128)(2,1)S(1)}, bf16[32,64,256]{2,1,0:T(8,128)(2,1)S(1)}, u32[]{:S(2)}, u32[]{:S(2)}) %collective-permute-start.40) | collective-permute-done | bytes 1048608 | tf_op jit(solution)/shard_map/ppermute | solution.py:27
  164.3 1.8 collective-permute-start.43
  166.9 3.6 %collective-permute-start.51 = (bf16[32,64,256]{2,1,0:T(8,128)(2,1)S(1)}, bf16[32,64,256]{2,1,0:T(8,128)(2,1)S(1)}, u32[]{:S(2)}, u32[]{:S(2)}) collective-permute-start(bf16[32,64,256]{2,1,0:T(8,128)(2,1)S(1)} %pad_maximum_fusion.2.rest_6_.rest_5_), channel_id=1, source_target_pairs={{0,2},{1,3},{6,4},{7,5},{8,10},{9,11},{14,12},{15,13},{16,18},{17,... | collective-permute-start | bytes 3145736 | tf_op jit(solution)/shard_map/ppermute | solution.py:27
  171.5 6.7 %collective-permute-done.37.rest_3_ = bf16[4,192,256]{2,1,0:T(8,128)(2,1)S(1)} collective-permute-done((bf16[4,192,256]{2,1,0:T(8,128)(2,1)S(1)}, bf16[4,192,256]{2,1,0:T(8,128)(2,1)S(1)}, u32[]{:S(2)}, u32[]{:S(2)}) %collective-permute-start.37) | collective-permute-done | bytes 393248 | tf_op jit(solution)/shard_map/ppermute | solution.py:27
  178.2 4.6 %attend.5 = (bf16[4,192,256]{2,1,0:T(8,128)(2,1)S(1)}, bf16[192,2048]{1,0:T(8,128)(2,1)S(1)}) custom-call(s32[2]{0:T(128)S(1)} %pad_add_fusion.me_ref, s32[4,96]{1,0:T(4,128)S(1)} %maximum_convert_fusion.list_ref, s32[4]{0:T(128)S(1)} %broadcast_select_fusion.2.pos_ref, bf16[4,192,256]{2,1,0:T(8,128)(2,1)S(1)} %project_out.4.rest_0_.rest_4_, ...), custom_call_target="tpu_custom_call" | custom-call | flops 1000000000 | tf_op jit(solution)/shard_map/attend/pallas_call | solution.py:171
  182.8 9.6 %collective-permute-done.51.rest_7_.rest_6_ = bf16[32,64,256]{2,1,0:T(8,128)(2,1)S(1)} collective-permute-done((bf16[32,64,256]{2,1,0:T(8,128)(2,1)S(1)}, bf16[32,64,256]{2,1,0:T(8,128)(2,1)S(1)}, u32[]{:S(2)}, u32[]{:S(2)}) %collective-permute-start.51) | collective-permute-done | bytes 1048608 | tf_op jit(solution)/shard_map/ppermute | solution.py:27
  192.4 6.5 %collective-permute-start.53 = (bf16[32,64,256]{2,1,0:T(8,128)(2,1)S(1)}, bf16[32,64,256]{2,1,0:T(8,128)(2,1)S(1)}, u32[]{:S(2)}, u32[]{:S(2)}) collective-permute-start(bf16[32,64,256]{2,1,0:T(8,128)(2,1)S(1)} %pad_maximum_fusion.2.rest_6_.rest_5_), channel_id=1, source_target_pairs={{0,4},{1,5},{6,2},{7,3},{8,12},{9,13},{14,10},{15,11},{16,20},{17,... | collective-permute-start | bytes 3145736 | tf_op jit(solution)/shard_map/ppermute | solution.py:27
  198.9 1.7 collective-permute-start.54
  202.4 8.3 %collective-permute-done.45.rest_1_ = bf16[4,192,256]{2,1,0:T(8,128)(2,1)S(1)} collective-permute-done((bf16[4,192,256]{2,1,0:T(8,128)(2,1)S(1)}, bf16[4,192,256]{2,1,0:T(8,128)(2,1)S(1)}, u32[]{:S(2)}, u32[]{:S(2)}) %collective-permute-start.45) | collective-permute-done | bytes 393248 | tf_op jit(solution)/shard_map/ppermute | solution.py:27
  210.7 1.9 collective-permute-start.56
  212.6 7.3 %collective-permute-done.53.rest_9_.rest_8_ = bf16[32,64,256]{2,1,0:T(8,128)(2,1)S(1)} collective-permute-done((bf16[32,64,256]{2,1,0:T(8,128)(2,1)S(1)}, bf16[32,64,256]{2,1,0:T(8,128)(2,1)S(1)}, u32[]{:S(2)}, u32[]{:S(2)}) %collective-permute-start.53) | collective-permute-done | bytes 1048608 | tf_op jit(solution)/shard_map/ppermute | solution.py:27
  220.3 2.1 collective-permute-start.57
  222.4 4.5 %collective-permute-done.47.rest_3_ = bf16[4,192,256]{2,1,0:T(8,128)(2,1)S(1)} collective-permute-done((bf16[4,192,256]{2,1,0:T(8,128)(2,1)S(1)}, bf16[4,192,256]{2,1,0:T(8,128)(2,1)S(1)}, u32[]{:S(2)}, u32[]{:S(2)}) %collective-permute-start.47) | collective-permute-done | bytes 393248 | tf_op jit(solution)/shard_map/ppermute | solution.py:27
  226.9 2.2 project_out.5.rest_0_.rest_4_
  229.1 4.1 %collective-permute-start.64 = (bf16[32,64,256]{2,1,0:T(8,128)(2,1)S(1)}, bf16[32,64,256]{2,1,0:T(8,128)(2,1)S(1)}, u32[]{:S(2)}, u32[]{:S(2)}) collective-permute-start(bf16[32,64,256]{2,1,0:T(8,128)(2,1)S(1)} %pad_maximum_fusion.3.rest_6_.rest_5_), channel_id=1, source_target_pairs={{0,2},{1,3},{6,4},{7,5},{8,10},{9,11},{14,12},{15,13},{16,18},{17,... | collective-permute-start | bytes 3145736 | tf_op jit(solution)/shard_map/ppermute | solution.py:27
  234.3 6.6 %collective-permute-done.48.rest_1_ = bf16[4,192,256]{2,1,0:T(8,128)(2,1)S(1)} collective-permute-done((bf16[4,192,256]{2,1,0:T(8,128)(2,1)S(1)}, bf16[4,192,256]{2,1,0:T(8,128)(2,1)S(1)}, u32[]{:S(2)}, u32[]{:S(2)}) %collective-permute-start.48) | collective-permute-done | bytes 393248 | tf_op jit(solution)/shard_map/ppermute | solution.py:27
  241.4 7.7 %collective-permute-done.50.rest_3_ = bf16[4,192,256]{2,1,0:T(8,128)(2,1)S(1)} collective-permute-done((bf16[4,192,256]{2,1,0:T(8,128)(2,1)S(1)}, bf16[4,192,256]{2,1,0:T(8,128)(2,1)S(1)}, u32[]{:S(2)}, u32[]{:S(2)}) %collective-permute-start.50) | collective-permute-done | bytes 393248 | tf_op jit(solution)/shard_map/ppermute | solution.py:27
  249.1 4.6 %attend.6 = (bf16[4,192,256]{2,1,0:T(8,128)(2,1)S(1)}, bf16[192,2048]{1,0:T(8,128)(2,1)S(1)}) custom-call(s32[2]{0:T(128)S(1)} %pad_add_fusion.me_ref, s32[4,96]{1,0:T(4,128)S(1)} %maximum_convert_fusion.list_ref, s32[4]{0:T(128)S(1)} %broadcast_select_fusion.2.pos_ref, bf16[4,192,256]{2,1,0:T(8,128)(2,1)S(1)} %project_out.5.rest_0_.rest_4_, ...), custom_call_target="tpu_custom_call" | custom-call | flops 1000000000 | tf_op jit(solution)/shard_map/attend/pallas_call | solution.py:171
  254.6 5.2 %collective-permute-start.66 = (bf16[32,64,256]{2,1,0:T(8,128)(2,1)S(1)}, bf16[32,64,256]{2,1,0:T(8,128)(2,1)}, u32[]{:S(2)}, u32[]{:S(2)}) collective-permute-start(bf16[32,64,256]{2,1,0:T(8,128)(2,1)S(1)} %pad_maximum_fusion.3.rest_6_.rest_5_), channel_id=1, source_target_pairs={{0,4},{1,5},{6,2},{7,3},{8,12},{9,13},{14,10},{15,11},{16,20},{17,... | collective-permute-start | bytes 3145736 | tf_op jit(solution)/shard_map/ppermute | solution.py:27
  260.9 5.1 %collective-permute-start.67 = (bf16[32,64,256]{2,1,0:T(8,128)(2,1)S(1)}, bf16[32,64,256]{2,1,0:T(8,128)(2,1)S(1)}, u32[]{:S(2)}, u32[]{:S(2)}) collective-permute-start(bf16[32,64,256]{2,1,0:T(8,128)(2,1)S(1)} %pad_maximum_fusion.3.rest_6_.rest_5_), channel_id=1, source_target_pairs={{0,8},{1,9},{2,10},{3,11},{4,12},{5,13},{6,14},{7,15},{8,0},{9,1},... | collective-permute-start | bytes 3145736 | tf_op jit(solution)/shard_map/ppermute | solution.py:27
  267.5 12.1 %collective-permute-start.68 = (bf16[32,64,256]{2,1,0:T(8,128)(2,1)S(1)}, bf16[32,64,256]{2,1,0:T(8,128)(2,1)}, u32[]{:S(2)}, u32[]{:S(2)}) collective-permute-start(bf16[32,64,256]{2,1,0:T(8,128)(2,1)S(1)} %collective-permute-done.64.rest_7_.rest_6_), channel_id=1, source_target_pairs={{0,8},{1,9},{2,10},{3,11},{4,12},{5,13},{6,14},{7,15},{8,0},{9,1},... | collective-permute-start | bytes 3145736 | tf_op jit(solution)/shard_map/ppermute | solution.py:27
  279.5 2.7 collective-permute-start.69
  282.2 2.2 project_out.6.rest_0_.rest_4_
  286.7 4.8 %collective-permute-done.61.rest_1_ = bf16[4,192,256]{2,1,0:T(8,128)(2,1)} collective-permute-done((bf16[4,192,256]{2,1,0:T(8,128)(2,1)S(1)}, bf16[4,192,256]{2,1,0:T(8,128)(2,1)}, u32[]{:S(2)}, u32[]{:S(2)}) %collective-permute-start.61) | collective-permute-done | bytes 393248 | tf_op jit(solution)/shard_map/ppermute | solution.py:27
  293.0 3.1 collective-permute-done.62.rest_2_
  296.1 5.5 %collective-permute-done.63.rest_3_ = bf16[4,192,256]{2,1,0:T(8,128)(2,1)} collective-permute-done((bf16[4,192,256]{2,1,0:T(8,128)(2,1)}, bf16[4,192,256]{2,1,0:T(8,128)(2,1)}, u32[]{:S(2)}, u32[]{:S(2)}) %collective-permute-start.63) | collective-permute-done | bytes 393248 | tf_op jit(solution)/shard_map/ppermute | solution.py:27
  304.6 6.1 %attend.7 = (bf16[4,192,256]{2,1,0:T(8,128)(2,1)S(1)}, bf16[192,2048]{1,0:T(8,128)(2,1)S(1)}) custom-call(s32[2]{0:T(128)S(1)} %pad_add_fusion.me_ref, s32[4,96]{1,0:T(4,128)S(1)} %maximum_convert_fusion.list_ref, s32[4]{0:T(128)S(1)} %broadcast_select_fusion.2.pos_ref, bf16[4,192,256]{2,1,0:T(8,128)(2,1)S(1)} %project_out.6.rest_0_.rest_4_, ...), custom_call_target="tpu_custom_call" | custom-call | flops 1000000000 | tf_op jit(solution)/shard_map/attend/pallas_call | solution.py:171
  312.4 6.0 %collective-permute-done.73.rest_1_ = bf16[4,192,256]{2,1,0:T(8,128)(2,1)S(1)} collective-permute-done((bf16[4,192,256]{2,1,0:T(8,128)(2,1)S(1)}, bf16[4,192,256]{2,1,0:T(8,128)(2,1)S(1)}, u32[]{:S(2)}, u32[]{:S(2)}) %collective-permute-start.73) | collective-permute-done | bytes 393248 | tf_op jit(solution)/shard_map/ppermute | solution.py:27
  319.6 9.4 %collective-permute-done.75.rest_3_ = bf16[4,192,256]{2,1,0:T(8,128)(2,1)S(1)} collective-permute-done((bf16[4,192,256]{2,1,0:T(8,128)(2,1)S(1)}, bf16[4,192,256]{2,1,0:T(8,128)(2,1)S(1)}, u32[]{:S(2)}, u32[]{:S(2)}) %collective-permute-start.75) | collective-permute-done | bytes 393248 | tf_op jit(solution)/shard_map/ppermute | solution.py:27
  329.0 3.3 project_out.7
  332.3 1.3 collective-permute-start.77
  333.6 1.3 collective-permute-start.76
  334.9 12.1 %collective-permute-done.77 = bf16[4,192,256]{2,1,0:T(8,128)(2,1)S(1)} collective-permute-done((bf16[4,192,256]{2,1,0:T(8,128)(2,1)}, bf16[4,192,256]{2,1,0:T(8,128)(2,1)S(1)}, u32[]{:S(2)}, u32[]{:S(2)}) %collective-permute-start.77) | collective-permute-done | bytes 393248 | tf_op jit(solution)/shard_map/ppermute | solution.py:27
  347.0 1.5 collective-permute-done.76
  (291 shorter events, 63.5 us)
Async XLA Ops:
  0.8 17.3 %collective-permute-start = (f32[32]{0:T(128)S(1)}, f32[32]{0:T(128)S(1)}, u32[]{:S(2)}, u32[]{:S(2)}) collective-permute-start(f32[32]{0:T(128)S(1)} %convert_element_type.44), channel_id=1, source_target_pairs={{0,1},{1,0},{2,3},{3,2},{4,5},{5,4},{6,7},{7,6},{8,9},{9,8},{10,11... | collective-permute-start | bytes 392 | tf_op jit(solution)/shard_map/ppermute | solution.py:27
  5.0 16.4 %collective-permute-start.3 = (bf16[4,192,256]{2,1,0:T(8,128)(2,1)S(1)}, bf16[4,192,256]{2,1,0:T(8,128)(2,1)}, u32[]{:S(2)}, u32[]{:S(2)}) collective-permute-start(bf16[4,192,256]{2,1,0:T(8,128)(2,1)S(1)} %bitcast.63), channel_id=1, source_target_pairs={{8,10},{9,11},{14,12},{15,13},{24,26},{25,27},{30,28},{31,29}} | collective-permute-start | bytes 1179656 | tf_op jit(solution)/shard_map/ppermute | solution.py:27
  11.6 22.1 %collective-permute-start.4 = (bf16[24,64,256]{2,1,0:T(8,128)(2,1)}, bf16[24,64,256]{2,1,0:T(8,128)(2,1)}, u32[]{:S(2)}, u32[]{:S(2)}) collective-permute-start(bf16[24,64,256]{2,1,0:T(8,128)(2,1)} %pad_maximum_fusion.4), channel_id=1, source_target_pairs={{0,8},{1,9},{2,10},{3,11},{4,12},{5,13},{6,14},{7,15},{16,24},{17,... | collective-permute-start | bytes 2359304 | tf_op jit(solution)/shard_map/ppermute | solution.py:27
  13.9 19.8 %collective-permute-start.5 = (bf16[24,64,256]{2,1,0:T(8,128)(2,1)}, bf16[24,64,256]{2,1,0:T(8,128)(2,1)}, u32[]{:S(2)}, u32[]{:S(2)}) collective-permute-start(bf16[24,64,256]{2,1,0:T(8,128)(2,1)} %pad_maximum_fusion.5), channel_id=1, source_target_pairs={{0,16},{1,17},{2,18},{3,19},{4,20},{5,21},{6,22},{7,23},{16,0},{17... | collective-permute-start | bytes 2359304 | tf_op jit(solution)/shard_map/ppermute | solution.py:27
  16.6 21.4 %collective-permute-start.6 = (bf16[24,64,256]{2,1,0:T(8,128)(2,1)}, bf16[24,64,256]{2,1,0:T(8,128)(2,1)}, u32[]{:S(2)}, u32[]{:S(2)}) collective-permute-start(bf16[24,64,256]{2,1,0:T(8,128)(2,1)} %pad_maximum_fusion.6), channel_id=1, source_target_pairs={{0,24},{1,25},{2,26},{3,27},{4,28},{5,29},{6,30},{7,31},{16,8},{17... | collective-permute-start | bytes 2359304 | tf_op jit(solution)/shard_map/ppermute | solution.py:27
  18.1 9.8 %collective-permute-start.7 = (bf16[2,4,2,64,256]{4,3,2,0,1:T(8,128)(2,1)S(1)}, bf16[2,4,2,64,256]{4,3,2,0,1:T(8,128)(2,1)}, u32[]{:S(2)}, u32[]{:S(2)}) collective-permute-start(bf16[2,4,2,64,256]{4,3,2,0,1:T(8,128)(2,1)S(1)} %bitcast.74), channel_id=1, source_target_pairs={{0,1},{1,0},{2,3},{3,2},{4,5},{5,4},{6,7},{7,6},{8,9},{9,8},{10,11... | collective-permute-start | bytes 1572872 | tf_op jit(solution)/shard_map/ppermute | solution.py:27
  22.0 19.0 %collective-permute-start.23 = (s32[3,4,4]{2,1,0:T(4,128)S(1)}, s32[3,4,4]{2,1,0:T(4,128)S(1)}, u32[]{:S(2)}, u32[]{:S(2)}) collective-permute-start(s32[3,4,4]{2,1,0:T(4,128)S(1)} %copy-done.65), channel_id=1, source_target_pairs={{8,10},{9,11},{14,12},{15,13},{24,26},{25,27},{30,28},{31,29}} | collective-permute-start | bytes 584 | tf_op jit(solution)/shard_map/ppermute | solution.py:27
  27.9 16.1 %collective-permute-start.1 = (f32[1,4256]{1,0:T(1,128)S(1)}, f32[1,4256]{1,0:T(1,128)S(1)}, u32[]{:S(2)}, u32[]{:S(2)}) collective-permute-start(f32[1,4256]{1,0:T(1,128)S(1)} %broadcast_in_dim.12), channel_id=1, source_target_pairs={{0,8},{1,9},{2,10},{3,11},{4,12},{5,13},{6,14},{7,15},{8,0},{9,1},... | collective-permute-start | bytes 51080 | tf_op jit(solution)/shard_map/ppermute | solution.py:27
  38.8 7.3 %collective-permute-start.8 = (bf16[8,64,256]{2,1,0:T(8,128)(2,1)S(1)}, bf16[8,64,256]{2,1,0:T(8,128)(2,1)S(1)}, u32[]{:S(2)}, u32[]{:S(2)}) collective-permute-start(bf16[8,64,256]{2,1,0:T(8,128)(2,1)S(1)} %bitcast.79), channel_id=1, source_target_pairs={{0,8},{1,9},{2,10},{3,11},{4,12},{5,13},{6,14},{7,15},{8,0},{9,1},... | collective-permute-start | bytes 786440 | tf_op jit(solution)/shard_map/ppermute | solution.py:27
  38.9 9.1 %collective-permute-start.9 = (bf16[8,64,256]{2,1,0:T(8,128)(2,1)}, bf16[8,64,256]{2,1,0:T(8,128)(2,1)S(1)}, u32[]{:S(2)}, u32[]{:S(2)}) collective-permute-start(bf16[8,64,256]{2,1,0:T(8,128)(2,1)} %bitcast.22), channel_id=1, source_target_pairs={{0,16},{1,17},{2,18},{3,19},{4,20},{5,21},{6,22},{7,23},{8,24},{9,... | collective-permute-start | bytes 786440 | tf_op jit(solution)/shard_map/ppermute | solution.py:27
  39.1 14.7 %collective-permute-start.10 = (bf16[8,64,256]{2,1,0:T(8,128)(2,1)S(1)}, bf16[8,64,256]{2,1,0:T(8,128)(2,1)}, u32[]{:S(2)}, u32[]{:S(2)}) collective-permute-start(bf16[8,64,256]{2,1,0:T(8,128)(2,1)S(1)} %bitcast.78), channel_id=1, source_target_pairs={{0,24},{1,25},{2,26},{3,27},{4,28},{5,29},{6,30},{7,31},{8,16},{9,... | collective-permute-start | bytes 786440 | tf_op jit(solution)/shard_map/ppermute | solution.py:27
  41.0 19.5 %collective-permute-start.13 = (bf16[4,192,256]{2,1,0:T(8,128)(2,1)S(1)}, bf16[4,192,256]{2,1,0:T(8,128)(2,1)S(1)}, u32[]{:S(2)}, u32[]{:S(2)}) collective-permute-start(bf16[4,192,256]{2,1,0:T(8,128)(2,1)S(1)} %broadcast_select_fusion.1.rest_0_.rest_4_), channel_id=1, source_target_pairs={{0,1},{1,0},{2,3},{3,2},{4,5},{5,4},{6,7},{7,6},{8,24},{9,25},{10,... | collective-permute-start | bytes 1179656 | tf_op jit(solution)/shard_map/ppermute | solution.py:27
  43.9 25.3 %collective-permute-start.11 = (bf16[24,64,256]{2,1,0:T(8,128)(2,1)S(1)}, bf16[24,64,256]{2,1,0:T(8,128)(2,1)}, u32[]{:S(2)}, u32[]{:S(2)}) collective-permute-start(bf16[24,64,256]{2,1,0:T(8,128)(2,1)S(1)} %get-tuple-element.33.rest_6_), channel_id=1, source_target_pairs={{0,2},{1,3},{6,4},{7,5},{8,10},{9,11},{14,12},{15,13},{16,18},{17,... | collective-permute-start | bytes 2359304 | tf_op jit(solution)/shard_map/ppermute | solution.py:27
  46.1 25.2 %collective-permute-start.12 = (bf16[24,64,256]{2,1,0:T(8,128)(2,1)S(1)}, bf16[24,64,256]{2,1,0:T(8,128)(2,1)}, u32[]{:S(2)}, u32[]{:S(2)}) collective-permute-start(bf16[24,64,256]{2,1,0:T(8,128)(2,1)S(1)} %get-tuple-element.33.rest_6_), channel_id=1, source_target_pairs={{2,4},{3,5},{4,2},{5,3},{10,12},{11,13},{12,10},{13,11},{18,20},{1... | collective-permute-start | bytes 2359304 | tf_op jit(solution)/shard_map/ppermute | solution.py:27
  48.0 13.5 %collective-permute-start.14 = (bf16[4,192,256]{2,1,0:T(8,128)(2,1)S(1)}, bf16[4,192,256]{2,1,0:T(8,128)(2,1)S(1)}, u32[]{:S(2)}, u32[]{:S(2)}) collective-permute-start(bf16[4,192,256]{2,1,0:T(8,128)(2,1)S(1)} %broadcast_select_fusion.1.rest_0_.rest_4_), channel_id=1, source_target_pairs={{0,16},{1,17},{2,18},{3,19},{4,20},{5,21},{6,22},{7,23},{8,9},{9,8... | collective-permute-start | bytes 1179656 | tf_op jit(solution)/shard_map/ppermute | solution.py:27
  53.8 22.4 %collective-permute-start.28 = (bf16[24,64,256]{2,1,0:T(8,128)(2,1)S(1)}, bf16[24,64,256]{2,1,0:T(8,128)(2,1)S(1)}, u32[]{:S(2)}, u32[]{:S(2)}) collective-permute-start(bf16[24,64,256]{2,1,0:T(8,128)(2,1)S(1)} %get-tuple-element.33.rest_6_), channel_id=1, source_target_pairs={{0,8},{1,9},{2,10},{3,11},{4,12},{5,13},{6,14},{7,15},{8,0},{9,1},... | collective-permute-start | bytes 2359304 | tf_op jit(solution)/shard_map/ppermute | solution.py:27
  61.5 13.4 %collective-permute-start.2 = (f32[2,4256]{1,0:T(2,128)S(1)}, f32[2,4256]{1,0:T(2,128)S(1)}, u32[]{:S(2)}, u32[]{:S(2)}) collective-permute-start(f32[2,4256]{1,0:T(2,128)S(1)} %pad_maximum_fusion.12), channel_id=1, source_target_pairs={{0,16},{1,17},{2,18},{3,19},{4,20},{5,21},{6,22},{7,23},{8,24},{9,... | collective-permute-start | bytes 102152 | tf_op jit(solution)/shard_map/ppermute | solution.py:27
  67.9 39.3 %collective-permute-start.25 = (bf16[24,64,256]{2,1,0:T(8,128)(2,1)}, bf16[24,64,256]{2,1,0:T(8,128)(2,1)S(1)}, u32[]{:S(2)}, u32[]{:S(2)}) collective-permute-start(bf16[24,64,256]{2,1,0:T(8,128)(2,1)} %pad_maximum_fusion.4), channel_id=1, source_target_pairs={{8,0},{9,1},{10,2},{11,3},{12,4},{13,5},{14,6},{15,7},{24,16},{25,... | collective-permute-start | bytes 2359304 | tf_op jit(solution)/shard_map/ppermute | solution.py:27
  69.2 38.4 %collective-permute-start.26 = (bf16[24,64,256]{2,1,0:T(8,128)(2,1)}, bf16[24,64,256]{2,1,0:T(8,128)(2,1)S(1)}, u32[]{:S(2)}, u32[]{:S(2)}) collective-permute-start(bf16[24,64,256]{2,1,0:T(8,128)(2,1)} %pad_maximum_fusion.5), channel_id=1, source_target_pairs={{8,24},{9,25},{10,26},{11,27},{12,28},{13,29},{14,30},{15,31},{24,... | collective-permute-start | bytes 2359304 | tf_op jit(solution)/shard_map/ppermute | solution.py:27
  71.4 36.4 %collective-permute-start.27 = (bf16[24,64,256]{2,1,0:T(8,128)(2,1)}, bf16[24,64,256]{2,1,0:T(8,128)(2,1)S(1)}, u32[]{:S(2)}, u32[]{:S(2)}) collective-permute-start(bf16[24,64,256]{2,1,0:T(8,128)(2,1)} %pad_maximum_fusion.6), channel_id=1, source_target_pairs={{8,16},{9,17},{10,18},{11,19},{12,20},{13,21},{14,22},{15,23},{24,... | collective-permute-start | bytes 2359304 | tf_op jit(solution)/shard_map/ppermute | solution.py:27
  76.2 10.1 %collective-permute-start.17 = (bf16[8,64,256]{2,1,0:T(8,128)(2,1)S(1)}, bf16[8,64,256]{2,1,0:T(8,128)(2,1)S(1)}, u32[]{:S(2)}, u32[]{:S(2)}) collective-permute-start(bf16[8,64,256]{2,1,0:T(8,128)(2,1)S(1)} %get-tuple-element.31.rest_5_), channel_id=1, source_target_pairs={{2,4},{3,5},{4,2},{5,3},{10,12},{11,13},{12,10},{13,11},{18,20},{1... | collective-permute-start | bytes 786440 | tf_op jit(solution)/shard_map/ppermute | solution.py:27
  80.3 33.6 %collective-permute-start.24 = (bf16[24,64,256]{2,1,0:T(8,128)(2,1)S(1)}, bf16[24,64,256]{2,1,0:T(8,128)(2,1)}, u32[]{:S(2)}, u32[]{:S(2)}) collective-permute-start(bf16[24,64,256]{2,1,0:T(8,128)(2,1)S(1)} %get-tuple-element.33.rest_6_), channel_id=1, source_target_pairs={{0,4},{1,5},{6,2},{7,3},{8,12},{9,13},{14,10},{15,11},{16,20},{17,... | collective-permute-start | bytes 2359304 | tf_op jit(solution)/shard_map/ppermute | solution.py:27
  86.3 20.8 %collective-permute-start.18 = (bf16[8,64,256]{2,1,0:T(8,128)(2,1)S(1)}, bf16[8,64,256]{2,1,0:T(8,128)(2,1)S(1)}, u32[]{:S(2)}, u32[]{:S(2)}) collective-permute-start(bf16[8,64,256]{2,1,0:T(8,128)(2,1)S(1)} %get-tuple-element.31.rest_5_), channel_id=1, source_target_pairs={{0,4},{1,5},{6,2},{7,3},{8,12},{9,13},{14,10},{15,11},{16,20},{17,... | collective-permute-start | bytes 786440 | tf_op jit(solution)/shard_map/ppermute | solution.py:27
  107.1 7.5 %collective-permute-start.20 = (bf16[8,64,256]{2,1,0:T(8,128)(2,1)S(1)}, bf16[8,64,256]{2,1,0:T(8,128)(2,1)S(1)}, u32[]{:S(2)}, u32[]{:S(2)}) collective-permute-start(bf16[8,64,256]{2,1,0:T(8,128)(2,1)S(1)} %collective-permute-done.16.rest_6_), channel_id=1, source_target_pairs={{0,8},{1,9},{2,10},{3,11},{4,12},{5,13},{6,14},{7,15},{8,0},{9,1},... | collective-permute-start | bytes 786440 | tf_op jit(solution)/shard_map/ppermute | solution.py:27
  107.7 8.1 %collective-permute-start.21 = (bf16[8,64,256]{2,1,0:T(8,128)(2,1)S(1)}, bf16[8,64,256]{2,1,0:T(8,128)(2,1)S(1)}, u32[]{:S(2)}, u32[]{:S(2)}) collective-permute-start(bf16[8,64,256]{2,1,0:T(8,128)(2,1)S(1)} %collective-permute-done.17.rest_7_), channel_id=1, source_target_pairs={{0,8},{1,9},{2,10},{3,11},{4,12},{5,13},{6,14},{7,15},{8,0},{9,1},... | collective-permute-start | bytes 786440 | tf_op jit(solution)/shard_map/ppermute | solution.py:27
  107.7 8.9 %collective-permute-start.22 = (bf16[8,64,256]{2,1,0:T(8,128)(2,1)S(1)}, bf16[8,64,256]{2,1,0:T(8,128)(2,1)S(1)}, u32[]{:S(2)}, u32[]{:S(2)}) collective-permute-start(bf16[8,64,256]{2,1,0:T(8,128)(2,1)S(1)} %collective-permute-done.18.rest_8_), channel_id=1, source_target_pairs={{0,8},{1,9},{2,10},{3,11},{4,12},{5,13},{6,14},{7,15},{8,0},{9,1},... | collective-permute-start | bytes 786440 | tf_op jit(solution)/shard_map/ppermute | solution.py:27
  110.1 26.2 %collective-permute-start.38 = (bf16[32,64,256]{2,1,0:T(8,128)(2,1)S(1)}, bf16[32,64,256]{2,1,0:T(8,128)(2,1)S(1)}, u32[]{:S(2)}, u32[]{:S(2)}) collective-permute-start(bf16[32,64,256]{2,1,0:T(8,128)(2,1)S(1)} %pad_maximum_fusion.1.rest_6_.rest_5_), channel_id=1, source_target_pairs={{0,2},{1,3},{6,4},{7,5},{8,10},{9,11},{14,12},{15,13},{16,18},{17,... | collective-permute-start | bytes 3145736 | tf_op jit(solution)/shard_map/ppermute | solution.py:27
  113.9 22.4 %collective-permute-start.39 = (bf16[32,64,256]{2,1,0:T(8,128)(2,1)S(1)}, bf16[32,64,256]{2,1,0:T(8,128)(2,1)S(1)}, u32[]{:S(2)}, u32[]{:S(2)}) collective-permute-start(bf16[32,64,256]{2,1,0:T(8,128)(2,1)S(1)} %pad_maximum_fusion.1.rest_6_.rest_5_), channel_id=1, source_target_pairs={{2,4},{3,5},{4,2},{5,3},{10,12},{11,13},{12,10},{13,11},{18,20},{1... | collective-permute-start | bytes 3145736 | tf_op jit(solution)/shard_map/ppermute | solution.py:27
  132.6 11.8 %collective-permute-start.32 = (bf16[4,192,256]{2,1,0:T(8,128)(2,1)S(1)}, bf16[4,192,256]{2,1,0:T(8,128)(2,1)S(1)}, u32[]{:S(2)}, u32[]{:S(2)}) collective-permute-start(bf16[4,192,256]{2,1,0:T(8,128)(2,1)S(1)} %attend.4.rest_0_), channel_id=1, source_target_pairs={{0,1},{1,0},{2,3},{3,2},{4,5},{5,4},{6,7},{7,6},{8,24},{9,25},{10,... | collective-permute-start | bytes 1179656 | tf_op jit(solution)/shard_map/ppermute | solution.py:27
  136.3 28.0 %collective-permute-start.40 = (bf16[32,64,256]{2,1,0:T(8,128)(2,1)S(1)}, bf16[32,64,256]{2,1,0:T(8,128)(2,1)S(1)}, u32[]{:S(2)}, u32[]{:S(2)}) collective-permute-start(bf16[32,64,256]{2,1,0:T(8,128)(2,1)S(1)} %pad_maximum_fusion.1.rest_6_.rest_5_), channel_id=1, source_target_pairs={{0,4},{1,5},{6,2},{7,3},{8,12},{9,13},{14,10},{15,11},{16,20},{17,... | collective-permute-start | bytes 3145736 | tf_op jit(solution)/shard_map/ppermute | solution.py:27
  143.0 23.1 %collective-permute-start.41 = (bf16[32,64,256]{2,1,0:T(8,128)(2,1)S(1)}, bf16[32,64,256]{2,1,0:T(8,128)(2,1)S(1)}, u32[]{:S(2)}, u32[]{:S(2)}) collective-permute-start(bf16[32,64,256]{2,1,0:T(8,128)(2,1)S(1)} %pad_maximum_fusion.1.rest_6_.rest_5_), channel_id=1, source_target_pairs={{0,8},{1,9},{2,10},{3,11},{4,12},{5,13},{6,14},{7,15},{8,0},{9,1},... | collective-permute-start | bytes 3145736 | tf_op jit(solution)/shard_map/ppermute | solution.py:27
  144.4 10.9 %collective-permute-start.34 = (bf16[4,192,256]{2,1,0:T(8,128)(2,1)S(1)}, bf16[4,192,256]{2,1,0:T(8,128)(2,1)S(1)}, u32[]{:S(2)}, u32[]{:S(2)}) collective-permute-start(bf16[4,192,256]{2,1,0:T(8,128)(2,1)S(1)} %collective-permute-done.32.rest_1_), channel_id=1, source_target_pairs={{0,16},{1,17},{2,18},{3,19},{4,20},{5,21},{6,22},{7,23},{8,9},{9,8... | collective-permute-start | bytes 1179656 | tf_op jit(solution)/shard_map/ppermute | solution.py:27
  145.8 25.5 %collective-permute-start.42 = (bf16[32,64,256]{2,1,0:T(8,128)(2,1)S(1)}, bf16[32,64,256]{2,1,0:T(8,128)(2,1)S(1)}, u32[]{:S(2)}, u32[]{:S(2)}) collective-permute-start(bf16[32,64,256]{2,1,0:T(8,128)(2,1)S(1)} %collective-permute-done.38.rest_7_.rest_6_), channel_id=1, source_target_pairs={{0,8},{1,9},{2,10},{3,11},{4,12},{5,13},{6,14},{7,15},{8,0},{9,1},... | collective-permute-start | bytes 3145736 | tf_op jit(solution)/shard_map/ppermute | solution.py:27
  157.6 9.3 %collective-permute-start.35 = (bf16[4,192,256]{2,1,0:T(8,128)(2,1)S(1)}, bf16[4,192,256]{2,1,0:T(8,128)(2,1)S(1)}, u32[]{:S(2)}, u32[]{:S(2)}) collective-permute-start(bf16[4,192,256]{2,1,0:T(8,128)(2,1)S(1)} %project_out.4.rest_0_.rest_4_), channel_id=1, source_target_pairs={{0,1},{1,0},{2,3},{3,2},{4,5},{5,4},{6,7},{7,6},{8,24},{9,25},{10,... | collective-permute-start | bytes 1179656 | tf_op jit(solution)/shard_map/ppermute | solution.py:27
  157.7 12.8 %collective-permute-start.36 = (bf16[4,192,256]{2,1,0:T(8,128)(2,1)S(1)}, bf16[4,192,256]{2,1,0:T(8,128)(2,1)S(1)}, u32[]{:S(2)}, u32[]{:S(2)}) collective-permute-start(bf16[4,192,256]{2,1,0:T(8,128)(2,1)S(1)} %project_out.4.rest_0_.rest_4_), channel_id=1, source_target_pairs={{0,16},{1,17},{2,18},{3,19},{4,20},{5,21},{6,22},{7,23},{8,9},{9,8... | collective-permute-start | bytes 1179656 | tf_op jit(solution)/shard_map/ppermute | solution.py:27
  166.1 12.1 %collective-permute-start.44 = (bf16[32,64,256]{2,1,0:T(8,128)(2,1)S(1)}, bf16[32,64,256]{2,1,0:T(8,128)(2,1)S(1)}, u32[]{:S(2)}, u32[]{:S(2)}) collective-permute-start(bf16[32,64,256]{2,1,0:T(8,128)(2,1)S(1)} %collective-permute-done.40.rest_9_.rest_8_), channel_id=1, source_target_pairs={{0,8},{1,9},{2,10},{3,11},{4,12},{5,13},{6,14},{7,15},{8,0},{9,1},... | collective-permute-start | bytes 3145736 | tf_op jit(solution)/shard_map/ppermute | solution.py:27
  166.9 25.5 %collective-permute-start.51 = (bf16[32,64,256]{2,1,0:T(8,128)(2,1)S(1)}, bf16[32,64,256]{2,1,0:T(8,128)(2,1)S(1)}, u32[]{:S(2)}, u32[]{:S(2)}) collective-permute-start(bf16[32,64,256]{2,1,0:T(8,128)(2,1)S(1)} %pad_maximum_fusion.2.rest_6_.rest_5_), channel_id=1, source_target_pairs={{0,2},{1,3},{6,4},{7,5},{8,10},{9,11},{14,12},{15,13},{16,18},{17,... | collective-permute-start | bytes 3145736 | tf_op jit(solution)/shard_map/ppermute | solution.py:27
  170.5 21.9 %collective-permute-start.52 = (bf16[32,64,256]{2,1,0:T(8,128)(2,1)S(1)}, bf16[32,64,256]{2,1,0:T(8,128)(2,1)S(1)}, u32[]{:S(2)}, u32[]{:S(2)}) collective-permute-start(bf16[32,64,256]{2,1,0:T(8,128)(2,1)S(1)} %pad_maximum_fusion.2.rest_6_.rest_5_), channel_id=1, source_target_pairs={{2,4},{3,5},{4,2},{5,3},{10,12},{11,13},{12,10},{13,11},{18,20},{1... | collective-permute-start | bytes 3145736 | tf_op jit(solution)/shard_map/ppermute | solution.py:27
  192.4 27.5 %collective-permute-start.53 = (bf16[32,64,256]{2,1,0:T(8,128)(2,1)S(1)}, bf16[32,64,256]{2,1,0:T(8,128)(2,1)S(1)}, u32[]{:S(2)}, u32[]{:S(2)}) collective-permute-start(bf16[32,64,256]{2,1,0:T(8,128)(2,1)S(1)} %pad_maximum_fusion.2.rest_6_.rest_5_), channel_id=1, source_target_pairs={{0,4},{1,5},{6,2},{7,3},{8,12},{9,13},{14,10},{15,11},{16,20},{17,... | collective-permute-start | bytes 3145736 | tf_op jit(solution)/shard_map/ppermute | solution.py:27
  198.9 34.2 %collective-permute-start.54 = (bf16[32,64,256]{2,1,0:T(8,128)(2,1)S(1)}, bf16[32,64,256]{2,1,0:T(8,128)(2,1)S(1)}, u32[]{:S(2)}, u32[]{:S(2)}) collective-permute-start(bf16[32,64,256]{2,1,0:T(8,128)(2,1)S(1)} %pad_maximum_fusion.2.rest_6_.rest_5_), channel_id=1, source_target_pairs={{0,8},{1,9},{2,10},{3,11},{4,12},{5,13},{6,14},{7,15},{8,0},{9,1},... | collective-permute-start | bytes 3145736 | tf_op jit(solution)/shard_map/ppermute | solution.py:27
  200.6 10.1 %collective-permute-start.45 = (bf16[4,192,256]{2,1,0:T(8,128)(2,1)S(1)}, bf16[4,192,256]{2,1,0:T(8,128)(2,1)S(1)}, u32[]{:S(2)}, u32[]{:S(2)}) collective-permute-start(bf16[4,192,256]{2,1,0:T(8,128)(2,1)S(1)} %get-tuple-element.40.rest_0_), channel_id=1, source_target_pairs={{0,1},{1,0},{2,3},{3,2},{4,5},{5,4},{6,7},{7,6},{8,24},{9,25},{10,... | collective-permute-start | bytes 1179656 | tf_op jit(solution)/shard_map/ppermute | solution.py:27
  200.6 33.3 %collective-permute-start.55 = (bf16[32,64,256]{2,1,0:T(8,128)(2,1)S(1)}, bf16[32,64,256]{2,1,0:T(8,128)(2,1)S(1)}, u32[]{:S(2)}, u32[]{:S(2)}) collective-permute-start(bf16[32,64,256]{2,1,0:T(8,128)(2,1)S(1)} %collective-permute-done.51.rest_7_.rest_6_), channel_id=1, source_target_pairs={{0,8},{1,9},{2,10},{3,11},{4,12},{5,13},{6,14},{7,15},{8,0},{9,1},... | collective-permute-start | bytes 3145736 | tf_op jit(solution)/shard_map/ppermute | solution.py:27
  201.1 19.1 %collective-permute-start.46 = (bf16[4,192,256]{2,1,0:T(8,128)(2,1)S(1)}, bf16[4,192,256]{2,1,0:T(8,128)(2,1)S(1)}, u32[]{:S(2)}, u32[]{:S(2)}) collective-permute-start(bf16[4,192,256]{2,1,0:T(8,128)(2,1)S(1)} %get-tuple-element.40.rest_0_), channel_id=1, source_target_pairs={{0,16},{1,17},{2,18},{3,19},{4,20},{5,21},{6,22},{7,23},{8,9},{9,8... | collective-permute-start | bytes 1179656 | tf_op jit(solution)/shard_map/ppermute | solution.py:27
  210.7 23.3 %collective-permute-start.56 = (bf16[32,64,256]{2,1,0:T(8,128)(2,1)S(1)}, bf16[32,64,256]{2,1,0:T(8,128)(2,1)S(1)}, u32[]{:S(2)}, u32[]{:S(2)}) collective-permute-start(bf16[32,64,256]{2,1,0:T(8,128)(2,1)S(1)} %collective-permute-done.52.rest_8_.rest_7_), channel_id=1, source_target_pairs={{0,8},{1,9},{2,10},{3,11},{4,12},{5,13},{6,14},{7,15},{8,0},{9,1},... | collective-permute-start | bytes 3145736 | tf_op jit(solution)/shard_map/ppermute | solution.py:27
  220.3 28.9 %collective-permute-start.57 = (bf16[32,64,256]{2,1,0:T(8,128)(2,1)S(1)}, bf16[32,64,256]{2,1,0:T(8,128)(2,1)S(1)}, u32[]{:S(2)}, u32[]{:S(2)}) collective-permute-start(bf16[32,64,256]{2,1,0:T(8,128)(2,1)S(1)} %collective-permute-done.53.rest_9_.rest_8_), channel_id=1, source_target_pairs={{0,8},{1,9},{2,10},{3,11},{4,12},{5,13},{6,14},{7,15},{8,0},{9,1},... | collective-permute-start | bytes 3145736 | tf_op jit(solution)/shard_map/ppermute | solution.py:27
  229.1 25.5 %collective-permute-start.64 = (bf16[32,64,256]{2,1,0:T(8,128)(2,1)S(1)}, bf16[32,64,256]{2,1,0:T(8,128)(2,1)S(1)}, u32[]{:S(2)}, u32[]{:S(2)}) collective-permute-start(bf16[32,64,256]{2,1,0:T(8,128)(2,1)S(1)} %pad_maximum_fusion.3.rest_6_.rest_5_), channel_id=1, source_target_pairs={{0,2},{1,3},{6,4},{7,5},{8,10},{9,11},{14,12},{15,13},{16,18},{17,... | collective-permute-start | bytes 3145736 | tf_op jit(solution)/shard_map/ppermute | solution.py:27
  233.2 21.4 %collective-permute-start.65 = (bf16[32,64,256]{2,1,0:T(8,128)(2,1)S(1)}, bf16[32,64,256]{2,1,0:T(8,128)(2,1)S(1)}, u32[]{:S(2)}, u32[]{:S(2)}) collective-permute-start(bf16[32,64,256]{2,1,0:T(8,128)(2,1)S(1)} %pad_maximum_fusion.3.rest_6_.rest_5_), channel_id=1, source_target_pairs={{2,4},{3,5},{4,2},{5,3},{10,12},{11,13},{12,10},{13,11},{18,20},{1... | collective-permute-start | bytes 3145736 | tf_op jit(solution)/shard_map/ppermute | solution.py:27
  234.0 7.4 %collective-permute-start.49 = (bf16[4,192,256]{2,1,0:T(8,128)(2,1)S(1)}, bf16[4,192,256]{2,1,0:T(8,128)(2,1)S(1)}, u32[]{:S(2)}, u32[]{:S(2)}) collective-permute-start(bf16[4,192,256]{2,1,0:T(8,128)(2,1)S(1)} %project_out.5.rest_0_.rest_4_), channel_id=1, source_target_pairs={{0,16},{1,17},{2,18},{3,19},{4,20},{5,21},{6,22},{7,23},{8,9},{9,8... | collective-permute-start | bytes 1179656 | tf_op jit(solution)/shard_map/ppermute | solution.py:27
  240.9 8.2 %collective-permute-start.50 = (bf16[4,192,256]{2,1,0:T(8,128)(2,1)S(1)}, bf16[4,192,256]{2,1,0:T(8,128)(2,1)S(1)}, u32[]{:S(2)}, u32[]{:S(2)}) collective-permute-start(bf16[4,192,256]{2,1,0:T(8,128)(2,1)S(1)} %collective-permute-done.48.rest_1_), channel_id=1, source_target_pairs={{0,16},{1,17},{2,18},{3,19},{4,20},{5,21},{6,22},{7,23},{8,9},{9,8... | collective-permute-start | bytes 1179656 | tf_op jit(solution)/shard_map/ppermute | solution.py:27
  254.6 24.9 %collective-permute-start.66 = (bf16[32,64,256]{2,1,0:T(8,128)(2,1)S(1)}, bf16[32,64,256]{2,1,0:T(8,128)(2,1)}, u32[]{:S(2)}, u32[]{:S(2)}) collective-permute-start(bf16[32,64,256]{2,1,0:T(8,128)(2,1)S(1)} %pad_maximum_fusion.3.rest_6_.rest_5_), channel_id=1, source_target_pairs={{0,4},{1,5},{6,2},{7,3},{8,12},{9,13},{14,10},{15,11},{16,20},{17,... | collective-permute-start | bytes 3145736 | tf_op jit(solution)/shard_map/ppermute | solution.py:27
  259.8 7.4 %collective-permute-start.58 = (bf16[4,192,256]{2,1,0:T(8,128)(2,1)S(1)}, bf16[4,192,256]{2,1,0:T(8,128)(2,1)S(1)}, u32[]{:S(2)}, u32[]{:S(2)}) collective-permute-start(bf16[4,192,256]{2,1,0:T(8,128)(2,1)S(1)} %get-tuple-element.43.rest_0_), channel_id=1, source_target_pairs={{0,1},{1,0},{2,3},{3,2},{4,5},{5,4},{6,7},{7,6},{8,24},{9,25},{10,... | collective-permute-start | bytes 1179656 | tf_op jit(solution)/shard_map/ppermute | solution.py:27
  260.9 24.7 %collective-permute-start.67 = (bf16[32,64,256]{2,1,0:T(8,128)(2,1)S(1)}, bf16[32,64,256]{2,1,0:T(8,128)(2,1)S(1)}, u32[]{:S(2)}, u32[]{:S(2)}) collective-permute-start(bf16[32,64,256]{2,1,0:T(8,128)(2,1)S(1)} %pad_maximum_fusion.3.rest_6_.rest_5_), channel_id=1, source_target_pairs={{0,8},{1,9},{2,10},{3,11},{4,12},{5,13},{6,14},{7,15},{8,0},{9,1},... | collective-permute-start | bytes 3145736 | tf_op jit(solution)/shard_map/ppermute | solution.py:27
  266.0 16.2 %collective-permute-start.59 = (bf16[4,192,256]{2,1,0:T(8,128)(2,1)S(1)}, bf16[4,192,256]{2,1,0:T(8,128)(2,1)S(1)}, u32[]{:S(2)}, u32[]{:S(2)}) collective-permute-start(bf16[4,192,256]{2,1,0:T(8,128)(2,1)S(1)} %get-tuple-element.43.rest_0_), channel_id=1, source_target_pairs={{0,16},{1,17},{2,18},{3,19},{4,20},{5,21},{6,22},{7,23},{8,9},{9,8... | collective-permute-start | bytes 1179656 | tf_op jit(solution)/shard_map/ppermute | solution.py:27
  267.3 14.9 %collective-permute-start.60 = (bf16[4,192,256]{2,1,0:T(8,128)(2,1)S(1)}, bf16[4,192,256]{2,1,0:T(8,128)(2,1)S(1)}, u32[]{:S(2)}, u32[]{:S(2)}) collective-permute-start(bf16[4,192,256]{2,1,0:T(8,128)(2,1)S(1)} %collective-permute-done.58.rest_1_), channel_id=1, source_target_pairs={{0,16},{1,17},{2,18},{3,19},{4,20},{5,21},{6,22},{7,23},{8,9},{9,8... | collective-permute-start | bytes 1179656 | tf_op jit(solution)/shard_map/ppermute | solution.py:27
  267.5 24.3 %collective-permute-start.68 = (bf16[32,64,256]{2,1,0:T(8,128)(2,1)S(1)}, bf16[32,64,256]{2,1,0:T(8,128)(2,1)}, u32[]{:S(2)}, u32[]{:S(2)}) collective-permute-start(bf16[32,64,256]{2,1,0:T(8,128)(2,1)S(1)} %collective-permute-done.64.rest_7_.rest_6_), channel_id=1, source_target_pairs={{0,8},{1,9},{2,10},{3,11},{4,12},{5,13},{6,14},{7,15},{8,0},{9,1},... | collective-permute-start | bytes 3145736 | tf_op jit(solution)/shard_map/ppermute | solution.py:27
  279.5 13.5 %collective-permute-start.69 = (bf16[32,64,256]{2,1,0:T(8,128)(2,1)S(1)}, bf16[32,64,256]{2,1,0:T(8,128)(2,1)}, u32[]{:S(2)}, u32[]{:S(2)}) collective-permute-start(bf16[32,64,256]{2,1,0:T(8,128)(2,1)S(1)} %collective-permute-done.65.rest_8_.rest_7_), channel_id=1, source_target_pairs={{0,8},{1,9},{2,10},{3,11},{4,12},{5,13},{6,14},{7,15},{8,0},{9,1},... | collective-permute-start | bytes 3145736 | tf_op jit(solution)/shard_map/ppermute | solution.py:27
  282.2 19.5 %collective-permute-start.70 = (bf16[32,64,256]{2,1,0:T(8,128)(2,1)}, bf16[32,64,256]{2,1,0:T(8,128)(2,1)}, u32[]{:S(2)}, u32[]{:S(2)}) collective-permute-start(bf16[32,64,256]{2,1,0:T(8,128)(2,1)} %collective-permute-done.66.rest_9_.rest_8_), channel_id=1, source_target_pairs={{0,8},{1,9},{2,10},{3,11},{4,12},{5,13},{6,14},{7,15},{8,0},{9,1},... | collective-permute-start | bytes 3145736 | tf_op jit(solution)/shard_map/ppermute | solution.py:27
  286.5 9.6 %collective-permute-start.62 = (bf16[4,192,256]{2,1,0:T(8,128)(2,1)S(1)}, bf16[4,192,256]{2,1,0:T(8,128)(2,1)}, u32[]{:S(2)}, u32[]{:S(2)}) collective-permute-start(bf16[4,192,256]{2,1,0:T(8,128)(2,1)S(1)} %project_out.6.rest_0_.rest_4_), channel_id=1, source_target_pairs={{0,16},{1,17},{2,18},{3,19},{4,20},{5,21},{6,22},{7,23},{8,9},{9,8... | collective-permute-start | bytes 1179656 | tf_op jit(solution)/shard_map/ppermute | solution.py:27
  291.5 10.1 %collective-permute-start.63 = (bf16[4,192,256]{2,1,0:T(8,128)(2,1)}, bf16[4,192,256]{2,1,0:T(8,128)(2,1)}, u32[]{:S(2)}, u32[]{:S(2)}) collective-permute-start(bf16[4,192,256]{2,1,0:T(8,128)(2,1)} %collective-permute-done.61.rest_1_), channel_id=1, source_target_pairs={{0,16},{1,17},{2,18},{3,19},{4,20},{5,21},{6,22},{7,23},{8,9},{9,8... | collective-permute-start | bytes 1179656 | tf_op jit(solution)/shard_map/ppermute | solution.py:27
  291.7 26.9 %collective-permute-start.72 = (bf16[192,2048]{1,0:T(8,128)(2,1)}, bf16[192,2048]{1,0:T(8,128)(2,1)S(1)}, u32[]{:S(2)}, u32[]{:S(2)}) collective-permute-start(bf16[192,2048]{1,0:T(8,128)(2,1)} %copy-done.38), channel_id=1, source_target_pairs={{2,10},{3,11},{4,12},{5,13},{10,8},{11,9},{12,14},{13,15},{18,26},... | collective-permute-start | bytes 2359304 | tf_op jit(solution)/shard_map/ppermute | solution.py:27
  310.8 7.7 %collective-permute-start.71 = (bf16[192,2048]{1,0:T(8,128)(2,1)S(1)}, bf16[192,2048]{1,0:T(8,128)(2,1)S(1)}, u32[]{:S(2)}, u32[]{:S(2)}) collective-permute-start(bf16[192,2048]{1,0:T(8,128)(2,1)S(1)} %broadcast_select_fusion), channel_id=1, source_target_pairs={{2,2},{3,3},{4,4},{5,5},{10,0},{11,1},{12,6},{13,7},{18,18},{19,19... | collective-permute-start | bytes 2359304 | tf_op jit(solution)/shard_map/ppermute | solution.py:27
  318.4 10.6 %collective-permute-start.75 = (bf16[4,192,256]{2,1,0:T(8,128)(2,1)S(1)}, bf16[4,192,256]{2,1,0:T(8,128)(2,1)S(1)}, u32[]{:S(2)}, u32[]{:S(2)}) collective-permute-start(bf16[4,192,256]{2,1,0:T(8,128)(2,1)S(1)} %collective-permute-done.73.rest_1_), channel_id=1, source_target_pairs={{0,16},{1,17},{2,18},{3,19},{4,20},{5,21},{6,22},{7,23},{8,9},{9,8... | collective-permute-start | bytes 1179656 | tf_op jit(solution)/shard_map/ppermute | solution.py:27
  332.3 14.7 %collective-permute-start.77 = (bf16[4,192,256]{2,1,0:T(8,128)(2,1)}, bf16[4,192,256]{2,1,0:T(8,128)(2,1)S(1)}, u32[]{:S(2)}, u32[]{:S(2)}) collective-permute-start(bf16[4,192,256]{2,1,0:T(8,128)(2,1)} %project_out.7), channel_id=1, source_target_pairs={{18,26},{19,27},{20,28},{21,29},{26,24},{27,25},{28,30},{29,31}} | collective-permute-start | bytes 1179656 | tf_op jit(solution)/shard_map/ppermute | solution.py:27
  333.6 14.9 %collective-permute-start.76 = (bf16[4,192,256]{2,1,0:T(8,128)(2,1)}, bf16[4,192,256]{2,1,0:T(8,128)(2,1)S(1)}, u32[]{:S(2)}, u32[]{:S(2)}) collective-permute-start(bf16[4,192,256]{2,1,0:T(8,128)(2,1)} %project_out.7), channel_id=1, source_target_pairs={{2,26},{3,27},{4,28},{5,29},{10,24},{11,25},{12,30},{13,31}} | collective-permute-start | bytes 1179656 | tf_op jit(solution)/shard_map/ppermute | solution.py:27
  (85 other events, 975.2 us)
where the time goes:
time: 355 us; the launch traced here: 352 us
  waiting for transfers between devices  160 us (45%)
  starting transfers between devices  114 us (32%)
  Pallas kernels  30.8 us (9%)
  local copies, waits for them, and re-layouts  30.5 us (9%)
  other arithmetic  15.8 us (4%)
    ppermute x78, waiting for transfers between devices, hop(): return lax.ppermute(value, AXES, pairs)  160 us
    ppermute x78, starting transfers between devices, hop(): return lax.ppermute(value, AXES, pairs)  114 us
    unnamed x142, local copies, waits for them, and re-layouts  21.9 us
    pallas_call x4, Pallas kernels, attend(): pl.pallas_call(functools.partial(attend_kernel, section, tuple((first for...  20.9 us
    pallas_call x4, Pallas kernels, project_out(): pl.pallas_call(functools.partial(output_kernel, section, tuple((first for...  9.95 us
  transfers between devices with their start and end apart: 78, of which 28 were waited for; matrix products, arithmetic and copies ran while one was open for 6% of the time, Pallas kernels for 8%

commit v1 on v0

v1 whole, which is shorter than its diff:
```python
import functools

import jax
import jax.numpy as jnp
from jax import lax
from jax.experimental import pallas as pl
from jax.experimental.pallas import tpu as pltpu
from jax.sharding import PartitionSpec as P

HD = 128
MBLK = 16
ATTEND_US = 1
PROJECT_US = 1
AXES = ("pipe", "fsdp", "tensor")
VMEM_LIMIT = 32 * 1024 * 1024
CUT_VMEM = 48 * 1024 * 1024
PICK_VMEM = 12 * 1024 * 1024


def hop(value, sizes, target):
    pipe, fsdp, tensor = sizes
    pairs = []
    for p in range(pipe):
        for z in range(fsdp):
            for x in range(tensor):
                to = target(p, z, x)
                if to is not None:
                    pairs.append(((p * fsdp + z) * tensor + x, (to[0] * fsdp + to[1]) * tensor + to[2]))
    return lax.ppermute(value, AXES, pairs)


def after(value, *earlier):
    return lax.optimization_barrier((value, *earlier))[0]


def weight_copies(parts, first, total, sems, pos_ref):
    copies = []
    for i, part in enumerate(parts):
        rows = part.shape[1]
        start = pl.multiple_of(pos_ref[i // 2] * rows, rows)
        source = part.at[pl.ds(first, total.shape[1])]
        copies.append(pltpu.make_async_copy(source, total.at[i % 2, :, pl.ds(start, rows), :], sems.at[i]))
    return copies


def slot_of(block, me_ref, cols, blocks):
    half = blocks // 2
    dx = (block // half) ^ me_ref[1]
    d = ((block % half) // cols) ^ me_ref[0]
    piece = jnp.where((me_ref[0] & 1) == 1, 2 * dx + (d >> 1), (d & 2) + dx)
    return (piece * 2 + (d & 1)) * cols + block % cols


def attend_kernel(section, n_parts, seq_len, me_ref, list_ref, pos_ref, mask_ref, *rest):
    pieces, gain_ref, parts = rest[:4], rest[4], rest[5 : 5 + n_parts]
    outs, (weights, normed, proj, sems) = rest[5 + n_parts : -4], rest[-4:]
    out_ref = outs[0]
    copies = weight_copies(parts, 0, weights, sems, pos_ref)
    for copy in copies:
        copy.start()
    cols, (per_piece, rows, width) = out_ref.shape[0] // 2, pieces[0].shape
    blocks = 4 * per_piece
    row = me_ref[0] ^ section
    first_gain = gain_ref.shape[1] - blocks * width
    square = jnp.zeros((rows, width), jnp.float32)
    for piece in pieces:
        for t in range(per_piece):
            block = piece[t].astype(jnp.float32)
            square += block * block
    mean = jnp.sum(square, axis=-1, keepdims=True) / (blocks * width)
    inv_rms = lax.rsqrt(mean + 1e-05)
    for i, piece in enumerate(pieces):
        for t in range(per_piece):
            odd = me_ref[0] & 1
            dx = jnp.where(odd == 1, i // 2, i % 2)
            dy = jnp.where(odd == 1, i % 2, i // 2)
            place = ((me_ref[1] ^ dx) * (blocks // 2) + (me_ref[0] ^ (2 * dy + t // cols)) * cols + t % cols) * width
            gain = gain_ref[pl.ds(row, 1), pl.ds(pl.multiple_of(first_gain + place, HD), width)]
            normed[i * per_piece + t] = (piece[t].astype(jnp.float32) * inv_rms * gain).astype(jnp.bfloat16)
    if len(outs) > 1:
        keeper_y = (section - 1) // 2
        odd = me_ref[0] & 1
        for dy in range(2):
            for t in range(per_piece):
                place = ((keeper_y ^ dy) * per_piece + (odd ^ (t // cols)) * cols + t % cols) * width
                value = jnp.where(odd == 1, pieces[dy][t], pieces[2 * dy][t])
                outs[1][:, pl.ds(pl.multiple_of(place, width), width)] = value
    for copy in copies:
        copy.wait()
    count = weights.shape[1]
    per = count // (3 * cols)
    wide = blocks // 2
    for core in range(2):
        for kind in range(3):
            for c in range(cols):
                total = None
                for i in range(per):
                    n = (kind * per + i) * cols + c
                    where = (kind * per + i) * wide + (me_ref[0] ^ core) * cols + c
                    slot = slot_of(list_ref[row, where].astype(jnp.int32), me_ref, cols, blocks)
                    term = jnp.dot(normed[slot], weights[core, n], preferred_element_type=jnp.float32)
                    total = term if total is None else total + term
                proj[kind, core * cols + c] = total.astype(jnp.bfloat16)
    heads = [(c, pl.ds(h * HD, HD)) for c in range(2 * cols) for h in range(width // HD)]
    along = seq_len // MBLK
    square_shape = (seq_len, seq_len)
    pair = (lax.broadcasted_iota(jnp.int32, square_shape, 0) // MBLK) * along
    pair = pair + lax.broadcasted_iota(jnp.int32, square_shape, 1) // MBLK
    for n in range(rows // seq_len):
        allowed = jnp.zeros(square_shape, jnp.int32)
        for i in range(along):
            for j in range(along):
                allowed = jnp.where(pair == i * along + j, mask_ref[n, i, j], allowed)
        span = pl.ds(n * seq_len, seq_len)
        scores = [
            lax.dot_general(
                proj[0, c, span, lanes],
                proj[1, c, span, lanes],
                (((1,), (1,)), ((), ())),
                preferred_element_type=jnp.float32,
            )
            for c, lanes in heads
        ]
        scores = jnp.stack(scores) * HD ** (-0.5)
        scores = jnp.where(allowed[None] == 1, scores, jnp.float32(-1e30))
        exp_scores = jnp.exp(scores - jnp.max(scores, axis=-1, keepdims=True))
        probs = (exp_scores / jnp.sum(exp_scores, axis=-1, keepdims=True)).astype(jnp.bfloat16)
        for i, (c, lanes) in enumerate(heads):
            attended = jnp.dot(probs[i], proj[2, c, span, lanes], preferred_element_type=jnp.float32)
            out_ref[c, span, lanes] = attended.astype(jnp.bfloat16)


def output_kernel(section, first, n_parts, list_first, me_ref, list_ref, other_ref, pos_ref, *rest):
    pieces, u_ref, parts = rest[:4], rest[4], rest[5 : 5 + n_parts]
    out_ref, weights, heads, sems, head_sems = rest[5 + n_parts :]
    copies = weight_copies(parts, first, weights, sems, pos_ref)
    per_piece = pieces[0].shape[0]
    for i, piece in enumerate(pieces):
        copy = pltpu.make_async_copy(piece, heads.at[pl.ds(i * per_piece, per_piece)], head_sems.at[i])
        copies.append(copy)
    for copy in copies:
        copy.start()
    for copy in copies:
        copy.wait()
    blocks = 4 * per_piece
    cols = out_ref.shape[0] // 2
    count = weights.shape[1]
    per = count // cols
    wide = blocks // 2
    row = me_ref[0] ^ section
    for core in range(2):
        for c in range(cols):
            total = None
            for i in range(per):
                half = i // (per // 2)
                where = list_first + ((i % (per // 2)) * 2 + me_ref[1]) * wide + (me_ref[0] ^ core) * cols + c
                block = (other_ref if half else list_ref)[row, where].astype(jnp.int32) + (me_ref[1] ^ half) * wide
                slot = slot_of(block, me_ref, cols, blocks)
                term = jnp.dot(heads[slot], weights[core, i * cols + c], preferred_element_type=jnp.float32)
                total = term if total is None else total + term
            to = core * cols + c
            out_ref[to] = (u_ref[to].astype(jnp.float32) + total).astype(jnp.bfloat16)


def cut_kernel(me_ref, *rest):
    blocks, outs, sems = rest[:4], rest[4:-1], rest[-1]
    p, x = me_ref[0], me_ref[1]
    cols_half = blocks[0].shape[2]
    cols = cols_half // len(outs)
    copies = []
    for d, out in enumerate(outs):
        at = 0
        for kind, ref in enumerate(blocks):
            first = (x * cols_half if kind == 3 else 0) + (p ^ d) * cols
            for i in range(ref.shape[1]):
                source = ref.at[0, i, pl.ds(first, cols)]
                copies.append(pltpu.make_async_copy(source, out.at[pl.ds(at, cols)], sems.at[len(copies)]))
                at += cols
    for copy in copies:
        copy.start()
    for copy in copies:
        copy.wait()


def prepare_kernel(oper_t, cols, me_ref, o_ref, token_ref, q_rows, k_rows, v_rows, o_rows, gain_ref, *rest):
    o_send, piece_ref, packed_ref, sems = rest
    p, x = me_ref[0], me_ref[1]
    cols_half = 4 * cols
    copies = []
    for d in range(4):
        for i in range(oper_t):
            to = o_send.at[pl.ds((d * oper_t + i) * cols, cols)]
            copies.append((o_ref.at[0, i, pl.ds((1 - x) * cols_half + (p ^ d) * cols, cols)], to))
    width = piece_ref.shape[2]
    for t in range(2 * cols):
        place = (((p >> 1) * 2 + ((p & 1) ^ (t // cols))) * cols + t % cols) * width
        copies.append((token_ref.at[:, pl.ds(pl.multiple_of(place, width), width)], piece_ref.at[t]))
    copies = [pltpu.make_async_copy(source, to, sems.at[i]) for i, (source, to) in enumerate(copies)]
    for copy in copies:
        copy.start()
    feats = gain_ref.shape[1]
    first = packed_ref.shape[1] - feats
    lane = lax.broadcasted_iota(jnp.int32, (1, first), 1)
    row = jnp.zeros((1, first), jnp.int32)
    at = 0
    for ref in (q_rows, k_rows, v_rows, o_rows):
        for i in range(ref.shape[1]):
            for c in range(ref.shape[2]):
                row = jnp.where(lane == at, ref[0, i, c], row)
                at += 1
    packed_ref[:, pl.ds(0, first)] = row.astype(jnp.float32)
    packed_ref[:, pl.ds(first, feats)] = gain_ref[...]
    for copy in copies:
        copy.wait()


def pick_kernel(choice, counts, me_ref, *rest):
    sources, (out, sems) = list(rest[:-2]), rest[-2:]
    copies = []
    for number, count in enumerate(counts):
        mine, sources = sources[:count], sources[count:]
        when = False
        for q, n in enumerate(choice):
            if n == number:
                when = (me_ref[0] == q) | when
        at = 0
        for j, source in enumerate(mine):
            size = source.shape[0]
            copies.append((when, pltpu.make_async_copy(source, out.at[pl.ds(at, size)], sems.at[j])))
            at += size
    for when, copy in copies:
        pl.when(when)(copy.start)
    for when, copy in copies:
        pl.when(when)(copy.wait)


SMEM = pl.BlockSpec(memory_space=pltpu.SMEM)
VMEM = pl.BlockSpec(memory_space=pltpu.VMEM)
ANY = pl.BlockSpec(memory_space=pl.ANY)


def hint(us):
    return pl.CostEstimate(flops=int(us * 1e9), bytes_accessed=0, transcendentals=0)


def attend(section, me, lists, gains, pos, mask, pieces, count, parts):
    cols, rows, width = pieces[0].shape
    depth = sum(part.shape[1] for part in parts) // 2
    outs = [jax.ShapeDtypeStruct((cols, rows, width), jnp.bfloat16)]
    if section > 0:
        outs.append(jax.ShapeDtypeStruct((rows, 2 * cols * width), jnp.bfloat16))
    return pl.pallas_call(
        functools.partial(attend_kernel, section, len(parts), rows // mask.shape[0]),
        out_shape=outs,
        in_specs=[SMEM] * 4 + [VMEM] * 5 + [ANY] * len(parts),
        out_specs=[VMEM] * len(outs),
        scratch_shapes=[
            pltpu.VMEM((2, count, depth, width), jnp.bfloat16),
            pltpu.VMEM((4 * cols, rows, width), jnp.bfloat16),
            pltpu.VMEM((3, cols, rows, width), jnp.bfloat16),
            pltpu.SemaphoreType.DMA((len(parts),)),
        ],
        compiler_params=pltpu.CompilerParams(vmem_limit_bytes=VMEM_LIMIT),
        cost_estimate=hint(ATTEND_US),
        name="attend",
    )(me, lists, pos, mask, *pieces, gains, *parts)


def project_out(section, me, lists, lists_x, list_first, pos, pieces, u_piece, first, count, parts):
    cols, rows, width = u_piece.shape
    depth = sum(part.shape[1] for part in parts) // 2
    return pl.pallas_call(
        functools.partial(output_kernel, section, first, len(parts), list_first),
        out_shape=jax.ShapeDtypeStruct(u_piece.shape, jnp.bfloat16),
        in_specs=[SMEM] * 4 + [ANY] * 4 + [VMEM] + [ANY] * len(parts),
        out_specs=VMEM,
        scratch_shapes=[
            pltpu.VMEM((2, count, depth, width), jnp.bfloat16),
            pltpu.VMEM((4 * cols, rows, width), jnp.bfloat16),
            pltpu.SemaphoreType.DMA((len(parts),)),
            pltpu.SemaphoreType.DMA((4,)),
        ],
        compiler_params=pltpu.CompilerParams(vmem_limit_bytes=VMEM_LIMIT),
        cost_estimate=hint(PROJECT_US),
        name="project_out",
    )(me, lists, lists_x, pos, *pieces, u_piece, *parts)


def cut(me, q_blocks, k_blocks, v_blocks, o_blocks):
    per, cols_half, shard, width = q_blocks.shape[1:]
    cols = cols_half // 4
    oper_t = o_blocks.shape[1]
    return pl.pallas_call(
        cut_kernel,
        out_shape=[jax.ShapeDtypeStruct(((3 * per + oper_t) * cols, shard, width), jnp.bfloat16)] * 4,
        in_specs=[SMEM] + [ANY] * 4,
        out_specs=[VMEM] * 4,
        scratch_shapes=[pltpu.SemaphoreType.DMA((4 * (3 * per + oper_t),))],
        compiler_params=pltpu.CompilerParams(vmem_limit_bytes=CUT_VMEM),
        cost_estimate=hint(1),
        name="cut",
    )(me, q_blocks, k_blocks, v_blocks, o_blocks)


def prepare(me, o_blocks, tokens, q_rows, k_rows, v_rows, o_rows, gains):
    oper_t, cols_all, shard, width = o_blocks.shape[1:]
    cols = cols_all // 8
    bf16 = lambda *shape: jax.ShapeDtypeStruct(shape, jnp.bfloat16)
    lists = sum(r.size for r in (q_rows, k_rows, v_rows, o_rows))
    lists += -lists % 128
    outs = [bf16(4 * oper_t * cols, shard, width), bf16(2 * cols, tokens.shape[0], width)]
    outs.append(jax.ShapeDtypeStruct((1, lists + gains.shape[1]), jnp.float32))
    return pl.pallas_call(
        functools.partial(prepare_kernel, oper_t, cols),
        out_shape=outs,
        in_specs=[SMEM] + [ANY] * 2 + [SMEM] * 4 + [VMEM],
        out_specs=[VMEM] * 3,
        scratch_shapes=[pltpu.SemaphoreType.DMA((4 * oper_t + 2 * cols,))],
        compiler_params=pltpu.CompilerParams(vmem_limit_bytes=PICK_VMEM),
        cost_estimate=hint(1),
        name="prepare",
    )(me, o_blocks, tokens, q_rows, k_rows, v_rows, o_rows, gains)


def pick(me, choice, candidates):
    used = sorted(set(choice))
    choice = tuple(used.index(n) for n in choice)
    candidates = [candidates[n] for n in used]
    first = candidates[0][0]
    size = sum(value.shape[0] for value in candidates[0])
    values = [value for candidate in candidates for value in candidate]
    return pl.pallas_call(
        functools.partial(pick_kernel, choice, tuple(len(candidate) for candidate in candidates)),
        out_shape=jax.ShapeDtypeStruct((size, *first.shape[1:]), first.dtype),
        in_specs=[SMEM] + [ANY] * len(values),
        out_specs=VMEM,
        scratch_shapes=[pltpu.SemaphoreType.DMA((max(len(candidate) for candidate in candidates),))],
        compiler_params=pltpu.CompilerParams(vmem_limit_bytes=PICK_VMEM),
        cost_estimate=hint(1),
        name="pick",
    )(me, *values)


def body(sizes, tokens, norm_gains, q_blocks, k_blocks, v_blocks, o_blocks, q_rows, k_rows, v_rows, o_rows, mask_blocks):
    sections, fsdp, tensor = sizes
    assert sections == 4 and tensor == 2
    send = lambda value, target: hop(value, sizes, target)
    p = lax.axis_index("pipe")
    z = lax.axis_index("fsdp")
    x = lax.axis_index("tensor")
    per, cols_half, shard, width = q_blocks.shape[1:]
    oper_t, cols_all = o_blocks.shape[1:3]
    cols = cols_half // sections
    rows = tokens.shape[0]
    feats = cols_all * width

    to_x = lambda p, z, x: (p, z, 1 - x)
    to_core = lambda p, z, x: (p ^ 1, z, x)
    to_pipe = lambda d: lambda p, z, x: (p ^ d, z, x)
    me = jnp.stack([p, x]).astype(jnp.int32)
    cut_for = cut(me, q_blocks, k_blocks, v_blocks, o_blocks)
    o_send, piece, packed = prepare(
        after(me, cut_for[2]), o_blocks, tokens, q_rows, k_rows, v_rows, o_rows, norm_gains
    )
    o_came = send(o_send, to_x)
    o_each = o_came.shape[0] // sections
    o_for = [o_came[d * o_each : (d + 1) * o_each] for d in range(sections)]
    packed = jnp.concatenate([packed] + [send(packed, to_pipe(d)) for d in (1, 2, 3)])
    lists = packed[:, : packed.shape[1] - norm_gains.shape[1]]

    pair_up = fsdp == 4
    if pair_up:
        near_z = {0: 1, 3: 2}
        far_z = {0: 2, 3: 1}
        swap_z = {1: 2, 2: 1}
        back_z = {1: 0, 2: 3}
        step = lambda where: (lambda p, z, x: (p, where[z], x) if z in where else None)
        inner = (z == 1) | (z == 2)

    mask = mask_blocks
    if pair_up:
        odd_near = lambda p, z, x: (p, near_z[z], x) if p & 1 and z in near_z else None
        piece = pick(me, (0, 1, 0, 1), [[piece], [send(piece, odd_near)]])
        mask = jnp.where((p & 1) == 1, send(mask, odd_near), mask)

    by_first = lambda p, z, x: (p ^ 2, z, x) if p & 1 else (p, z, 1 - x)
    by_second = lambda p, z, x: (p, z, 1 - x) if p & 1 else (p ^ 2, z, x)

    def share(value):
        first = send(value, by_first)
        return [value, first, send(value, by_second), send(first, by_second)]

    def exchange(values, ways):
        return {
            (d, pipes): [send(value, lambda p, z, x: (p ^ d, z, x) if p in pipes else None) for value in values[d]]
            for d, pipes in ways
        }

    def piece_of(section, came):
        keys = list(came)
        choice = []
        for q in range(sections):
            choice.append(next((i for i, (d, pipes) in enumerate(keys) if d == q ^ section and section in pipes), len(keys)))
        return pick(me, tuple(choice), [*came.values(), [cut_for[0], o_for[0]]])

    if pair_up:
        low = z < 2
        pos = jnp.where(low, jnp.array([1, 0, 2, 3]), jnp.array([2, 3, 1, 0])).astype(jnp.int32)

        def first_leg(piece, *tie):
            piece = after(piece, *tie) if tie else piece
            return [piece, send(piece, step(near_z)), send(piece, step(swap_z))]

        def second_leg(leg, *tie):
            return leg + [send(after(leg[0], *leg[1:], *tie), step(far_z))]

        def along_z(piece, tie=()):
            leg = first_leg(piece, *tie)
            return leg + [send(leg[0], step(far_z))]
    else:
        pos = jnp.zeros((1,), jnp.int32)

        def first_leg(piece, *tie):
            return [lax.all_gather(piece, "fsdp", axis=1, tiled=True)]

        def second_leg(leg, *tie):
            return leg

        def along_z(piece, tie=()):
            return [lax.all_gather(piece, "fsdp", axis=1, tiled=True)]

    def with_core(parts):
        return [each for part in parts for each in (part, send(part, to_core))]

    def deliver(core):
        if not pair_up:
            return kept[core]
        return send(
            kept[core],
            lambda p, z, x: (p - (p & 1) + core, back_z[z] if p & 1 else z, x) if z in back_z else None,
        )

    kept = [None, None]
    results = [None, None]
    o_for = [after(value, piece, mask) for value in o_for]
    round_a = exchange(list(zip(cut_for, o_for)), [(2, (0, 3)), (3, (0, 3)), (1, (0, 1, 2, 3))])
    leg = first_leg(piece_of(0, round_a))
    arrived = [value for values in list(round_a.values())[:2] for value in values]
    both_for = {d: [pick(me, (0,) * sections, [[after(cut_for[d], *arrived), o_for[d]]])] for d in (2, 3)}
    u = after(piece, *arrived)
    pieces = share(u)
    both_for = {d: [after(value, *pieces[1:]) for value in values] for d, values in both_for.items()}
    round_b = exchange(both_for, [(2, (1, 2)), (3, (1, 2))])
    round_b[1, (0, 1, 2, 3)] = round_a[1, (0, 1, 2, 3)]
    leg = second_leg(leg, pieces[1], packed)
    most = with_core(leg[:-1])
    in_count = 3 * per * cols
    out_count = leg[0].shape[0] - in_count
    lists_x = send(lists, to_x)
    for s in range(sections):
        last_leg = leg[-1:]
        if s > 0:
            pieces = share(u)
            last_leg = [after(part, pieces[1]) for part in last_leg]
        weights = most + with_core(last_leg)
        if s + 1 < sections:
            came = round_b if s + 1 in (1, 2) else round_a
            leg = first_leg(piece_of(s + 1, came), *last_leg)
        heads, *before = attend(s, me, lists, packed, pos, mask, pieces, in_count, weights)
        if s > 0:
            core = (s - 1) & 1
            kept[core] = before[0] if kept[core] is None else jnp.where((p >> 1) == 0, kept[core], before[0])
        if s == sections - 1:
            results = [deliver(core) for core in range(2)]
        pieces = share(heads)
        if s + 1 < sections:
            leg = second_leg(leg, *(pieces[1:] if s == 0 else pieces[1:2]))
            most = with_core(leg[:-1])
        if s == sections - 1:
            pieces[0] = after(pieces[0], *results)
        u = project_out(s, me, lists, lists_x, 3 * per * cols_half, pos, pieces, u, in_count, out_count, weights)

    final = u
    last_core = (sections - 1) & 1
    if pair_up:
        home = lambda z, core: back_z[z] if core else z
    else:
        home = lambda z, core: z if core == last_core else None
    halves = []
    for y in range(2):

        def to_last(p, z, x, y=y):
            to = home(z, p & 1) if (p >> 1) == y and (not pair_up or z in back_z) else None
            return None if to is None else (sections - 1, to, x)

        halves.append(send(final, to_last))
    made_by = jnp.where(inner, 0, 1) if pair_up else last_core
    blocks = jnp.stack(halves).reshape(2, 2, cols, rows, width)
    blocks = jnp.where(made_by == 1, blocks[:, ::-1], blocks)
    last = jnp.transpose(blocks, (3, 0, 1, 2, 4)).reshape(rows, -1)
    result = jnp.where((p & 1) == 1, results[1], results[0])
    return jnp.where(p == sections - 1, last, result)[None]


def solution(mesh):
    placed = (
        P("fsdp", "tensor"),
        P("pipe", None),
        P("pipe", None, "tensor", "fsdp", None),
        P("pipe", None, "tensor", "fsdp", None),
        P("pipe", None, "tensor", "fsdp", None),
        P("pipe", "tensor", None, "fsdp", None),
        P("pipe", None, "tensor"),
        P("pipe", None, "tensor"),
        P("pipe", None, "tensor"),
        P("pipe", "tensor", None),
        P("fsdp", None, None),
    )
    sizes = tuple(mesh.shape[axis] for axis in AXES)
    return jax.shard_map(
        functools.partial(body, sizes),
        mesh=mesh,
        in_specs=placed,
        out_specs=P("pipe", "fsdp", "tensor"),
        check_vma=False,
    )
```

time: 355 us -> 332 us (0.935)
  Pallas kernels: 30.8 us -> 51.6 us
  local copies, waits for them, and re-layouts: 30.5 us -> 14.6 us
  other arithmetic: 15.8 us -> 1.44 us
  starting transfers between devices: 114 us -> 104 us
    pallas_call x8 -> x17, Pallas kernels: 30.8 us -> 51.6 us  [the longest x4 21.6 us: attend(): pl.pallas_call(functools.partial(attend_kernel, section, len(parts), rows...]
    ppermute x78 -> x71, starting transfers between devices: 114 us -> 104 us  [hop(): return lax.ppermute(value, AXES, pairs)]
    unnamed x142 -> x70, local copies, waits for them, and re-layouts: 21.9 us -> 11.9 us
    select_n x4 -> x1, other arithmetic: 7.01 us -> 0.01 us  [body(): mask = jnp.where(p & 1 == 1, send(mask, odd_near), mask)]
    concatenate x8 -> x1, other arithmetic: 4.77 us -> 0.07 us  [body(): jnp.concatenate([packed] + [send(packed, to_pipe(d)) for d in (1, 2, 3)])]
    ppermute x78 -> x71, waiting for transfers between devices: 160 us -> 158 us  [hop(): return lax.ppermute(value, AXES, pairs)]
  transfers between devices with their start and end apart: 78 -> 71, of which waited for: 28 -> 38; matrix products, arithmetic and copies ran while one was open for 6% -> 0% of each run, Pallas kernels for 8% -> 12%
where the time goes in v1:
time: 332 us; the launch traced here: 330 us
  waiting for transfers between devices  158 us (48%)
  starting transfers between devices  104 us (31%)
  Pallas kernels  51.6 us (16%)
  local copies, waits for them, and re-layouts  14.6 us (4%)
    ppermute x71, waiting for transfers between devices, hop(): return lax.ppermute(value, AXES, pairs)  158 us
    ppermute x71, starting transfers between devices, hop(): return lax.ppermute(value, AXES, pairs)  104 us
    pallas_call x4, Pallas kernels, attend(): pl.pallas_call(functools.partial(attend_kernel, section, len(parts), rows...  21.6 us
    unnamed x70, local copies, waits for them, and re-layouts  11.9 us
    pallas_call x7, Pallas kernels, pick(): pl.pallas_call(functools.partial(pick_kernel, choice, tuple((len(candidat...  11.5 us
    pallas_call x4, Pallas kernels, project_out(): pl.pallas_call(functools.partial(output_kernel, section, first, len(parts...  9.86 us
  transfers between devices with their start and end apart: 71, of which 38 were waited for; matrix products, arithmetic and copies ran while one was open for 0% of the time, Pallas kernels for 12%

profile of v1, /device:TPU:5, one launch (start us, length us, event | category | flops | bytes accessed | tf_op | source)
XLA Modules:
  0.0 330.3 jit_solution(14891849024087397605)
XLA Ops:
  2.6 6.3 %cut.1 = (bf16[28,64,256]{2,1,0:T(8,128)(2,1)S(1)}, bf16[28,64,256]{2,1,0:T(8,128)(2,1)}, bf16[28,64,256]{2,1,0:T(8,128)(2,1)}, bf16[28,64,256]{2,1,0:T(8,128)(2,1)}) custom-call(s32[2]{0:T(128)S(1)} %pad_add_fusion.me_ref, bf16[1,4,8,64,256]{4,3,2,1,0:T(8,128)(2,1)S(1)} %copy-done.10, bf16[1,4,8,64,256]{4,3,2,1,0:T(8,128)(2,1)S(1)} %copy-done.11, ...), custom_call_target="tpu_custom_call" | custom-call | flops 1000000000 | tf_op jit(solution)/shard_map/cut/pallas_call | solution.py:293
  9.6 2.3 prepare.1
  13.2 3.9 %collective-permute-start.5 = (bf16[4,192,256]{2,1,0:T(8,128)(2,1)}, bf16[4,192,256]{2,1,0:T(8,128)(2,1)}, u32[]{:S(2)}, u32[]{:S(2)}) collective-permute-start(bf16[4,192,256]{2,1,0:T(8,128)(2,1)} %get-tuple-element.42.rest_0_), channel_id=1, source_target_pairs={{8,10},{9,11},{14,12},{15,13},{24,26},{25,27},{30,28},{31,29}} | collective-permute-start | bytes 1179656 | tf_op jit(solution)/shard_map/ppermute | solution.py:29
  17.2 2.2 collective-permute-start.6
  19.4 1.9 collective-permute-start.9
  21.3 3.0 collective-permute-start.4
  27.9 1.9 collective-permute-start.10
  31.2 10.4 %collective-permute-done.10.rest_3_ = bf16[4,64,256]{2,1,0:T(8,128)(2,1)S(1)} collective-permute-done((bf16[4,64,256]{2,1,0:T(8,128)(2,1)S(1)}, bf16[4,64,256]{2,1,0:T(8,128)(2,1)S(1)}, u32[]{:S(2)}, u32[]{:S(2)}) %collective-permute-start.10) | collective-permute-done | bytes 131104 | tf_op jit(solution)/shard_map/ppermute | solution.py:29
  43.4 1.9 collective-permute-start.11
  48.3 2.3 collective-permute-start.17
  59.4 3.6 %collective-permute-done.12.rest_2_ = bf16[4,192,256]{2,1,0:T(8,128)(2,1)S(1)} collective-permute-done((bf16[4,192,256]{2,1,0:T(8,128)(2,1)S(1)}, bf16[4,192,256]{2,1,0:T(8,128)(2,1)S(1)}, u32[]{:S(2)}, u32[]{:S(2)}) %collective-permute-start.12) | collective-permute-done | bytes 393248 | tf_op jit(solution)/shard_map/ppermute | solution.py:29
  63.7 3.5 %collective-permute-done.13.rest_3_ = bf16[4,192,256]{2,1,0:T(8,128)(2,1)S(1)} collective-permute-done((bf16[4,192,256]{2,1,0:T(8,128)(2,1)S(1)}, bf16[4,192,256]{2,1,0:T(8,128)(2,1)S(1)}, u32[]{:S(2)}, u32[]{:S(2)}) %collective-permute-start.13) | collective-permute-done | bytes 393248 | tf_op jit(solution)/shard_map/ppermute | solution.py:29
  68.7 2.3 collective-permute-done.17.rest_7_
  71.0 6.6 %collective-permute-start.21 = (bf16[32,64,256]{2,1,0:T(8,128)(2,1)S(1)}, bf16[32,64,256]{2,1,0:T(8,128)(2,1)}, u32[]{:S(2)}, u32[]{:S(2)}) collective-permute-start(bf16[32,64,256]{2,1,0:T(8,128)(2,1)S(1)} %pick.8.rest_5_), channel_id=1, source_target_pairs={{0,4},{1,5},{6,2},{7,3},{8,12},{9,13},{14,10},{15,11},{16,20},{17,... | collective-permute-start | bytes 3145736 | tf_op jit(solution)/shard_map/ppermute | solution.py:29
  77.6 2.7 pick.9
  81.6 4.8 %collective-permute-start.16 = (bf16[32,64,256]{2,1,0:T(8,128)(2,1)S(1)}, bf16[32,64,256]{2,1,0:T(8,128)(2,1)}, u32[]{:S(2)}, u32[]{:S(2)}) collective-permute-start(bf16[32,64,256]{2,1,0:T(8,128)(2,1)S(1)} %pick.8.rest_5_), channel_id=1, source_target_pairs={{0,8},{1,9},{2,10},{3,11},{4,12},{5,13},{6,14},{7,15},{8,0},{9,1},... | collective-permute-start | bytes 3145736 | tf_op jit(solution)/shard_map/ppermute | solution.py:29
  87.9 8.7 %collective-permute-done.21.rest_11_ = bf16[32,64,256]{2,1,0:T(8,128)(2,1)} collective-permute-done((bf16[32,64,256]{2,1,0:T(8,128)(2,1)S(1)}, bf16[32,64,256]{2,1,0:T(8,128)(2,1)}, u32[]{:S(2)}, u32[]{:S(2)}) %collective-permute-start.21) | collective-permute-done | bytes 1048608 | tf_op jit(solution)/shard_map/ppermute | solution.py:29
  96.7 3.3 collective-permute-start.22
  101.2 1.8 pick.11.rest_5_
  103.0 4.2 %collective-permute-start.32 = (bf16[32,64,256]{2,1,0:T(8,128)(2,1)S(1)}, bf16[32,64,256]{2,1,0:T(8,128)(2,1)S(1)}, u32[]{:S(2)}, u32[]{:S(2)}) collective-permute-start(bf16[32,64,256]{2,1,0:T(8,128)(2,1)S(1)} %pick.11.rest_5_), channel_id=1, source_target_pairs={{0,2},{1,3},{6,4},{7,5},{8,10},{9,11},{14,12},{15,13},{16,18},{17,... | collective-permute-start | bytes 3145736 | tf_op jit(solution)/shard_map/ppermute | solution.py:29
  108.1 6.1 %attend.4.rest_0_ = bf16[4,192,256]{2,1,0:T(8,128)(2,1)S(1)} custom-call(s32[2]{0:T(128)S(1)} %pad_add_fusion.me_ref, f32[4,128]{1,0:T(4,128)S(1)} %slice.20.list_ref, s32[4]{0:T(128)S(1)} %broadcast_select_fusion.2.pos_ref, s32[3,4,4]{2,1,0:T(4,128)S(1)} %broadcast_select_fusion.1.mask_ref, bf16[4,192,256]{2,1,0:T(8,128)(2,1)S(1)} %copy-done.9, ...), custom_call_target="tpu_custom_call" | custom-call | flops 1000000000 | tf_op jit(solution)/shard_map/attend/pallas_call | solution.py:252
  114.8 9.9 %collective-permute-done.23.rest_1_ = bf16[4,192,256]{2,1,0:T(8,128)(2,1)S(1)} collective-permute-done((bf16[4,192,256]{2,1,0:T(8,128)(2,1)S(1)}, bf16[4,192,256]{2,1,0:T(8,128)(2,1)S(1)}, u32[]{:S(2)}, u32[]{:S(2)}) %collective-permute-start.23) | collective-permute-done | bytes 393248 | tf_op jit(solution)/shard_map/ppermute | solution.py:29
  124.8 4.7 %collective-permute-done.32.rest_7_ = bf16[32,64,256]{2,1,0:T(8,128)(2,1)S(1)} collective-permute-done((bf16[32,64,256]{2,1,0:T(8,128)(2,1)S(1)}, bf16[32,64,256]{2,1,0:T(8,128)(2,1)S(1)}, u32[]{:S(2)}, u32[]{:S(2)}) %collective-permute-start.32) | collective-permute-done | bytes 1048608 | tf_op jit(solution)/shard_map/ppermute | solution.py:29
  129.4 2.2 collective-permute-done.25.rest_3_
  131.7 4.3 %collective-permute-start.36 = (bf16[32,64,256]{2,1,0:T(8,128)(2,1)S(1)}, bf16[32,64,256]{2,1,0:T(8,128)(2,1)S(1)}, u32[]{:S(2)}, u32[]{:S(2)}) collective-permute-start(bf16[32,64,256]{2,1,0:T(8,128)(2,1)S(1)} %pick.11.rest_5_), channel_id=1, source_target_pairs={{0,4},{1,5},{6,2},{7,3},{8,12},{9,13},{14,10},{15,11},{16,20},{17,... | collective-permute-start | bytes 3145736 | tf_op jit(solution)/shard_map/ppermute | solution.py:29
  137.0 2.4 collective-permute-done.3.other_ref
  139.4 2.8 project_out.4.rest_0_.rest_4_
  142.2 1.8 collective-permute-start.26
  144.5 5.0 %collective-permute-done.26.rest_1_ = bf16[4,192,256]{2,1,0:T(8,128)(2,1)S(1)} collective-permute-done((bf16[4,192,256]{2,1,0:T(8,128)(2,1)S(1)}, bf16[4,192,256]{2,1,0:T(8,128)(2,1)S(1)}, u32[]{:S(2)}, u32[]{:S(2)}) %collective-permute-start.26) | collective-permute-done | bytes 393248 | tf_op jit(solution)/shard_map/ppermute | solution.py:29
  149.5 8.2 %collective-permute-done.36.rest_11_ = bf16[32,64,256]{2,1,0:T(8,128)(2,1)S(1)} collective-permute-done((bf16[32,64,256]{2,1,0:T(8,128)(2,1)S(1)}, bf16[32,64,256]{2,1,0:T(8,128)(2,1)S(1)}, u32[]{:S(2)}, u32[]{:S(2)}) %collective-permute-start.36) | collective-permute-done | bytes 1048608 | tf_op jit(solution)/shard_map/ppermute | solution.py:29
  160.2 4.9 %collective-permute-start.45 = (bf16[32,64,256]{2,1,0:T(8,128)(2,1)S(1)}, bf16[32,64,256]{2,1,0:T(8,128)(2,1)S(1)}, u32[]{:S(2)}, u32[]{:S(2)}) collective-permute-start(bf16[32,64,256]{2,1,0:T(8,128)(2,1)S(1)} %pick.12.rest_5_), channel_id=1, source_target_pairs={{0,2},{1,3},{6,4},{7,5},{8,10},{9,11},{14,12},{15,13},{16,18},{17,... | collective-permute-start | bytes 3145736 | tf_op jit(solution)/shard_map/ppermute | solution.py:29
  167.6 5.5 %collective-permute-done.27.rest_2_ = bf16[4,192,256]{2,1,0:T(8,128)(2,1)S(1)} collective-permute-done((bf16[4,192,256]{2,1,0:T(8,128)(2,1)S(1)}, bf16[4,192,256]{2,1,0:T(8,128)(2,1)S(1)}, u32[]{:S(2)}, u32[]{:S(2)}) %collective-permute-start.27) | collective-permute-done | bytes 393248 | tf_op jit(solution)/shard_map/ppermute | solution.py:29
  173.0 4.2 %collective-permute-done.28.rest_3_ = bf16[4,192,256]{2,1,0:T(8,128)(2,1)S(1)} collective-permute-done((bf16[4,192,256]{2,1,0:T(8,128)(2,1)S(1)}, bf16[4,192,256]{2,1,0:T(8,128)(2,1)S(1)}, u32[]{:S(2)}, u32[]{:S(2)}) %collective-permute-start.28) | collective-permute-done | bytes 393248 | tf_op jit(solution)/shard_map/ppermute | solution.py:29
  177.2 4.6 %attend.5 = (bf16[4,192,256]{2,1,0:T(8,128)(2,1)S(1)}, bf16[192,2048]{1,0:T(8,128)(2,1)S(1)}) custom-call(s32[2]{0:T(128)S(1)} %pad_add_fusion.me_ref, f32[4,128]{1,0:T(4,128)S(1)} %slice.20.list_ref, s32[4]{0:T(128)S(1)} %broadcast_select_fusion.2.pos_ref, s32[3,4,4]{2,1,0:T(4,128)S(1)} %broadcast_select_fusion.1.mask_ref, ...), custom_call_target="tpu_custom_call" | custom-call | flops 1000000000 | tf_op jit(solution)/shard_map/attend/pallas_call | solution.py:252
  182.0 5.6 %collective-permute-done.45.rest_7_ = bf16[32,64,256]{2,1,0:T(8,128)(2,1)S(1)} collective-permute-done((bf16[32,64,256]{2,1,0:T(8,128)(2,1)S(1)}, bf16[32,64,256]{2,1,0:T(8,128)(2,1)S(1)}, u32[]{:S(2)}, u32[]{:S(2)}) %collective-permute-start.45) | collective-permute-done | bytes 1048608 | tf_op jit(solution)/shard_map/ppermute | solution.py:29
  188.9 4.4 %collective-permute-start.49 = (bf16[32,64,256]{2,1,0:T(8,128)(2,1)S(1)}, bf16[32,64,256]{2,1,0:T(8,128)(2,1)S(1)}, u32[]{:S(2)}, u32[]{:S(2)}) collective-permute-start(bf16[32,64,256]{2,1,0:T(8,128)(2,1)S(1)} %pick.12.rest_5_), channel_id=1, source_target_pairs={{0,4},{1,5},{6,2},{7,3},{8,12},{9,13},{14,10},{15,11},{16,20},{17,... | collective-permute-start | bytes 3145736 | tf_op jit(solution)/shard_map/ppermute | solution.py:29
  194.8 2.1 collective-permute-start.44
  196.9 3.4 %collective-permute-done.39.rest_2_ = bf16[4,192,256]{2,1,0:T(8,128)(2,1)S(1)} collective-permute-done((bf16[4,192,256]{2,1,0:T(8,128)(2,1)S(1)}, bf16[4,192,256]{2,1,0:T(8,128)(2,1)S(1)}, u32[]{:S(2)}, u32[]{:S(2)}) %collective-permute-start.39) | collective-permute-done | bytes 393248 | tf_op jit(solution)/shard_map/ppermute | solution.py:29
  200.3 4.2 %collective-permute-done.40.rest_3_ = bf16[4,192,256]{2,1,0:T(8,128)(2,1)S(1)} collective-permute-done((bf16[4,192,256]{2,1,0:T(8,128)(2,1)S(1)}, bf16[4,192,256]{2,1,0:T(8,128)(2,1)S(1)}, u32[]{:S(2)}, u32[]{:S(2)}) %collective-permute-start.40) | collective-permute-done | bytes 393248 | tf_op jit(solution)/shard_map/ppermute | solution.py:29
  204.5 2.2 project_out.5.rest_0_.rest_4_
  206.8 2.6 collective-permute-start.46
  209.4 4.3 %collective-permute-done.41.rest_1_ = bf16[4,192,256]{2,1,0:T(8,128)(2,1)S(1)} collective-permute-done((bf16[4,192,256]{2,1,0:T(8,128)(2,1)S(1)}, bf16[4,192,256]{2,1,0:T(8,128)(2,1)S(1)}, u32[]{:S(2)}, u32[]{:S(2)}) %collective-permute-start.41) | collective-permute-done | bytes 393248 | tf_op jit(solution)/shard_map/ppermute | solution.py:29
  214.4 2.5 collective-permute-start.50
  217.9 4.5 %collective-permute-start.58 = (bf16[32,64,256]{2,1,0:T(8,128)(2,1)S(1)}, bf16[32,64,256]{2,1,0:T(8,128)(2,1)S(1)}, u32[]{:S(2)}, u32[]{:S(2)}) collective-permute-start(bf16[32,64,256]{2,1,0:T(8,128)(2,1)S(1)} %pick.13.rest_5_), channel_id=1, source_target_pairs={{0,2},{1,3},{6,4},{7,5},{8,10},{9,11},{14,12},{15,13},{16,18},{17,... | collective-permute-start | bytes 3145736 | tf_op jit(solution)/shard_map/ppermute | solution.py:29
  225.6 5.5 %collective-permute-done.42.rest_2_ = bf16[4,192,256]{2,1,0:T(8,128)(2,1)S(1)} collective-permute-done((bf16[4,192,256]{2,1,0:T(8,128)(2,1)S(1)}, bf16[4,192,256]{2,1,0:T(8,128)(2,1)S(1)}, u32[]{:S(2)}, u32[]{:S(2)}) %collective-permute-start.42) | collective-permute-done | bytes 393248 | tf_op jit(solution)/shard_map/ppermute | solution.py:29
  231.0 4.2 %collective-permute-done.43.rest_3_ = bf16[4,192,256]{2,1,0:T(8,128)(2,1)S(1)} collective-permute-done((bf16[4,192,256]{2,1,0:T(8,128)(2,1)S(1)}, bf16[4,192,256]{2,1,0:T(8,128)(2,1)S(1)}, u32[]{:S(2)}, u32[]{:S(2)}) %collective-permute-start.43) | collective-permute-done | bytes 393248 | tf_op jit(solution)/shard_map/ppermute | solution.py:29
  235.2 4.6 %attend.6 = (bf16[4,192,256]{2,1,0:T(8,128)(2,1)S(1)}, bf16[192,2048]{1,0:T(8,128)(2,1)S(1)}) custom-call(s32[2]{0:T(128)S(1)} %pad_add_fusion.me_ref, f32[4,128]{1,0:T(4,128)S(1)} %slice.20.list_ref, s32[4]{0:T(128)S(1)} %broadcast_select_fusion.2.pos_ref, s32[3,4,4]{2,1,0:T(4,128)S(1)} %broadcast_select_fusion.1.mask_ref, ...), custom_call_target="tpu_custom_call" | custom-call | flops 1000000000 | tf_op jit(solution)/shard_map/attend/pallas_call | solution.py:252
  239.9 5.0 %collective-permute-done.58.rest_7_ = bf16[32,64,256]{2,1,0:T(8,128)(2,1)S(1)} collective-permute-done((bf16[32,64,256]{2,1,0:T(8,128)(2,1)S(1)}, bf16[32,64,256]{2,1,0:T(8,128)(2,1)S(1)}, u32[]{:S(2)}, u32[]{:S(2)}) %collective-permute-start.58) | collective-permute-done | bytes 1048608 | tf_op jit(solution)/shard_map/ppermute | solution.py:29
  244.9 1.9 collective-permute-done.51.rest_1_
  246.8 4.8 %collective-permute-start.62 = (bf16[32,64,256]{2,1,0:T(8,128)(2,1)S(1)}, bf16[32,64,256]{2,1,0:T(8,128)(2,1)}, u32[]{:S(2)}, u32[]{:S(2)}) collective-permute-start(bf16[32,64,256]{2,1,0:T(8,128)(2,1)S(1)} %pick.13.rest_5_), channel_id=1, source_target_pairs={{0,4},{1,5},{6,2},{7,3},{8,12},{9,13},{14,10},{15,11},{16,20},{17,... | collective-permute-start | bytes 3145736 | tf_op jit(solution)/shard_map/ppermute | solution.py:29
  253.1 5.5 %collective-permute-done.52.rest_2_ = bf16[4,192,256]{2,1,0:T(8,128)(2,1)S(1)} collective-permute-done((bf16[4,192,256]{2,1,0:T(8,128)(2,1)S(1)}, bf16[4,192,256]{2,1,0:T(8,128)(2,1)S(1)}, u32[]{:S(2)}, u32[]{:S(2)}) %collective-permute-start.52) | collective-permute-done | bytes 393248 | tf_op jit(solution)/shard_map/ppermute | solution.py:29
  258.6 4.2 %collective-permute-done.53.rest_3_ = bf16[4,192,256]{2,1,0:T(8,128)(2,1)S(1)} collective-permute-done((bf16[4,192,256]{2,1,0:T(8,128)(2,1)S(1)}, bf16[4,192,256]{2,1,0:T(8,128)(2,1)S(1)}, u32[]{:S(2)}, u32[]{:S(2)}) %collective-permute-start.53) | collective-permute-done | bytes 393248 | tf_op jit(solution)/shard_map/ppermute | solution.py:29
  262.8 2.2 project_out.6.rest_0_.rest_4_
  265.1 2.3 collective-permute-start.57
  268.0 4.1 %collective-permute-done.54.rest_1_ = bf16[4,192,256]{2,1,0:T(8,128)(2,1)S(1)} collective-permute-done((bf16[4,192,256]{2,1,0:T(8,128)(2,1)S(1)}, bf16[4,192,256]{2,1,0:T(8,128)(2,1)S(1)}, u32[]{:S(2)}, u32[]{:S(2)}) %collective-permute-start.54) | collective-permute-done | bytes 393248 | tf_op jit(solution)/shard_map/ppermute | solution.py:29
  272.2 2.8 collective-permute-start.63
  278.9 3.1 collective-permute-done.55.rest_2_
  282.0 4.2 %collective-permute-done.56.rest_3_ = bf16[4,192,256]{2,1,0:T(8,128)(2,1)} collective-permute-done((bf16[4,192,256]{2,1,0:T(8,128)(2,1)S(1)}, bf16[4,192,256]{2,1,0:T(8,128)(2,1)}, u32[]{:S(2)}, u32[]{:S(2)}) %collective-permute-start.56) | collective-permute-done | bytes 393248 | tf_op jit(solution)/shard_map/ppermute | solution.py:29
  287.4 6.3 %attend.7 = (bf16[4,192,256]{2,1,0:T(8,128)(2,1)S(1)}, bf16[192,2048]{1,0:T(8,128)(2,1)S(1)}) custom-call(s32[2]{0:T(128)S(1)} %pad_add_fusion.me_ref, f32[4,128]{1,0:T(4,128)S(1)} %slice.20.list_ref, s32[4]{0:T(128)S(1)} %broadcast_select_fusion.2.pos_ref, s32[3,4,4]{2,1,0:T(4,128)S(1)} %broadcast_select_fusion.1.mask_ref, ...), custom_call_target="tpu_custom_call" | custom-call | flops 1000000000 | tf_op jit(solution)/shard_map/attend/pallas_call | solution.py:252
  294.7 8.8 %collective-permute-done.66.rest_1_ = bf16[4,192,256]{2,1,0:T(8,128)(2,1)S(1)} collective-permute-done((bf16[4,192,256]{2,1,0:T(8,128)(2,1)S(1)}, bf16[4,192,256]{2,1,0:T(8,128)(2,1)S(1)}, u32[]{:S(2)}, u32[]{:S(2)}) %collective-permute-start.66) | collective-permute-done | bytes 393248 | tf_op jit(solution)/shard_map/ppermute | solution.py:29
  303.9 6.5 %collective-permute-done.68.rest_3_ = bf16[4,192,256]{2,1,0:T(8,128)(2,1)S(1)} collective-permute-done((bf16[4,192,256]{2,1,0:T(8,128)(2,1)S(1)}, bf16[4,192,256]{2,1,0:T(8,128)(2,1)S(1)}, u32[]{:S(2)}, u32[]{:S(2)}) %collective-permute-start.68) | collective-permute-done | bytes 393248 | tf_op jit(solution)/shard_map/ppermute | solution.py:29
  310.4 2.6 project_out.7
  315.7 9.0 %collective-permute-done.69 = bf16[4,192,256]{2,1,0:T(8,128)(2,1)S(1)} collective-permute-done((bf16[4,192,256]{2,1,0:T(8,128)(2,1)S(1)}, bf16[4,192,256]{2,1,0:T(8,128)(2,1)S(1)}, u32[]{:S(2)}, u32[]{:S(2)}) %collective-permute-start.69) | collective-permute-done | bytes 393248 | tf_op jit(solution)/shard_map/ppermute | solution.py:29
  324.7 2.2 collective-permute-done.70
  (177 shorter events, 59.6 us)
Async XLA Ops:
  12.0 14.7 %collective-permute-start.7 = (bf16[16,64,256]{2,1,0:T(8,128)(2,1)S(1)}, bf16[16,64,256]{2,1,0:T(8,128)(2,1)}, u32[]{:S(2)}, u32[]{:S(2)}) collective-permute-start(bf16[16,64,256]{2,1,0:T(8,128)(2,1)S(1)} %get-tuple-element.43), channel_id=1, source_target_pairs={{0,1},{1,0},{2,3},{3,2},{4,5},{5,4},{6,7},{7,6},{8,9},{9,8},{10,11... | collective-permute-start | bytes 1572872 | tf_op jit(solution)/shard_map/ppermute | solution.py:29
  13.2 11.9 %collective-permute-start.5 = (bf16[4,192,256]{2,1,0:T(8,128)(2,1)}, bf16[4,192,256]{2,1,0:T(8,128)(2,1)}, u32[]{:S(2)}, u32[]{:S(2)}) collective-permute-start(bf16[4,192,256]{2,1,0:T(8,128)(2,1)} %get-tuple-element.42.rest_0_), channel_id=1, source_target_pairs={{8,10},{9,11},{14,12},{15,13},{24,26},{25,27},{30,28},{31,29}} | collective-permute-start | bytes 1179656 | tf_op jit(solution)/shard_map/ppermute | solution.py:29
  17.2 25.3 %collective-permute-start.6 = (bf16[28,64,256]{2,1,0:T(8,128)(2,1)}, bf16[28,64,256]{2,1,0:T(8,128)(2,1)S(1)}, u32[]{:S(2)}, u32[]{:S(2)}) collective-permute-start(bf16[28,64,256]{2,1,0:T(8,128)(2,1)} %get-tuple-element.53.rest_0_), channel_id=1, source_target_pairs={{0,16},{1,17},{2,18},{3,19},{4,20},{5,21},{6,22},{7,23},{24,8},{25... | collective-permute-start | bytes 2752520 | tf_op jit(solution)/shard_map/ppermute | solution.py:29
  19.4 24.0 %collective-permute-start.9 = (bf16[28,64,256]{2,1,0:T(8,128)(2,1)}, bf16[28,64,256]{2,1,0:T(8,128)(2,1)}, u32[]{:S(2)}, u32[]{:S(2)}) collective-permute-start(bf16[28,64,256]{2,1,0:T(8,128)(2,1)} %get-tuple-element.55.rest_0_), channel_id=1, source_target_pairs={{0,24},{1,25},{2,26},{3,27},{4,28},{5,29},{6,30},{7,31},{24,0},{25... | collective-permute-start | bytes 2752520 | tf_op jit(solution)/shard_map/ppermute | solution.py:29
  25.1 20.2 %collective-permute-start.14 = (bf16[28,64,256]{2,1,0:T(8,128)(2,1)}, bf16[28,64,256]{2,1,0:T(8,128)(2,1)S(1)}, u32[]{:S(2)}, u32[]{:S(2)}) collective-permute-start(bf16[28,64,256]{2,1,0:T(8,128)(2,1)} %get-tuple-element.48), channel_id=1, source_target_pairs={{0,8},{1,9},{2,10},{3,11},{4,12},{5,13},{6,14},{7,15},{8,0},{9,1},... | collective-permute-start | bytes 2752520 | tf_op jit(solution)/shard_map/ppermute | solution.py:29
  27.9 13.7 %collective-permute-start.10 = (bf16[4,64,256]{2,1,0:T(8,128)(2,1)S(1)}, bf16[4,64,256]{2,1,0:T(8,128)(2,1)S(1)}, u32[]{:S(2)}, u32[]{:S(2)}) collective-permute-start(bf16[4,64,256]{2,1,0:T(8,128)(2,1)S(1)} %get-tuple-element.46.rest_1_), channel_id=1, source_target_pairs={{0,24},{1,25},{2,26},{3,27},{4,28},{5,29},{6,30},{7,31},{24,0},{25... | collective-permute-start | bytes 393224 | tf_op jit(solution)/shard_map/ppermute | solution.py:29
  29.9 12.6 %collective-permute-start.8 = (bf16[4,64,256]{2,1,0:T(8,128)(2,1)S(1)}, bf16[4,64,256]{2,1,0:T(8,128)(2,1)S(1)}, u32[]{:S(2)}, u32[]{:S(2)}) collective-permute-start(bf16[4,64,256]{2,1,0:T(8,128)(2,1)S(1)} %get-tuple-element.44.rest_1_), channel_id=1, source_target_pairs={{0,16},{1,17},{2,18},{3,19},{4,20},{5,21},{6,22},{7,23},{24,8},{25... | collective-permute-start | bytes 393224 | tf_op jit(solution)/shard_map/ppermute | solution.py:29
  43.4 13.9 %collective-permute-start.11 = (bf16[4,192,256]{2,1,0:T(8,128)(2,1)S(1)}, bf16[4,192,256]{2,1,0:T(8,128)(2,1)S(1)}, u32[]{:S(2)}, u32[]{:S(2)}) collective-permute-start(bf16[4,192,256]{2,1,0:T(8,128)(2,1)S(1)} %pick.7.rest_0_.rest_4_), channel_id=1, source_target_pairs={{0,1},{1,0},{2,3},{3,2},{4,5},{5,4},{6,7},{7,6},{8,24},{9,25},{10,... | collective-permute-start | bytes 1179656 | tf_op jit(solution)/shard_map/ppermute | solution.py:29
  48.3 22.7 %collective-permute-start.17 = (bf16[32,64,256]{2,1,0:T(8,128)(2,1)S(1)}, bf16[32,64,256]{2,1,0:T(8,128)(2,1)}, u32[]{:S(2)}, u32[]{:S(2)}) collective-permute-start(bf16[32,64,256]{2,1,0:T(8,128)(2,1)S(1)} %pick.8.rest_5_), channel_id=1, source_target_pairs={{0,2},{1,3},{6,4},{7,5},{8,10},{9,11},{14,12},{15,13},{16,18},{17,... | collective-permute-start | bytes 3145736 | tf_op jit(solution)/shard_map/ppermute | solution.py:29
  50.5 20.4 %collective-permute-start.19 = (bf16[32,64,256]{2,1,0:T(8,128)(2,1)S(1)}, bf16[32,64,256]{2,1,0:T(8,128)(2,1)}, u32[]{:S(2)}, u32[]{:S(2)}) collective-permute-start(bf16[32,64,256]{2,1,0:T(8,128)(2,1)S(1)} %pick.8.rest_5_), channel_id=1, source_target_pairs={{2,4},{3,5},{4,2},{5,3},{10,12},{11,13},{12,10},{13,11},{18,20},{1... | collective-permute-start | bytes 3145736 | tf_op jit(solution)/shard_map/ppermute | solution.py:29
  56.1 6.9 %collective-permute-start.12 = (bf16[4,192,256]{2,1,0:T(8,128)(2,1)S(1)}, bf16[4,192,256]{2,1,0:T(8,128)(2,1)S(1)}, u32[]{:S(2)}, u32[]{:S(2)}) collective-permute-start(bf16[4,192,256]{2,1,0:T(8,128)(2,1)S(1)} %pick.7.rest_0_.rest_4_), channel_id=1, source_target_pairs={{0,16},{1,17},{2,18},{3,19},{4,20},{5,21},{6,22},{7,23},{8,9},{9,8... | collective-permute-start | bytes 1179656 | tf_op jit(solution)/shard_map/ppermute | solution.py:29
  57.3 9.9 %collective-permute-start.13 = (bf16[4,192,256]{2,1,0:T(8,128)(2,1)S(1)}, bf16[4,192,256]{2,1,0:T(8,128)(2,1)S(1)}, u32[]{:S(2)}, u32[]{:S(2)}) collective-permute-start(bf16[4,192,256]{2,1,0:T(8,128)(2,1)S(1)} %collective-permute-done.11.rest_1_), channel_id=1, source_target_pairs={{0,16},{1,17},{2,18},{3,19},{4,20},{5,21},{6,22},{7,23},{8,9},{9,8... | collective-permute-start | bytes 1179656 | tf_op jit(solution)/shard_map/ppermute | solution.py:29
  67.9 18.5 %collective-permute-start.30 = (bf16[32,64,256]{2,1,0:T(8,128)(2,1)S(1)}, bf16[32,64,256]{2,1,0:T(8,128)(2,1)S(1)}, u32[]{:S(2)}, u32[]{:S(2)}) collective-permute-start(bf16[32,64,256]{2,1,0:T(8,128)(2,1)S(1)} %pick.10), channel_id=1, source_target_pairs={{8,16},{9,17},{10,18},{11,19},{12,20},{13,21},{14,22},{15,23},{16,... | collective-permute-start | bytes 3145736 | tf_op jit(solution)/shard_map/ppermute | solution.py:29
  71.0 25.7 %collective-permute-start.21 = (bf16[32,64,256]{2,1,0:T(8,128)(2,1)S(1)}, bf16[32,64,256]{2,1,0:T(8,128)(2,1)}, u32[]{:S(2)}, u32[]{:S(2)}) collective-permute-start(bf16[32,64,256]{2,1,0:T(8,128)(2,1)S(1)} %pick.8.rest_5_), channel_id=1, source_target_pairs={{0,4},{1,5},{6,2},{7,3},{8,12},{9,13},{14,10},{15,11},{16,20},{17,... | collective-permute-start | bytes 3145736 | tf_op jit(solution)/shard_map/ppermute | solution.py:29
  80.3 19.6 %collective-permute-start.29 = (bf16[32,64,256]{2,1,0:T(8,128)(2,1)}, bf16[32,64,256]{2,1,0:T(8,128)(2,1)}, u32[]{:S(2)}, u32[]{:S(2)}) collective-permute-start(bf16[32,64,256]{2,1,0:T(8,128)(2,1)} %pick.9), channel_id=1, source_target_pairs={{8,24},{9,25},{10,26},{11,27},{12,28},{13,29},{14,30},{15,31},{16,... | collective-permute-start | bytes 3145736 | tf_op jit(solution)/shard_map/ppermute | solution.py:29
  81.6 25.6 %collective-permute-start.16 = (bf16[32,64,256]{2,1,0:T(8,128)(2,1)S(1)}, bf16[32,64,256]{2,1,0:T(8,128)(2,1)}, u32[]{:S(2)}, u32[]{:S(2)}) collective-permute-start(bf16[32,64,256]{2,1,0:T(8,128)(2,1)S(1)} %pick.8.rest_5_), channel_id=1, source_target_pairs={{0,8},{1,9},{2,10},{3,11},{4,12},{5,13},{6,14},{7,15},{8,0},{9,1},... | collective-permute-start | bytes 3145736 | tf_op jit(solution)/shard_map/ppermute | solution.py:29
  86.5 21.5 %collective-permute-start.18 = (bf16[32,64,256]{2,1,0:T(8,128)(2,1)}, bf16[32,64,256]{2,1,0:T(8,128)(2,1)}, u32[]{:S(2)}, u32[]{:S(2)}) collective-permute-start(bf16[32,64,256]{2,1,0:T(8,128)(2,1)} %collective-permute-done.17.rest_7_), channel_id=1, source_target_pairs={{0,8},{1,9},{2,10},{3,11},{4,12},{5,13},{6,14},{7,15},{8,0},{9,1},... | collective-permute-start | bytes 3145736 | tf_op jit(solution)/shard_map/ppermute | solution.py:29
  87.4 20.6 %collective-permute-start.20 = (bf16[32,64,256]{2,1,0:T(8,128)(2,1)}, bf16[32,64,256]{2,1,0:T(8,128)(2,1)}, u32[]{:S(2)}, u32[]{:S(2)}) collective-permute-start(bf16[32,64,256]{2,1,0:T(8,128)(2,1)} %collective-permute-done.19.rest_9_), channel_id=1, source_target_pairs={{0,8},{1,9},{2,10},{3,11},{4,12},{5,13},{6,14},{7,15},{8,0},{9,1},... | collective-permute-start | bytes 3145736 | tf_op jit(solution)/shard_map/ppermute | solution.py:29
  96.7 11.3 %collective-permute-start.22 = (bf16[32,64,256]{2,1,0:T(8,128)(2,1)}, bf16[32,64,256]{2,1,0:T(8,128)(2,1)}, u32[]{:S(2)}, u32[]{:S(2)}) collective-permute-start(bf16[32,64,256]{2,1,0:T(8,128)(2,1)} %collective-permute-done.21.rest_11_), channel_id=1, source_target_pairs={{0,8},{1,9},{2,10},{3,11},{4,12},{5,13},{6,14},{7,15},{8,0},{9,1},... | collective-permute-start | bytes 3145736 | tf_op jit(solution)/shard_map/ppermute | solution.py:29
  103.0 26.4 %collective-permute-start.32 = (bf16[32,64,256]{2,1,0:T(8,128)(2,1)S(1)}, bf16[32,64,256]{2,1,0:T(8,128)(2,1)S(1)}, u32[]{:S(2)}, u32[]{:S(2)}) collective-permute-start(bf16[32,64,256]{2,1,0:T(8,128)(2,1)S(1)} %pick.11.rest_5_), channel_id=1, source_target_pairs={{0,2},{1,3},{6,4},{7,5},{8,10},{9,11},{14,12},{15,13},{16,18},{17,... | collective-permute-start | bytes 3145736 | tf_op jit(solution)/shard_map/ppermute | solution.py:29
  107.2 22.2 %collective-permute-start.34 = (bf16[32,64,256]{2,1,0:T(8,128)(2,1)S(1)}, bf16[32,64,256]{2,1,0:T(8,128)(2,1)S(1)}, u32[]{:S(2)}, u32[]{:S(2)}) collective-permute-start(bf16[32,64,256]{2,1,0:T(8,128)(2,1)S(1)} %pick.11.rest_5_), channel_id=1, source_target_pairs={{2,4},{3,5},{4,2},{5,3},{10,12},{11,13},{12,10},{13,11},{18,20},{1... | collective-permute-start | bytes 3145736 | tf_op jit(solution)/shard_map/ppermute | solution.py:29
  114.2 10.6 %collective-permute-start.23 = (bf16[4,192,256]{2,1,0:T(8,128)(2,1)S(1)}, bf16[4,192,256]{2,1,0:T(8,128)(2,1)S(1)}, u32[]{:S(2)}, u32[]{:S(2)}) collective-permute-start(bf16[4,192,256]{2,1,0:T(8,128)(2,1)S(1)} %attend.4.rest_0_), channel_id=1, source_target_pairs={{0,1},{1,0},{2,3},{3,2},{4,5},{5,4},{6,7},{7,6},{8,24},{9,25},{10,... | collective-permute-start | bytes 1179656 | tf_op jit(solution)/shard_map/ppermute | solution.py:29
  114.8 14.6 %collective-permute-start.24 = (bf16[4,192,256]{2,1,0:T(8,128)(2,1)S(1)}, bf16[4,192,256]{2,1,0:T(8,128)(2,1)S(1)}, u32[]{:S(2)}, u32[]{:S(2)}) collective-permute-start(bf16[4,192,256]{2,1,0:T(8,128)(2,1)S(1)} %attend.4.rest_0_), channel_id=1, source_target_pairs={{0,16},{1,17},{2,18},{3,19},{4,20},{5,21},{6,22},{7,23},{8,9},{9,8... | collective-permute-start | bytes 1179656 | tf_op jit(solution)/shard_map/ppermute | solution.py:29
  124.8 6.9 %collective-permute-start.25 = (bf16[4,192,256]{2,1,0:T(8,128)(2,1)S(1)}, bf16[4,192,256]{2,1,0:T(8,128)(2,1)S(1)}, u32[]{:S(2)}, u32[]{:S(2)}) collective-permute-start(bf16[4,192,256]{2,1,0:T(8,128)(2,1)S(1)} %collective-permute-done.23.rest_1_), channel_id=1, source_target_pairs={{0,16},{1,17},{2,18},{3,19},{4,20},{5,21},{6,22},{7,23},{8,9},{9,8... | collective-permute-start | bytes 1179656 | tf_op jit(solution)/shard_map/ppermute | solution.py:29
  131.7 26.0 %collective-permute-start.36 = (bf16[32,64,256]{2,1,0:T(8,128)(2,1)S(1)}, bf16[32,64,256]{2,1,0:T(8,128)(2,1)S(1)}, u32[]{:S(2)}, u32[]{:S(2)}) collective-permute-start(bf16[32,64,256]{2,1,0:T(8,128)(2,1)S(1)} %pick.11.rest_5_), channel_id=1, source_target_pairs={{0,4},{1,5},{6,2},{7,3},{8,12},{9,13},{14,10},{15,11},{16,20},{17,... | collective-permute-start | bytes 3145736 | tf_op jit(solution)/shard_map/ppermute | solution.py:29
  135.9 29.2 %collective-permute-start.31 = (bf16[32,64,256]{2,1,0:T(8,128)(2,1)S(1)}, bf16[32,64,256]{2,1,0:T(8,128)(2,1)S(1)}, u32[]{:S(2)}, u32[]{:S(2)}) collective-permute-start(bf16[32,64,256]{2,1,0:T(8,128)(2,1)S(1)} %pick.11.rest_5_), channel_id=1, source_target_pairs={{0,8},{1,9},{2,10},{3,11},{4,12},{5,13},{6,14},{7,15},{8,0},{9,1},... | collective-permute-start | bytes 3145736 | tf_op jit(solution)/shard_map/ppermute | solution.py:29
  142.2 7.3 %collective-permute-start.26 = (bf16[4,192,256]{2,1,0:T(8,128)(2,1)S(1)}, bf16[4,192,256]{2,1,0:T(8,128)(2,1)S(1)}, u32[]{:S(2)}, u32[]{:S(2)}) collective-permute-start(bf16[4,192,256]{2,1,0:T(8,128)(2,1)S(1)} %project_out.4.rest_0_.rest_4_), channel_id=1, source_target_pairs={{0,1},{1,0},{2,3},{3,2},{4,5},{5,4},{6,7},{7,6},{8,24},{9,25},{10,... | collective-permute-start | bytes 1179656 | tf_op jit(solution)/shard_map/ppermute | solution.py:29
  144.0 22.0 %collective-permute-start.33 = (bf16[32,64,256]{2,1,0:T(8,128)(2,1)S(1)}, bf16[32,64,256]{2,1,0:T(8,128)(2,1)S(1)}, u32[]{:S(2)}, u32[]{:S(2)}) collective-permute-start(bf16[32,64,256]{2,1,0:T(8,128)(2,1)S(1)} %collective-permute-done.32.rest_7_), channel_id=1, source_target_pairs={{0,8},{1,9},{2,10},{3,11},{4,12},{5,13},{6,14},{7,15},{8,0},{9,1},... | collective-permute-start | bytes 3145736 | tf_op jit(solution)/shard_map/ppermute | solution.py:29
  144.0 22.1 %collective-permute-start.35 = (bf16[32,64,256]{2,1,0:T(8,128)(2,1)S(1)}, bf16[32,64,256]{2,1,0:T(8,128)(2,1)S(1)}, u32[]{:S(2)}, u32[]{:S(2)}) collective-permute-start(bf16[32,64,256]{2,1,0:T(8,128)(2,1)S(1)} %collective-permute-done.34.rest_9_), channel_id=1, source_target_pairs={{0,8},{1,9},{2,10},{3,11},{4,12},{5,13},{6,14},{7,15},{8,0},{9,1},... | collective-permute-start | bytes 3145736 | tf_op jit(solution)/shard_map/ppermute | solution.py:29
  157.6 19.6 %collective-permute-start.37 = (bf16[32,64,256]{2,1,0:T(8,128)(2,1)S(1)}, bf16[32,64,256]{2,1,0:T(8,128)(2,1)S(1)}, u32[]{:S(2)}, u32[]{:S(2)}) collective-permute-start(bf16[32,64,256]{2,1,0:T(8,128)(2,1)S(1)} %collective-permute-done.36.rest_11_), channel_id=1, source_target_pairs={{0,8},{1,9},{2,10},{3,11},{4,12},{5,13},{6,14},{7,15},{8,0},{9,1},... | collective-permute-start | bytes 3145736 | tf_op jit(solution)/shard_map/ppermute | solution.py:29
  160.2 27.4 %collective-permute-start.45 = (bf16[32,64,256]{2,1,0:T(8,128)(2,1)S(1)}, bf16[32,64,256]{2,1,0:T(8,128)(2,1)S(1)}, u32[]{:S(2)}, u32[]{:S(2)}) collective-permute-start(bf16[32,64,256]{2,1,0:T(8,128)(2,1)S(1)} %pick.12.rest_5_), channel_id=1, source_target_pairs={{0,2},{1,3},{6,4},{7,5},{8,10},{9,11},{14,12},{15,13},{16,18},{17,... | collective-permute-start | bytes 3145736 | tf_op jit(solution)/shard_map/ppermute | solution.py:29
  165.1 22.5 %collective-permute-start.47 = (bf16[32,64,256]{2,1,0:T(8,128)(2,1)S(1)}, bf16[32,64,256]{2,1,0:T(8,128)(2,1)S(1)}, u32[]{:S(2)}, u32[]{:S(2)}) collective-permute-start(bf16[32,64,256]{2,1,0:T(8,128)(2,1)S(1)} %pick.12.rest_5_), channel_id=1, source_target_pairs={{2,4},{3,5},{4,2},{5,3},{10,12},{11,13},{12,10},{13,11},{18,20},{1... | collective-permute-start | bytes 3145736 | tf_op jit(solution)/shard_map/ppermute | solution.py:29
  166.0 7.0 %collective-permute-start.27 = (bf16[4,192,256]{2,1,0:T(8,128)(2,1)S(1)}, bf16[4,192,256]{2,1,0:T(8,128)(2,1)S(1)}, u32[]{:S(2)}, u32[]{:S(2)}) collective-permute-start(bf16[4,192,256]{2,1,0:T(8,128)(2,1)S(1)} %project_out.4.rest_0_.rest_4_), channel_id=1, source_target_pairs={{0,16},{1,17},{2,18},{3,19},{4,20},{5,21},{6,22},{7,23},{8,9},{9,8... | collective-permute-start | bytes 1179656 | tf_op jit(solution)/shard_map/ppermute | solution.py:29
  166.1 11.1 %collective-permute-start.28 = (bf16[4,192,256]{2,1,0:T(8,128)(2,1)S(1)}, bf16[4,192,256]{2,1,0:T(8,128)(2,1)S(1)}, u32[]{:S(2)}, u32[]{:S(2)}) collective-permute-start(bf16[4,192,256]{2,1,0:T(8,128)(2,1)S(1)} %collective-permute-done.26.rest_1_), channel_id=1, source_target_pairs={{0,16},{1,17},{2,18},{3,19},{4,20},{5,21},{6,22},{7,23},{8,9},{9,8... | collective-permute-start | bytes 1179656 | tf_op jit(solution)/shard_map/ppermute | solution.py:29
  181.9 7.0 %collective-permute-start.38 = (bf16[4,192,256]{2,1,0:T(8,128)(2,1)S(1)}, bf16[4,192,256]{2,1,0:T(8,128)(2,1)S(1)}, u32[]{:S(2)}, u32[]{:S(2)}) collective-permute-start(bf16[4,192,256]{2,1,0:T(8,128)(2,1)S(1)} %get-tuple-element.60.rest_0_), channel_id=1, source_target_pairs={{0,1},{1,0},{2,3},{3,2},{4,5},{5,4},{6,7},{7,6},{8,24},{9,25},{10,... | collective-permute-start | bytes 1179656 | tf_op jit(solution)/shard_map/ppermute | solution.py:29
  188.9 25.5 %collective-permute-start.49 = (bf16[32,64,256]{2,1,0:T(8,128)(2,1)S(1)}, bf16[32,64,256]{2,1,0:T(8,128)(2,1)S(1)}, u32[]{:S(2)}, u32[]{:S(2)}) collective-permute-start(bf16[32,64,256]{2,1,0:T(8,128)(2,1)S(1)} %pick.12.rest_5_), channel_id=1, source_target_pairs={{0,4},{1,5},{6,2},{7,3},{8,12},{9,13},{14,10},{15,11},{16,20},{17,... | collective-permute-start | bytes 3145736 | tf_op jit(solution)/shard_map/ppermute | solution.py:29
  193.3 7.0 %collective-permute-start.39 = (bf16[4,192,256]{2,1,0:T(8,128)(2,1)S(1)}, bf16[4,192,256]{2,1,0:T(8,128)(2,1)S(1)}, u32[]{:S(2)}, u32[]{:S(2)}) collective-permute-start(bf16[4,192,256]{2,1,0:T(8,128)(2,1)S(1)} %get-tuple-element.60.rest_0_), channel_id=1, source_target_pairs={{0,16},{1,17},{2,18},{3,19},{4,20},{5,21},{6,22},{7,23},{8,9},{9,8... | collective-permute-start | bytes 1179656 | tf_op jit(solution)/shard_map/ppermute | solution.py:29
  193.4 11.1 %collective-permute-start.40 = (bf16[4,192,256]{2,1,0:T(8,128)(2,1)S(1)}, bf16[4,192,256]{2,1,0:T(8,128)(2,1)S(1)}, u32[]{:S(2)}, u32[]{:S(2)}) collective-permute-start(bf16[4,192,256]{2,1,0:T(8,128)(2,1)S(1)} %collective-permute-done.38.rest_1_), channel_id=1, source_target_pairs={{0,16},{1,17},{2,18},{3,19},{4,20},{5,21},{6,22},{7,23},{8,9},{9,8... | collective-permute-start | bytes 1179656 | tf_op jit(solution)/shard_map/ppermute | solution.py:29
  194.8 27.6 %collective-permute-start.44 = (bf16[32,64,256]{2,1,0:T(8,128)(2,1)S(1)}, bf16[32,64,256]{2,1,0:T(8,128)(2,1)S(1)}, u32[]{:S(2)}, u32[]{:S(2)}) collective-permute-start(bf16[32,64,256]{2,1,0:T(8,128)(2,1)S(1)} %pick.12.rest_5_), channel_id=1, source_target_pairs={{0,8},{1,9},{2,10},{3,11},{4,12},{5,13},{6,14},{7,15},{8,0},{9,1},... | collective-permute-start | bytes 3145736 | tf_op jit(solution)/shard_map/ppermute | solution.py:29
  206.7 7.0 %collective-permute-start.41 = (bf16[4,192,256]{2,1,0:T(8,128)(2,1)S(1)}, bf16[4,192,256]{2,1,0:T(8,128)(2,1)S(1)}, u32[]{:S(2)}, u32[]{:S(2)}) collective-permute-start(bf16[4,192,256]{2,1,0:T(8,128)(2,1)S(1)} %project_out.5.rest_0_.rest_4_), channel_id=1, source_target_pairs={{0,1},{1,0},{2,3},{3,2},{4,5},{5,4},{6,7},{7,6},{8,24},{9,25},{10,... | collective-permute-start | bytes 1179656 | tf_op jit(solution)/shard_map/ppermute | solution.py:29
  206.8 17.3 %collective-permute-start.46 = (bf16[32,64,256]{2,1,0:T(8,128)(2,1)S(1)}, bf16[32,64,256]{2,1,0:T(8,128)(2,1)S(1)}, u32[]{:S(2)}, u32[]{:S(2)}) collective-permute-start(bf16[32,64,256]{2,1,0:T(8,128)(2,1)S(1)} %collective-permute-done.45.rest_7_), channel_id=1, source_target_pairs={{0,8},{1,9},{2,10},{3,11},{4,12},{5,13},{6,14},{7,15},{8,0},{9,1},... | collective-permute-start | bytes 3145736 | tf_op jit(solution)/shard_map/ppermute | solution.py:29
  209.4 14.6 %collective-permute-start.48 = (bf16[32,64,256]{2,1,0:T(8,128)(2,1)S(1)}, bf16[32,64,256]{2,1,0:T(8,128)(2,1)S(1)}, u32[]{:S(2)}, u32[]{:S(2)}) collective-permute-start(bf16[32,64,256]{2,1,0:T(8,128)(2,1)S(1)} %collective-permute-done.47.rest_9_), channel_id=1, source_target_pairs={{0,8},{1,9},{2,10},{3,11},{4,12},{5,13},{6,14},{7,15},{8,0},{9,1},... | collective-permute-start | bytes 3145736 | tf_op jit(solution)/shard_map/ppermute | solution.py:29
  214.4 20.8 %collective-permute-start.50 = (bf16[32,64,256]{2,1,0:T(8,128)(2,1)S(1)}, bf16[32,64,256]{2,1,0:T(8,128)(2,1)S(1)}, u32[]{:S(2)}, u32[]{:S(2)}) collective-permute-start(bf16[32,64,256]{2,1,0:T(8,128)(2,1)S(1)} %collective-permute-done.49.rest_11_), channel_id=1, source_target_pairs={{0,8},{1,9},{2,10},{3,11},{4,12},{5,13},{6,14},{7,15},{8,0},{9,1},... | collective-permute-start | bytes 3145736 | tf_op jit(solution)/shard_map/ppermute | solution.py:29
  217.9 27.0 %collective-permute-start.58 = (bf16[32,64,256]{2,1,0:T(8,128)(2,1)S(1)}, bf16[32,64,256]{2,1,0:T(8,128)(2,1)S(1)}, u32[]{:S(2)}, u32[]{:S(2)}) collective-permute-start(bf16[32,64,256]{2,1,0:T(8,128)(2,1)S(1)} %pick.13.rest_5_), channel_id=1, source_target_pairs={{0,2},{1,3},{6,4},{7,5},{8,10},{9,11},{14,12},{15,13},{16,18},{17,... | collective-permute-start | bytes 3145736 | tf_op jit(solution)/shard_map/ppermute | solution.py:29
  222.4 22.5 %collective-permute-start.60 = (bf16[32,64,256]{2,1,0:T(8,128)(2,1)S(1)}, bf16[32,64,256]{2,1,0:T(8,128)(2,1)}, u32[]{:S(2)}, u32[]{:S(2)}) collective-permute-start(bf16[32,64,256]{2,1,0:T(8,128)(2,1)S(1)} %pick.13.rest_5_), channel_id=1, source_target_pairs={{2,4},{3,5},{4,2},{5,3},{10,12},{11,13},{12,10},{13,11},{18,20},{1... | collective-permute-start | bytes 3145736 | tf_op jit(solution)/shard_map/ppermute | solution.py:29
  224.1 6.9 %collective-permute-start.42 = (bf16[4,192,256]{2,1,0:T(8,128)(2,1)S(1)}, bf16[4,192,256]{2,1,0:T(8,128)(2,1)S(1)}, u32[]{:S(2)}, u32[]{:S(2)}) collective-permute-start(bf16[4,192,256]{2,1,0:T(8,128)(2,1)S(1)} %project_out.5.rest_0_.rest_4_), channel_id=1, source_target_pairs={{0,16},{1,17},{2,18},{3,19},{4,20},{5,21},{6,22},{7,23},{8,9},{9,8... | collective-permute-start | bytes 1179656 | tf_op jit(solution)/shard_map/ppermute | solution.py:29
  224.1 11.1 %collective-permute-start.43 = (bf16[4,192,256]{2,1,0:T(8,128)(2,1)S(1)}, bf16[4,192,256]{2,1,0:T(8,128)(2,1)S(1)}, u32[]{:S(2)}, u32[]{:S(2)}) collective-permute-start(bf16[4,192,256]{2,1,0:T(8,128)(2,1)S(1)} %collective-permute-done.41.rest_1_), channel_id=1, source_target_pairs={{0,16},{1,17},{2,18},{3,19},{4,20},{5,21},{6,22},{7,23},{8,9},{9,8... | collective-permute-start | bytes 1179656 | tf_op jit(solution)/shard_map/ppermute | solution.py:29
  239.9 7.0 %collective-permute-start.51 = (bf16[4,192,256]{2,1,0:T(8,128)(2,1)S(1)}, bf16[4,192,256]{2,1,0:T(8,128)(2,1)S(1)}, u32[]{:S(2)}, u32[]{:S(2)}) collective-permute-start(bf16[4,192,256]{2,1,0:T(8,128)(2,1)S(1)} %get-tuple-element.64.rest_0_), channel_id=1, source_target_pairs={{0,1},{1,0},{2,3},{3,2},{4,5},{5,4},{6,7},{7,6},{8,24},{9,25},{10,... | collective-permute-start | bytes 1179656 | tf_op jit(solution)/shard_map/ppermute | solution.py:29
  246.8 25.3 %collective-permute-start.62 = (bf16[32,64,256]{2,1,0:T(8,128)(2,1)S(1)}, bf16[32,64,256]{2,1,0:T(8,128)(2,1)}, u32[]{:S(2)}, u32[]{:S(2)}) collective-permute-start(bf16[32,64,256]{2,1,0:T(8,128)(2,1)S(1)} %pick.13.rest_5_), channel_id=1, source_target_pairs={{0,4},{1,5},{6,2},{7,3},{8,12},{9,13},{14,10},{15,11},{16,20},{17,... | collective-permute-start | bytes 3145736 | tf_op jit(solution)/shard_map/ppermute | solution.py:29
  251.7 6.9 %collective-permute-start.52 = (bf16[4,192,256]{2,1,0:T(8,128)(2,1)S(1)}, bf16[4,192,256]{2,1,0:T(8,128)(2,1)S(1)}, u32[]{:S(2)}, u32[]{:S(2)}) collective-permute-start(bf16[4,192,256]{2,1,0:T(8,128)(2,1)S(1)} %get-tuple-element.64.rest_0_), channel_id=1, source_target_pairs={{0,16},{1,17},{2,18},{3,19},{4,20},{5,21},{6,22},{7,23},{8,9},{9,8... | collective-permute-start | bytes 1179656 | tf_op jit(solution)/shard_map/ppermute | solution.py:29
  251.7 11.1 %collective-permute-start.53 = (bf16[4,192,256]{2,1,0:T(8,128)(2,1)S(1)}, bf16[4,192,256]{2,1,0:T(8,128)(2,1)S(1)}, u32[]{:S(2)}, u32[]{:S(2)}) collective-permute-start(bf16[4,192,256]{2,1,0:T(8,128)(2,1)S(1)} %collective-permute-done.51.rest_1_), channel_id=1, source_target_pairs={{0,16},{1,17},{2,18},{3,19},{4,20},{5,21},{6,22},{7,23},{8,9},{9,8... | collective-permute-start | bytes 1179656 | tf_op jit(solution)/shard_map/ppermute | solution.py:29
  265.0 7.0 %collective-permute-start.54 = (bf16[4,192,256]{2,1,0:T(8,128)(2,1)S(1)}, bf16[4,192,256]{2,1,0:T(8,128)(2,1)S(1)}, u32[]{:S(2)}, u32[]{:S(2)}) collective-permute-start(bf16[4,192,256]{2,1,0:T(8,128)(2,1)S(1)} %project_out.6.rest_0_.rest_4_), channel_id=1, source_target_pairs={{0,1},{1,0},{2,3},{3,2},{4,5},{5,4},{6,7},{7,6},{8,24},{9,25},{10,... | collective-permute-start | bytes 1179656 | tf_op jit(solution)/shard_map/ppermute | solution.py:29
  265.1 9.8 %collective-permute-start.57 = (bf16[32,64,256]{2,1,0:T(8,128)(2,1)S(1)}, bf16[32,64,256]{2,1,0:T(8,128)(2,1)S(1)}, u32[]{:S(2)}, u32[]{:S(2)}) collective-permute-start(bf16[32,64,256]{2,1,0:T(8,128)(2,1)S(1)} %pick.13.rest_5_), channel_id=1, source_target_pairs={{0,8},{1,9},{2,10},{3,11},{4,12},{5,13},{6,14},{7,15},{8,0},{9,1},... | collective-permute-start | bytes 3145736 | tf_op jit(solution)/shard_map/ppermute | solution.py:29
  267.5 9.9 %collective-permute-start.59 = (bf16[32,64,256]{2,1,0:T(8,128)(2,1)S(1)}, bf16[32,64,256]{2,1,0:T(8,128)(2,1)}, u32[]{:S(2)}, u32[]{:S(2)}) collective-permute-start(bf16[32,64,256]{2,1,0:T(8,128)(2,1)S(1)} %collective-permute-done.58.rest_7_), channel_id=1, source_target_pairs={{0,8},{1,9},{2,10},{3,11},{4,12},{5,13},{6,14},{7,15},{8,0},{9,1},... | collective-permute-start | bytes 3145736 | tf_op jit(solution)/shard_map/ppermute | solution.py:29
  267.5 11.4 %collective-permute-start.61 = (bf16[32,64,256]{2,1,0:T(8,128)(2,1)}, bf16[32,64,256]{2,1,0:T(8,128)(2,1)}, u32[]{:S(2)}, u32[]{:S(2)}) collective-permute-start(bf16[32,64,256]{2,1,0:T(8,128)(2,1)} %collective-permute-done.60.rest_9_), channel_id=1, source_target_pairs={{0,8},{1,9},{2,10},{3,11},{4,12},{5,13},{6,14},{7,15},{8,0},{9,1},... | collective-permute-start | bytes 3145736 | tf_op jit(solution)/shard_map/ppermute | solution.py:29
  272.2 14.0 %collective-permute-start.63 = (bf16[32,64,256]{2,1,0:T(8,128)(2,1)}, bf16[32,64,256]{2,1,0:T(8,128)(2,1)}, u32[]{:S(2)}, u32[]{:S(2)}) collective-permute-start(bf16[32,64,256]{2,1,0:T(8,128)(2,1)} %collective-permute-done.62.rest_11_), channel_id=1, source_target_pairs={{0,8},{1,9},{2,10},{3,11},{4,12},{5,13},{6,14},{7,15},{8,0},{9,1},... | collective-permute-start | bytes 3145736 | tf_op jit(solution)/shard_map/ppermute | solution.py:29
  275.0 7.0 %collective-permute-start.55 = (bf16[4,192,256]{2,1,0:T(8,128)(2,1)S(1)}, bf16[4,192,256]{2,1,0:T(8,128)(2,1)}, u32[]{:S(2)}, u32[]{:S(2)}) collective-permute-start(bf16[4,192,256]{2,1,0:T(8,128)(2,1)S(1)} %project_out.6.rest_0_.rest_4_), channel_id=1, source_target_pairs={{0,16},{1,17},{2,18},{3,19},{4,20},{5,21},{6,22},{7,23},{8,9},{9,8... | collective-permute-start | bytes 1179656 | tf_op jit(solution)/shard_map/ppermute | solution.py:29
  275.9 10.3 %collective-permute-start.56 = (bf16[4,192,256]{2,1,0:T(8,128)(2,1)S(1)}, bf16[4,192,256]{2,1,0:T(8,128)(2,1)}, u32[]{:S(2)}, u32[]{:S(2)}) collective-permute-start(bf16[4,192,256]{2,1,0:T(8,128)(2,1)S(1)} %collective-permute-done.54.rest_1_), channel_id=1, source_target_pairs={{0,16},{1,17},{2,18},{3,19},{4,20},{5,21},{6,22},{7,23},{8,9},{9,8... | collective-permute-start | bytes 1179656 | tf_op jit(solution)/shard_map/ppermute | solution.py:29
  277.4 26.1 %collective-permute-start.65 = (bf16[192,2048]{1,0:T(8,128)(2,1)}, bf16[192,2048]{1,0:T(8,128)(2,1)S(1)}, u32[]{:S(2)}, u32[]{:S(2)}) collective-permute-start(bf16[192,2048]{1,0:T(8,128)(2,1)} %copy-done.22), channel_id=1, source_target_pairs={{2,10},{3,11},{4,12},{5,13},{10,8},{11,9},{12,14},{13,15},{18,26},... | collective-permute-start | bytes 2359304 | tf_op jit(solution)/shard_map/ppermute | solution.py:29
  293.8 9.7 %collective-permute-start.64 = (bf16[192,2048]{1,0:T(8,128)(2,1)S(1)}, bf16[192,2048]{1,0:T(8,128)(2,1)S(1)}, u32[]{:S(2)}, u32[]{:S(2)}) collective-permute-start(bf16[192,2048]{1,0:T(8,128)(2,1)S(1)} %broadcast_select_fusion), channel_id=1, source_target_pairs={{2,2},{3,3},{4,4},{5,5},{10,0},{11,1},{12,6},{13,7},{18,18},{19,19... | collective-permute-start | bytes 2359304 | tf_op jit(solution)/shard_map/ppermute | solution.py:29
  294.5 9.0 %collective-permute-start.66 = (bf16[4,192,256]{2,1,0:T(8,128)(2,1)S(1)}, bf16[4,192,256]{2,1,0:T(8,128)(2,1)S(1)}, u32[]{:S(2)}, u32[]{:S(2)}) collective-permute-start(bf16[4,192,256]{2,1,0:T(8,128)(2,1)S(1)} %get-tuple-element.72.rest_0_), channel_id=1, source_target_pairs={{0,1},{1,0},{2,3},{3,2},{4,5},{5,4},{6,7},{7,6},{8,24},{9,25},{10,... | collective-permute-start | bytes 1179656 | tf_op jit(solution)/shard_map/ppermute | solution.py:29
  294.6 9.3 %collective-permute-start.67 = (bf16[4,192,256]{2,1,0:T(8,128)(2,1)S(1)}, bf16[4,192,256]{2,1,0:T(8,128)(2,1)S(1)}, u32[]{:S(2)}, u32[]{:S(2)}) collective-permute-start(bf16[4,192,256]{2,1,0:T(8,128)(2,1)S(1)} %get-tuple-element.72.rest_0_), channel_id=1, source_target_pairs={{0,16},{1,17},{2,18},{3,19},{4,20},{5,21},{6,22},{7,23},{8,9},{9,8... | collective-permute-start | bytes 1179656 | tf_op jit(solution)/shard_map/ppermute | solution.py:29
  313.1 11.7 %collective-permute-start.69 = (bf16[4,192,256]{2,1,0:T(8,128)(2,1)S(1)}, bf16[4,192,256]{2,1,0:T(8,128)(2,1)S(1)}, u32[]{:S(2)}, u32[]{:S(2)}) collective-permute-start(bf16[4,192,256]{2,1,0:T(8,128)(2,1)S(1)} %project_out.7), channel_id=1, source_target_pairs={{2,26},{3,27},{4,28},{5,29},{10,24},{11,25},{12,30},{13,31}} | collective-permute-start | bytes 1179656 | tf_op jit(solution)/shard_map/ppermute | solution.py:29
  314.4 12.6 %collective-permute-start.70 = (bf16[4,192,256]{2,1,0:T(8,128)(2,1)S(1)}, bf16[4,192,256]{2,1,0:T(8,128)(2,1)S(1)}, u32[]{:S(2)}, u32[]{:S(2)}) collective-permute-start(bf16[4,192,256]{2,1,0:T(8,128)(2,1)S(1)} %project_out.7), channel_id=1, source_target_pairs={{18,26},{19,27},{20,28},{21,29},{26,24},{27,25},{28,30},{29,31}} | collective-permute-start | bytes 1179656 | tf_op jit(solution)/shard_map/ppermute | solution.py:29
  (42 other events, 316.5 us)

commit v2 on v1

--- a/solution.py
+++ b/solution.py
@@ -387,8 +387,8 @@
     by_second = lambda p, z, x: (p, z, 1 - x) if p & 1 else (p ^ 2, z, x)
 
     def share(value):
-        first = send(value, by_first)
-        return [value, first, send(value, by_second), send(first, by_second)]
+        first, second = send(value, by_first), send(value, by_second)
+        return [value, first, second, send(after(first, second), by_second)]
 
     def exchange(values, ways):
         return {
@@ -409,7 +409,8 @@
 
         def first_leg(piece, *tie):
             piece = after(piece, *tie) if tie else piece
-            return [piece, send(piece, step(near_z)), send(piece, step(swap_z))]
+            swapped = send(piece, step(swap_z))
+            return [piece, send(piece, step(near_z)), swapped]
 
         def second_leg(leg, *tie):
             return leg + [send(after(leg[0], *leg[1:], *tie), step(far_z))]
@@ -453,6 +454,7 @@
     round_b = exchange(both_for, [(2, (1, 2)), (3, (1, 2))])
     round_b[1, (0, 1, 2, 3)] = round_a[1, (0, 1, 2, 3)]
     leg = second_leg(leg, pieces[1], packed)
+    coming = None
     most = with_core(leg[:-1])
     in_count = 3 * per * cols
     out_count = leg[0].shape[0] - in_count
@@ -461,11 +463,11 @@
         last_leg = leg[-1:]
         if s > 0:
             pieces = share(u)
-            last_leg = [after(part, pieces[1]) for part in last_leg]
+            last_leg = [after(part, pieces[3]) for part in last_leg]
         weights = most + with_core(last_leg)
         if s + 1 < sections:
-            came = round_b if s + 1 in (1, 2) else round_a
-            leg = first_leg(piece_of(s + 1, came), *last_leg)
+            coming = piece_of(1, round_b) if s == 0 else coming
+            leg = first_leg(coming, *last_leg)
         heads, *before = attend(s, me, lists, packed, pos, mask, pieces, in_count, weights)
         if s > 0:
             core = (s - 1) & 1
@@ -474,7 +476,11 @@
             results = [deliver(core) for core in range(2)]
         pieces = share(heads)
         if s + 1 < sections:
-            leg = second_leg(leg, *(pieces[1:] if s == 0 else pieces[1:2]))
+            tie = pieces[1:]
+            if s + 2 < sections:
+                coming = piece_of(s + 2, round_b if s == 0 else round_a)
+                tie = [*tie, coming]
+            leg = second_leg(leg, *tie)
             most = with_core(leg[:-1])
         if s == sections - 1:
             pieces[0] = after(pieces[0], *results)

time: 332 us -> 320 us (0.964)
  waiting for transfers between devices: 158 us -> 129 us
  starting transfers between devices: 104 us -> 118 us
    ppermute x71, waiting for transfers between devices: 158 us -> 129 us  [hop(): return lax.ppermute(value, AXES, pairs)]
    ppermute x71, starting transfers between devices: 104 us -> 118 us  [hop(): return lax.ppermute(value, AXES, pairs)]
    unnamed x70 -> x74, local copies, waits for them, and re-layouts: 11.9 us -> 15.1 us
  transfers between devices with their start and end apart: 71 -> 71, of which waited for: 38 -> 39; matrix products, arithmetic and copies ran while one was open for 0% -> 0% of each run, Pallas kernels for 12% -> 13%
where the time goes in v2:
time: 320 us; the launch traced here: 319 us
  waiting for transfers between devices  129 us (40%)
  starting transfers between devices  118 us (37%)
  Pallas kernels  51.6 us (16%)
  local copies, waits for them, and re-layouts  17.8 us (6%)
    ppermute x71, waiting for transfers between devices, hop(): return lax.ppermute(value, AXES, pairs)  129 us
    ppermute x71, starting transfers between devices, hop(): return lax.ppermute(value, AXES, pairs)  118 us
    pallas_call x4, Pallas kernels, attend(): pl.pallas_call(functools.partial(attend_kernel, section, len(parts), rows...  21.4 us
    unnamed x74, local copies, waits for them, and re-layouts  15.1 us
    pallas_call x7, Pallas kernels, pick(): pl.pallas_call(functools.partial(pick_kernel, choice, tuple((len(candidat...  11.5 us
    pallas_call x4, Pallas kernels, project_out(): pl.pallas_call(functools.partial(output_kernel, section, first, len(parts...  9.91 us
  transfers between devices with their start and end apart: 71, of which 39 were waited for; matrix products, arithmetic and copies ran while one was open for 0% of the time, Pallas kernels for 13%

profile of v2, /device:TPU:5, one launch (start us, length us, event | category | flops | bytes accessed | tf_op | source)
XLA Modules:
  0.0 318.6 jit_solution(9157522074280258936)
XLA Ops:
  2.6 6.4 %cut.1 = (bf16[28,64,256]{2,1,0:T(8,128)(2,1)S(1)}, bf16[28,64,256]{2,1,0:T(8,128)(2,1)}, bf16[28,64,256]{2,1,0:T(8,128)(2,1)}, bf16[28,64,256]{2,1,0:T(8,128)(2,1)}) custom-call(s32[2]{0:T(128)S(1)} %pad_add_fusion.me_ref, bf16[1,4,8,64,256]{4,3,2,1,0:T(8,128)(2,1)S(1)} %copy-done.8, bf16[1,4,8,64,256]{4,3,2,1,0:T(8,128)(2,1)S(1)} %copy-done.9, ...), custom_call_target="tpu_custom_call" | custom-call | flops 1000000000 | tf_op jit(solution)/shard_map/cut/pallas_call | solution.py:293
  9.6 2.3 prepare.1
  13.3 3.9 %collective-permute-start.5 = (bf16[4,192,256]{2,1,0:T(8,128)(2,1)}, bf16[4,192,256]{2,1,0:T(8,128)(2,1)}, u32[]{:S(2)}, u32[]{:S(2)}) collective-permute-start(bf16[4,192,256]{2,1,0:T(8,128)(2,1)} %get-tuple-element.50.rest_0_), channel_id=1, source_target_pairs={{8,10},{9,11},{14,12},{15,13},{24,26},{25,27},{30,28},{31,29}} | collective-permute-start | bytes 1179656 | tf_op jit(solution)/shard_map/ppermute | solution.py:29
  17.2 2.2 collective-permute-start.6
  19.4 1.9 collective-permute-start.9
  21.3 3.0 collective-permute-start.4
  28.0 1.9 collective-permute-start.10
  31.2 10.4 %collective-permute-done.10.rest_3_ = bf16[4,64,256]{2,1,0:T(8,128)(2,1)S(1)} collective-permute-done((bf16[4,64,256]{2,1,0:T(8,128)(2,1)S(1)}, bf16[4,64,256]{2,1,0:T(8,128)(2,1)S(1)}, u32[]{:S(2)}, u32[]{:S(2)}) %collective-permute-start.10) | collective-permute-done | bytes 131104 | tf_op jit(solution)/shard_map/ppermute | solution.py:29
  43.4 1.9 collective-permute-start.11
  46.8 1.7 pick.8.rest_5_
  48.5 2.3 collective-permute-start.17
  54.0 2.2 collective-permute-start.1
  56.9 1.9 collective-permute-start.2
  60.4 1.7 pick.10
  62.1 3.4 %collective-permute-done.13.rest_3_ = bf16[4,192,256]{2,1,0:T(8,128)(2,1)S(1)} collective-permute-done((bf16[4,192,256]{2,1,0:T(8,128)(2,1)S(1)}, bf16[4,192,256]{2,1,0:T(8,128)(2,1)S(1)}, u32[]{:S(2)}, u32[]{:S(2)}) %collective-permute-start.13) | collective-permute-done | bytes 393248 | tf_op jit(solution)/shard_map/ppermute | solution.py:29
  67.0 4.6 %collective-permute-done.17.rest_7_ = bf16[32,64,256]{2,1,0:T(8,128)(2,1)} collective-permute-done((bf16[32,64,256]{2,1,0:T(8,128)(2,1)S(1)}, bf16[32,64,256]{2,1,0:T(8,128)(2,1)}, u32[]{:S(2)}, u32[]{:S(2)}) %collective-permute-start.17) | collective-permute-done | bytes 1048608 | tf_op jit(solution)/shard_map/ppermute | solution.py:29
  71.5 6.2 %collective-permute-start.21 = (bf16[32,64,256]{2,1,0:T(8,128)(2,1)S(1)}, bf16[32,64,256]{2,1,0:T(8,128)(2,1)}, u32[]{:S(2)}, u32[]{:S(2)}) collective-permute-start(bf16[32,64,256]{2,1,0:T(8,128)(2,1)S(1)} %pick.8.rest_5_), channel_id=1, source_target_pairs={{0,4},{1,5},{6,2},{7,3},{8,12},{9,13},{14,10},{15,11},{16,20},{17,... | collective-permute-start | bytes 3145736 | tf_op jit(solution)/shard_map/ppermute | solution.py:29
  77.7 2.7 pick.9
  81.7 5.0 %collective-permute-start.16 = (bf16[32,64,256]{2,1,0:T(8,128)(2,1)S(1)}, bf16[32,64,256]{2,1,0:T(8,128)(2,1)}, u32[]{:S(2)}, u32[]{:S(2)}) collective-permute-start(bf16[32,64,256]{2,1,0:T(8,128)(2,1)S(1)} %pick.8.rest_5_), channel_id=1, source_target_pairs={{0,8},{1,9},{2,10},{3,11},{4,12},{5,13},{6,14},{7,15},{8,0},{9,1},... | collective-permute-start | bytes 3145736 | tf_op jit(solution)/shard_map/ppermute | solution.py:29
  88.2 8.7 %collective-permute-done.21.rest_11_ = bf16[32,64,256]{2,1,0:T(8,128)(2,1)} collective-permute-done((bf16[32,64,256]{2,1,0:T(8,128)(2,1)S(1)}, bf16[32,64,256]{2,1,0:T(8,128)(2,1)}, u32[]{:S(2)}, u32[]{:S(2)}) %collective-permute-start.21) | collective-permute-done | bytes 1048608 | tf_op jit(solution)/shard_map/ppermute | solution.py:29
  96.9 3.2 collective-permute-start.22
  101.4 1.8 pick.11.rest_5_
  103.2 4.2 %collective-permute-start.32 = (bf16[32,64,256]{2,1,0:T(8,128)(2,1)S(1)}, bf16[32,64,256]{2,1,0:T(8,128)(2,1)S(1)}, u32[]{:S(2)}, u32[]{:S(2)}) collective-permute-start(bf16[32,64,256]{2,1,0:T(8,128)(2,1)S(1)} %pick.11.rest_5_), channel_id=1, source_target_pairs={{0,2},{1,3},{6,4},{7,5},{8,10},{9,11},{14,12},{15,13},{16,18},{17,... | collective-permute-start | bytes 3145736 | tf_op jit(solution)/shard_map/ppermute | solution.py:29
  108.2 6.1 %attend.4.rest_0_ = bf16[4,192,256]{2,1,0:T(8,128)(2,1)S(1)} custom-call(s32[2]{0:T(128)S(1)} %pad_add_fusion.me_ref, f32[4,128]{1,0:T(4,128)S(1)} %slice.20.list_ref, s32[4]{0:T(128)S(1)} %broadcast_select_fusion.2.pos_ref, s32[3,4,4]{2,1,0:T(4,128)S(1)} %broadcast_select_fusion.1.mask_ref, bf16[4,192,256]{2,1,0:T(8,128)(2,1)S(1)} %copy-done.7, ...), custom_call_target="tpu_custom_call" | custom-call | flops 1000000000 | tf_op jit(solution)/shard_map/attend/pallas_call | solution.py:252
  115.6 8.7 %collective-permute-done.23.rest_1_ = bf16[4,192,256]{2,1,0:T(8,128)(2,1)S(1)} collective-permute-done((bf16[4,192,256]{2,1,0:T(8,128)(2,1)S(1)}, bf16[4,192,256]{2,1,0:T(8,128)(2,1)S(1)}, u32[]{:S(2)}, u32[]{:S(2)}) %collective-permute-start.23) | collective-permute-done | bytes 393248 | tf_op jit(solution)/shard_map/ppermute | solution.py:29
  127.5 2.0 collective-permute-done.32.rest_7_
  129.6 2.5 collective-permute-done.25.rest_3_
  132.0 4.0 %collective-permute-start.36 = (bf16[32,64,256]{2,1,0:T(8,128)(2,1)S(1)}, bf16[32,64,256]{2,1,0:T(8,128)(2,1)S(1)}, u32[]{:S(2)}, u32[]{:S(2)}) collective-permute-start(bf16[32,64,256]{2,1,0:T(8,128)(2,1)S(1)} %pick.11.rest_5_), channel_id=1, source_target_pairs={{0,4},{1,5},{6,2},{7,3},{8,12},{9,13},{14,10},{15,11},{16,20},{17,... | collective-permute-start | bytes 3145736 | tf_op jit(solution)/shard_map/ppermute | solution.py:29
  138.6 2.8 project_out.4.rest_0_.rest_4_
  142.7 5.6 %collective-permute-done.26.rest_1_ = bf16[4,192,256]{2,1,0:T(8,128)(2,1)S(1)} collective-permute-done((bf16[4,192,256]{2,1,0:T(8,128)(2,1)S(1)}, bf16[4,192,256]{2,1,0:T(8,128)(2,1)S(1)}, u32[]{:S(2)}, u32[]{:S(2)}) %collective-permute-start.26) | collective-permute-done | bytes 393248 | tf_op jit(solution)/shard_map/ppermute | solution.py:29
  150.7 4.0 %collective-permute-start.31 = (bf16[32,64,256]{2,1,0:T(8,128)(2,1)S(1)}, bf16[32,64,256]{2,1,0:T(8,128)(2,1)S(1)}, u32[]{:S(2)}, u32[]{:S(2)}) collective-permute-start(bf16[32,64,256]{2,1,0:T(8,128)(2,1)S(1)} %pick.11.rest_5_), channel_id=1, source_target_pairs={{0,8},{1,9},{2,10},{3,11},{4,12},{5,13},{6,14},{7,15},{8,0},{9,1},... | collective-permute-start | bytes 3145736 | tf_op jit(solution)/shard_map/ppermute | solution.py:29
  157.2 4.0 %collective-permute-start.37 = (bf16[32,64,256]{2,1,0:T(8,128)(2,1)S(1)}, bf16[32,64,256]{2,1,0:T(8,128)(2,1)S(1)}, u32[]{:S(2)}, u32[]{:S(2)}) collective-permute-start(bf16[32,64,256]{2,1,0:T(8,128)(2,1)S(1)} %collective-permute-done.36.rest_11_), channel_id=1, source_target_pairs={{0,8},{1,9},{2,10},{3,11},{4,12},{5,13},{6,14},{7,15},{8,0},{9,1},... | collective-permute-start | bytes 3145736 | tf_op jit(solution)/shard_map/ppermute | solution.py:29
  161.2 3.0 collective-permute-start.45
  165.1 4.6 %attend.5 = (bf16[4,192,256]{2,1,0:T(8,128)(2,1)S(1)}, bf16[192,2048]{1,0:T(8,128)(2,1)S(1)}) custom-call(s32[2]{0:T(128)S(1)} %pad_add_fusion.me_ref, f32[4,128]{1,0:T(4,128)S(1)} %slice.20.list_ref, s32[4]{0:T(128)S(1)} %broadcast_select_fusion.2.pos_ref, s32[3,4,4]{2,1,0:T(4,128)S(1)} %broadcast_select_fusion.1.mask_ref, ...), custom_call_target="tpu_custom_call" | custom-call | flops 1000000000 | tf_op jit(solution)/shard_map/attend/pallas_call | solution.py:252
  171.4 7.0 %collective-permute-done.38.rest_1_ = bf16[4,192,256]{2,1,0:T(8,128)(2,1)S(1)} collective-permute-done((bf16[4,192,256]{2,1,0:T(8,128)(2,1)S(1)}, bf16[4,192,256]{2,1,0:T(8,128)(2,1)S(1)}, u32[]{:S(2)}, u32[]{:S(2)}) %collective-permute-start.38) | collective-permute-done | bytes 393248 | tf_op jit(solution)/shard_map/ppermute | solution.py:29
  178.4 2.0 collective-permute-done.39.rest_2_
  182.9 3.8 %collective-permute-done.45.rest_7_ = bf16[32,64,256]{2,1,0:T(8,128)(2,1)S(1)} collective-permute-done((bf16[32,64,256]{2,1,0:T(8,128)(2,1)S(1)}, bf16[32,64,256]{2,1,0:T(8,128)(2,1)S(1)}, u32[]{:S(2)}, u32[]{:S(2)}) %collective-permute-start.45) | collective-permute-done | bytes 1048608 | tf_op jit(solution)/shard_map/ppermute | solution.py:29
  187.3 5.1 %collective-permute-start.49 = (bf16[32,64,256]{2,1,0:T(8,128)(2,1)S(1)}, bf16[32,64,256]{2,1,0:T(8,128)(2,1)S(1)}, u32[]{:S(2)}, u32[]{:S(2)}) collective-permute-start(bf16[32,64,256]{2,1,0:T(8,128)(2,1)S(1)} %pick.12.rest_5_), channel_id=1, source_target_pairs={{0,4},{1,5},{6,2},{7,3},{8,12},{9,13},{14,10},{15,11},{16,20},{17,... | collective-permute-start | bytes 3145736 | tf_op jit(solution)/shard_map/ppermute | solution.py:29
  192.4 2.2 project_out.5.rest_0_.rest_4_
  196.1 6.7 %collective-permute-done.41.rest_1_ = bf16[4,192,256]{2,1,0:T(8,128)(2,1)S(1)} collective-permute-done((bf16[4,192,256]{2,1,0:T(8,128)(2,1)S(1)}, bf16[4,192,256]{2,1,0:T(8,128)(2,1)S(1)}, u32[]{:S(2)}, u32[]{:S(2)}) %collective-permute-start.41) | collective-permute-done | bytes 393248 | tf_op jit(solution)/shard_map/ppermute | solution.py:29
  202.8 1.7 collective-permute-done.42.rest_2_
  205.8 1.7 collective-permute-start.44
  208.0 3.4 %collective-permute-done.43.rest_3_ = bf16[4,192,256]{2,1,0:T(8,128)(2,1)S(1)} collective-permute-done((bf16[4,192,256]{2,1,0:T(8,128)(2,1)S(1)}, bf16[4,192,256]{2,1,0:T(8,128)(2,1)S(1)}, u32[]{:S(2)}, u32[]{:S(2)}) %collective-permute-start.43) | collective-permute-done | bytes 393248 | tf_op jit(solution)/shard_map/ppermute | solution.py:29
  211.3 2.7 collective-permute-done.49.rest_11_
  214.0 1.7 collective-permute-start.50
  215.7 4.8 %collective-permute-start.58 = (bf16[32,64,256]{2,1,0:T(8,128)(2,1)S(1)}, bf16[32,64,256]{2,1,0:T(8,128)(2,1)S(1)}, u32[]{:S(2)}, u32[]{:S(2)}) collective-permute-start(bf16[32,64,256]{2,1,0:T(8,128)(2,1)S(1)} %pick.13.rest_5_), channel_id=1, source_target_pairs={{0,2},{1,3},{6,4},{7,5},{8,10},{9,11},{14,12},{15,13},{16,18},{17,... | collective-permute-start | bytes 3145736 | tf_op jit(solution)/shard_map/ppermute | solution.py:29
  220.5 1.7 collective-permute-start.60
  222.2 4.6 %attend.6 = (bf16[4,192,256]{2,1,0:T(8,128)(2,1)S(1)}, bf16[192,2048]{1,0:T(8,128)(2,1)S(1)}) custom-call(s32[2]{0:T(128)S(1)} %pad_add_fusion.me_ref, f32[4,128]{1,0:T(4,128)S(1)} %slice.20.list_ref, s32[4]{0:T(128)S(1)} %broadcast_select_fusion.2.pos_ref, s32[3,4,4]{2,1,0:T(4,128)S(1)} %broadcast_select_fusion.1.mask_ref, ...), custom_call_target="tpu_custom_call" | custom-call | flops 1000000000 | tf_op jit(solution)/shard_map/attend/pallas_call | solution.py:252
  228.4 7.0 %collective-permute-done.51.rest_1_ = bf16[4,192,256]{2,1,0:T(8,128)(2,1)S(1)} collective-permute-done((bf16[4,192,256]{2,1,0:T(8,128)(2,1)S(1)}, bf16[4,192,256]{2,1,0:T(8,128)(2,1)S(1)}, u32[]{:S(2)}, u32[]{:S(2)}) %collective-permute-start.51) | collective-permute-done | bytes 393248 | tf_op jit(solution)/shard_map/ppermute | solution.py:29
  235.5 2.0 collective-permute-done.52.rest_2_
  238.9 4.0 %collective-permute-done.58.rest_7_ = bf16[32,64,256]{2,1,0:T(8,128)(2,1)S(1)} collective-permute-done((bf16[32,64,256]{2,1,0:T(8,128)(2,1)S(1)}, bf16[32,64,256]{2,1,0:T(8,128)(2,1)S(1)}, u32[]{:S(2)}, u32[]{:S(2)}) %collective-permute-start.58) | collective-permute-done | bytes 1048608 | tf_op jit(solution)/shard_map/ppermute | solution.py:29
  244.4 5.3 %collective-permute-start.62 = (bf16[32,64,256]{2,1,0:T(8,128)(2,1)S(1)}, bf16[32,64,256]{2,1,0:T(8,128)(2,1)}, u32[]{:S(2)}, u32[]{:S(2)}) collective-permute-start(bf16[32,64,256]{2,1,0:T(8,128)(2,1)S(1)} %pick.13.rest_5_), channel_id=1, source_target_pairs={{0,4},{1,5},{6,2},{7,3},{8,12},{9,13},{14,10},{15,11},{16,20},{17,... | collective-permute-start | bytes 3145736 | tf_op jit(solution)/shard_map/ppermute | solution.py:29
  249.8 2.2 project_out.6.rest_0_.rest_4_
  253.4 6.7 %collective-permute-done.54.rest_1_ = bf16[4,192,256]{2,1,0:T(8,128)(2,1)S(1)} collective-permute-done((bf16[4,192,256]{2,1,0:T(8,128)(2,1)S(1)}, bf16[4,192,256]{2,1,0:T(8,128)(2,1)S(1)}, u32[]{:S(2)}, u32[]{:S(2)}) %collective-permute-start.54) | collective-permute-done | bytes 393248 | tf_op jit(solution)/shard_map/ppermute | solution.py:29
  260.1 1.7 collective-permute-done.55.rest_2_
  263.9 2.1 collective-permute-start.57
  266.5 3.0 collective-permute-done.56.rest_3_
  270.5 2.5 collective-permute-start.63
  277.6 6.1 %attend.7 = (bf16[4,192,256]{2,1,0:T(8,128)(2,1)S(1)}, bf16[192,2048]{1,0:T(8,128)(2,1)S(1)}) custom-call(s32[2]{0:T(128)S(1)} %pad_add_fusion.me_ref, f32[4,128]{1,0:T(4,128)S(1)} %slice.20.list_ref, s32[4]{0:T(128)S(1)} %broadcast_select_fusion.2.pos_ref, s32[3,4,4]{2,1,0:T(4,128)S(1)} %broadcast_select_fusion.1.mask_ref, ...), custom_call_target="tpu_custom_call" | custom-call | flops 1000000000 | tf_op jit(solution)/shard_map/attend/pallas_call | solution.py:252
  287.2 5.3 %collective-permute-done.66.rest_1_ = bf16[4,192,256]{2,1,0:T(8,128)(2,1)S(1)} collective-permute-done((bf16[4,192,256]{2,1,0:T(8,128)(2,1)S(1)}, bf16[4,192,256]{2,1,0:T(8,128)(2,1)S(1)}, u32[]{:S(2)}, u32[]{:S(2)}) %collective-permute-start.66) | collective-permute-done | bytes 393248 | tf_op jit(solution)/shard_map/ppermute | solution.py:29
  292.5 3.3 %collective-permute-done.67.rest_2_ = bf16[4,192,256]{2,1,0:T(8,128)(2,1)S(1)} collective-permute-done((bf16[4,192,256]{2,1,0:T(8,128)(2,1)S(1)}, bf16[4,192,256]{2,1,0:T(8,128)(2,1)S(1)}, u32[]{:S(2)}, u32[]{:S(2)}) %collective-permute-start.67) | collective-permute-done | bytes 393248 | tf_op jit(solution)/shard_map/ppermute | solution.py:29
  298.9 3.8 %collective-permute-done.68.rest_3_ = bf16[4,192,256]{2,1,0:T(8,128)(2,1)S(1)} collective-permute-done((bf16[4,192,256]{2,1,0:T(8,128)(2,1)S(1)}, bf16[4,192,256]{2,1,0:T(8,128)(2,1)S(1)}, u32[]{:S(2)}, u32[]{:S(2)}) %collective-permute-start.68) | collective-permute-done | bytes 393248 | tf_op jit(solution)/shard_map/ppermute | solution.py:29
  302.7 2.7 project_out.7
  308.0 6.8 %collective-permute-done.69 = bf16[4,192,256]{2,1,0:T(8,128)(2,1)S(1)} collective-permute-done((bf16[4,192,256]{2,1,0:T(8,128)(2,1)S(1)}, bf16[4,192,256]{2,1,0:T(8,128)(2,1)S(1)}, u32[]{:S(2)}, u32[]{:S(2)}) %collective-permute-start.69) | collective-permute-done | bytes 393248 | tf_op jit(solution)/shard_map/ppermute | solution.py:29
  (181 shorter events, 73.3 us)
Async XLA Ops:
  12.0 14.7 %collective-permute-start.7 = (bf16[16,64,256]{2,1,0:T(8,128)(2,1)S(1)}, bf16[16,64,256]{2,1,0:T(8,128)(2,1)}, u32[]{:S(2)}, u32[]{:S(2)}) collective-permute-start(bf16[16,64,256]{2,1,0:T(8,128)(2,1)S(1)} %get-tuple-element.51), channel_id=1, source_target_pairs={{0,1},{1,0},{2,3},{3,2},{4,5},{5,4},{6,7},{7,6},{8,9},{9,8},{10,11... | collective-permute-start | bytes 1572872 | tf_op jit(solution)/shard_map/ppermute | solution.py:29
  13.3 11.8 %collective-permute-start.5 = (bf16[4,192,256]{2,1,0:T(8,128)(2,1)}, bf16[4,192,256]{2,1,0:T(8,128)(2,1)}, u32[]{:S(2)}, u32[]{:S(2)}) collective-permute-start(bf16[4,192,256]{2,1,0:T(8,128)(2,1)} %get-tuple-element.50.rest_0_), channel_id=1, source_target_pairs={{8,10},{9,11},{14,12},{15,13},{24,26},{25,27},{30,28},{31,29}} | collective-permute-start | bytes 1179656 | tf_op jit(solution)/shard_map/ppermute | solution.py:29
  17.2 25.3 %collective-permute-start.6 = (bf16[28,64,256]{2,1,0:T(8,128)(2,1)}, bf16[28,64,256]{2,1,0:T(8,128)(2,1)S(1)}, u32[]{:S(2)}, u32[]{:S(2)}) collective-permute-start(bf16[28,64,256]{2,1,0:T(8,128)(2,1)} %get-tuple-element.64.rest_0_), channel_id=1, source_target_pairs={{0,16},{1,17},{2,18},{3,19},{4,20},{5,21},{6,22},{7,23},{24,8},{25... | collective-permute-start | bytes 2752520 | tf_op jit(solution)/shard_map/ppermute | solution.py:29
  19.4 24.1 %collective-permute-start.9 = (bf16[28,64,256]{2,1,0:T(8,128)(2,1)}, bf16[28,64,256]{2,1,0:T(8,128)(2,1)}, u32[]{:S(2)}, u32[]{:S(2)}) collective-permute-start(bf16[28,64,256]{2,1,0:T(8,128)(2,1)} %get-tuple-element.66.rest_0_), channel_id=1, source_target_pairs={{0,24},{1,25},{2,26},{3,27},{4,28},{5,29},{6,30},{7,31},{24,0},{25... | collective-permute-start | bytes 2752520 | tf_op jit(solution)/shard_map/ppermute | solution.py:29
  25.1 20.5 %collective-permute-start.14 = (bf16[28,64,256]{2,1,0:T(8,128)(2,1)}, bf16[28,64,256]{2,1,0:T(8,128)(2,1)S(1)}, u32[]{:S(2)}, u32[]{:S(2)}) collective-permute-start(bf16[28,64,256]{2,1,0:T(8,128)(2,1)} %get-tuple-element.57), channel_id=1, source_target_pairs={{0,8},{1,9},{2,10},{3,11},{4,12},{5,13},{6,14},{7,15},{8,0},{9,1},... | collective-permute-start | bytes 2752520 | tf_op jit(solution)/shard_map/ppermute | solution.py:29
  28.0 13.7 %collective-permute-start.10 = (bf16[4,64,256]{2,1,0:T(8,128)(2,1)S(1)}, bf16[4,64,256]{2,1,0:T(8,128)(2,1)S(1)}, u32[]{:S(2)}, u32[]{:S(2)}) collective-permute-start(bf16[4,64,256]{2,1,0:T(8,128)(2,1)S(1)} %get-tuple-element.54.rest_1_), channel_id=1, source_target_pairs={{0,24},{1,25},{2,26},{3,27},{4,28},{5,29},{6,30},{7,31},{24,0},{25... | collective-permute-start | bytes 393224 | tf_op jit(solution)/shard_map/ppermute | solution.py:29
  29.9 12.6 %collective-permute-start.8 = (bf16[4,64,256]{2,1,0:T(8,128)(2,1)S(1)}, bf16[4,64,256]{2,1,0:T(8,128)(2,1)S(1)}, u32[]{:S(2)}, u32[]{:S(2)}) collective-permute-start(bf16[4,64,256]{2,1,0:T(8,128)(2,1)S(1)} %get-tuple-element.52.rest_1_), channel_id=1, source_target_pairs={{0,16},{1,17},{2,18},{3,19},{4,20},{5,21},{6,22},{7,23},{24,8},{25... | collective-permute-start | bytes 393224 | tf_op jit(solution)/shard_map/ppermute | solution.py:29
  43.4 10.5 %collective-permute-start.11 = (bf16[4,192,256]{2,1,0:T(8,128)(2,1)S(1)}, bf16[4,192,256]{2,1,0:T(8,128)(2,1)S(1)}, u32[]{:S(2)}, u32[]{:S(2)}) collective-permute-start(bf16[4,192,256]{2,1,0:T(8,128)(2,1)S(1)} %pick.7.rest_0_.rest_4_), channel_id=1, source_target_pairs={{0,1},{1,0},{2,3},{3,2},{4,5},{5,4},{6,7},{7,6},{8,24},{9,25},{10,... | collective-permute-start | bytes 1179656 | tf_op jit(solution)/shard_map/ppermute | solution.py:29
  45.3 10.8 %collective-permute-start.12 = (bf16[4,192,256]{2,1,0:T(8,128)(2,1)S(1)}, bf16[4,192,256]{2,1,0:T(8,128)(2,1)S(1)}, u32[]{:S(2)}, u32[]{:S(2)}) collective-permute-start(bf16[4,192,256]{2,1,0:T(8,128)(2,1)S(1)} %pick.7.rest_0_.rest_4_), channel_id=1, source_target_pairs={{0,16},{1,17},{2,18},{3,19},{4,20},{5,21},{6,22},{7,23},{8,9},{9,8... | collective-permute-start | bytes 1179656 | tf_op jit(solution)/shard_map/ppermute | solution.py:29
  48.5 23.0 %collective-permute-start.17 = (bf16[32,64,256]{2,1,0:T(8,128)(2,1)S(1)}, bf16[32,64,256]{2,1,0:T(8,128)(2,1)}, u32[]{:S(2)}, u32[]{:S(2)}) collective-permute-start(bf16[32,64,256]{2,1,0:T(8,128)(2,1)S(1)} %pick.8.rest_5_), channel_id=1, source_target_pairs={{0,2},{1,3},{6,4},{7,5},{8,10},{9,11},{14,12},{15,13},{16,18},{17,... | collective-permute-start | bytes 3145736 | tf_op jit(solution)/shard_map/ppermute | solution.py:29
  50.8 20.7 %collective-permute-start.19 = (bf16[32,64,256]{2,1,0:T(8,128)(2,1)S(1)}, bf16[32,64,256]{2,1,0:T(8,128)(2,1)}, u32[]{:S(2)}, u32[]{:S(2)}) collective-permute-start(bf16[32,64,256]{2,1,0:T(8,128)(2,1)S(1)} %pick.8.rest_5_), channel_id=1, source_target_pairs={{2,4},{3,5},{4,2},{5,3},{10,12},{11,13},{12,10},{13,11},{18,20},{1... | collective-permute-start | bytes 3145736 | tf_op jit(solution)/shard_map/ppermute | solution.py:29
  58.9 6.6 %collective-permute-start.13 = (bf16[4,192,256]{2,1,0:T(8,128)(2,1)S(1)}, bf16[4,192,256]{2,1,0:T(8,128)(2,1)S(1)}, u32[]{:S(2)}, u32[]{:S(2)}) collective-permute-start(bf16[4,192,256]{2,1,0:T(8,128)(2,1)S(1)} %collective-permute-done.11.rest_1_), channel_id=1, source_target_pairs={{0,16},{1,17},{2,18},{3,19},{4,20},{5,21},{6,22},{7,23},{8,9},{9,8... | collective-permute-start | bytes 1179656 | tf_op jit(solution)/shard_map/ppermute | solution.py:29
  66.2 20.5 %collective-permute-start.30 = (bf16[32,64,256]{2,1,0:T(8,128)(2,1)S(1)}, bf16[32,64,256]{2,1,0:T(8,128)(2,1)S(1)}, u32[]{:S(2)}, u32[]{:S(2)}) collective-permute-start(bf16[32,64,256]{2,1,0:T(8,128)(2,1)S(1)} %pick.10), channel_id=1, source_target_pairs={{8,16},{9,17},{10,18},{11,19},{12,20},{13,21},{14,22},{15,23},{16,... | collective-permute-start | bytes 3145736 | tf_op jit(solution)/shard_map/ppermute | solution.py:29
  71.5 25.4 %collective-permute-start.21 = (bf16[32,64,256]{2,1,0:T(8,128)(2,1)S(1)}, bf16[32,64,256]{2,1,0:T(8,128)(2,1)}, u32[]{:S(2)}, u32[]{:S(2)}) collective-permute-start(bf16[32,64,256]{2,1,0:T(8,128)(2,1)S(1)} %pick.8.rest_5_), channel_id=1, source_target_pairs={{0,4},{1,5},{6,2},{7,3},{8,12},{9,13},{14,10},{15,11},{16,20},{17,... | collective-permute-start | bytes 3145736 | tf_op jit(solution)/shard_map/ppermute | solution.py:29
  80.4 19.7 %collective-permute-start.29 = (bf16[32,64,256]{2,1,0:T(8,128)(2,1)}, bf16[32,64,256]{2,1,0:T(8,128)(2,1)}, u32[]{:S(2)}, u32[]{:S(2)}) collective-permute-start(bf16[32,64,256]{2,1,0:T(8,128)(2,1)} %pick.9), channel_id=1, source_target_pairs={{8,24},{9,25},{10,26},{11,27},{12,28},{13,29},{14,30},{15,31},{16,... | collective-permute-start | bytes 3145736 | tf_op jit(solution)/shard_map/ppermute | solution.py:29
  81.7 25.6 %collective-permute-start.16 = (bf16[32,64,256]{2,1,0:T(8,128)(2,1)S(1)}, bf16[32,64,256]{2,1,0:T(8,128)(2,1)}, u32[]{:S(2)}, u32[]{:S(2)}) collective-permute-start(bf16[32,64,256]{2,1,0:T(8,128)(2,1)S(1)} %pick.8.rest_5_), channel_id=1, source_target_pairs={{0,8},{1,9},{2,10},{3,11},{4,12},{5,13},{6,14},{7,15},{8,0},{9,1},... | collective-permute-start | bytes 3145736 | tf_op jit(solution)/shard_map/ppermute | solution.py:29
  86.7 21.4 %collective-permute-start.18 = (bf16[32,64,256]{2,1,0:T(8,128)(2,1)}, bf16[32,64,256]{2,1,0:T(8,128)(2,1)}, u32[]{:S(2)}, u32[]{:S(2)}) collective-permute-start(bf16[32,64,256]{2,1,0:T(8,128)(2,1)} %collective-permute-done.17.rest_7_), channel_id=1, source_target_pairs={{0,8},{1,9},{2,10},{3,11},{4,12},{5,13},{6,14},{7,15},{8,0},{9,1},... | collective-permute-start | bytes 3145736 | tf_op jit(solution)/shard_map/ppermute | solution.py:29
  87.7 20.5 %collective-permute-start.20 = (bf16[32,64,256]{2,1,0:T(8,128)(2,1)}, bf16[32,64,256]{2,1,0:T(8,128)(2,1)}, u32[]{:S(2)}, u32[]{:S(2)}) collective-permute-start(bf16[32,64,256]{2,1,0:T(8,128)(2,1)} %collective-permute-done.19.rest_9_), channel_id=1, source_target_pairs={{0,8},{1,9},{2,10},{3,11},{4,12},{5,13},{6,14},{7,15},{8,0},{9,1},... | collective-permute-start | bytes 3145736 | tf_op jit(solution)/shard_map/ppermute | solution.py:29
  96.9 11.2 %collective-permute-start.22 = (bf16[32,64,256]{2,1,0:T(8,128)(2,1)}, bf16[32,64,256]{2,1,0:T(8,128)(2,1)}, u32[]{:S(2)}, u32[]{:S(2)}) collective-permute-start(bf16[32,64,256]{2,1,0:T(8,128)(2,1)} %collective-permute-done.21.rest_11_), channel_id=1, source_target_pairs={{0,8},{1,9},{2,10},{3,11},{4,12},{5,13},{6,14},{7,15},{8,0},{9,1},... | collective-permute-start | bytes 3145736 | tf_op jit(solution)/shard_map/ppermute | solution.py:29
  103.2 26.4 %collective-permute-start.32 = (bf16[32,64,256]{2,1,0:T(8,128)(2,1)S(1)}, bf16[32,64,256]{2,1,0:T(8,128)(2,1)S(1)}, u32[]{:S(2)}, u32[]{:S(2)}) collective-permute-start(bf16[32,64,256]{2,1,0:T(8,128)(2,1)S(1)} %pick.11.rest_5_), channel_id=1, source_target_pairs={{0,2},{1,3},{6,4},{7,5},{8,10},{9,11},{14,12},{15,13},{16,18},{17,... | collective-permute-start | bytes 3145736 | tf_op jit(solution)/shard_map/ppermute | solution.py:29
  107.4 22.2 %collective-permute-start.34 = (bf16[32,64,256]{2,1,0:T(8,128)(2,1)S(1)}, bf16[32,64,256]{2,1,0:T(8,128)(2,1)S(1)}, u32[]{:S(2)}, u32[]{:S(2)}) collective-permute-start(bf16[32,64,256]{2,1,0:T(8,128)(2,1)S(1)} %pick.11.rest_5_), channel_id=1, source_target_pairs={{2,4},{3,5},{4,2},{5,3},{10,12},{11,13},{12,10},{13,11},{18,20},{1... | collective-permute-start | bytes 3145736 | tf_op jit(solution)/shard_map/ppermute | solution.py:29
  114.3 10.1 %collective-permute-start.23 = (bf16[4,192,256]{2,1,0:T(8,128)(2,1)S(1)}, bf16[4,192,256]{2,1,0:T(8,128)(2,1)S(1)}, u32[]{:S(2)}, u32[]{:S(2)}) collective-permute-start(bf16[4,192,256]{2,1,0:T(8,128)(2,1)S(1)} %attend.4.rest_0_), channel_id=1, source_target_pairs={{0,1},{1,0},{2,3},{3,2},{4,5},{5,4},{6,7},{7,6},{8,24},{9,25},{10,... | collective-permute-start | bytes 1179656 | tf_op jit(solution)/shard_map/ppermute | solution.py:29
  114.4 10.7 %collective-permute-start.24 = (bf16[4,192,256]{2,1,0:T(8,128)(2,1)S(1)}, bf16[4,192,256]{2,1,0:T(8,128)(2,1)S(1)}, u32[]{:S(2)}, u32[]{:S(2)}) collective-permute-start(bf16[4,192,256]{2,1,0:T(8,128)(2,1)S(1)} %attend.4.rest_0_), channel_id=1, source_target_pairs={{0,16},{1,17},{2,18},{3,19},{4,20},{5,21},{6,22},{7,23},{8,9},{9,8... | collective-permute-start | bytes 1179656 | tf_op jit(solution)/shard_map/ppermute | solution.py:29
  125.1 6.9 %collective-permute-start.25 = (bf16[4,192,256]{2,1,0:T(8,128)(2,1)S(1)}, bf16[4,192,256]{2,1,0:T(8,128)(2,1)S(1)}, u32[]{:S(2)}, u32[]{:S(2)}) collective-permute-start(bf16[4,192,256]{2,1,0:T(8,128)(2,1)S(1)} %collective-permute-done.23.rest_1_), channel_id=1, source_target_pairs={{0,16},{1,17},{2,18},{3,19},{4,20},{5,21},{6,22},{7,23},{8,9},{9,8... | collective-permute-start | bytes 1179656 | tf_op jit(solution)/shard_map/ppermute | solution.py:29
  132.0 25.2 %collective-permute-start.36 = (bf16[32,64,256]{2,1,0:T(8,128)(2,1)S(1)}, bf16[32,64,256]{2,1,0:T(8,128)(2,1)S(1)}, u32[]{:S(2)}, u32[]{:S(2)}) collective-permute-start(bf16[32,64,256]{2,1,0:T(8,128)(2,1)S(1)} %pick.11.rest_5_), channel_id=1, source_target_pairs={{0,4},{1,5},{6,2},{7,3},{8,12},{9,13},{14,10},{15,11},{16,20},{17,... | collective-permute-start | bytes 3145736 | tf_op jit(solution)/shard_map/ppermute | solution.py:29
  141.3 7.0 %collective-permute-start.26 = (bf16[4,192,256]{2,1,0:T(8,128)(2,1)S(1)}, bf16[4,192,256]{2,1,0:T(8,128)(2,1)S(1)}, u32[]{:S(2)}, u32[]{:S(2)}) collective-permute-start(bf16[4,192,256]{2,1,0:T(8,128)(2,1)S(1)} %project_out.4.rest_0_.rest_4_), channel_id=1, source_target_pairs={{0,1},{1,0},{2,3},{3,2},{4,5},{5,4},{6,7},{7,6},{8,24},{9,25},{10,... | collective-permute-start | bytes 1179656 | tf_op jit(solution)/shard_map/ppermute | solution.py:29
  141.4 8.1 %collective-permute-start.27 = (bf16[4,192,256]{2,1,0:T(8,128)(2,1)S(1)}, bf16[4,192,256]{2,1,0:T(8,128)(2,1)S(1)}, u32[]{:S(2)}, u32[]{:S(2)}) collective-permute-start(bf16[4,192,256]{2,1,0:T(8,128)(2,1)S(1)} %project_out.4.rest_0_.rest_4_), channel_id=1, source_target_pairs={{0,16},{1,17},{2,18},{3,19},{4,20},{5,21},{6,22},{7,23},{8,9},{9,8... | collective-permute-start | bytes 1179656 | tf_op jit(solution)/shard_map/ppermute | solution.py:29
  149.5 7.3 %collective-permute-start.28 = (bf16[4,192,256]{2,1,0:T(8,128)(2,1)S(1)}, bf16[4,192,256]{2,1,0:T(8,128)(2,1)S(1)}, u32[]{:S(2)}, u32[]{:S(2)}) collective-permute-start(bf16[4,192,256]{2,1,0:T(8,128)(2,1)S(1)} %collective-permute-done.26.rest_1_), channel_id=1, source_target_pairs={{0,16},{1,17},{2,18},{3,19},{4,20},{5,21},{6,22},{7,23},{8,9},{9,8... | collective-permute-start | bytes 1179656 | tf_op jit(solution)/shard_map/ppermute | solution.py:29
  150.7 13.4 %collective-permute-start.31 = (bf16[32,64,256]{2,1,0:T(8,128)(2,1)S(1)}, bf16[32,64,256]{2,1,0:T(8,128)(2,1)S(1)}, u32[]{:S(2)}, u32[]{:S(2)}) collective-permute-start(bf16[32,64,256]{2,1,0:T(8,128)(2,1)S(1)} %pick.11.rest_5_), channel_id=1, source_target_pairs={{0,8},{1,9},{2,10},{3,11},{4,12},{5,13},{6,14},{7,15},{8,0},{9,1},... | collective-permute-start | bytes 3145736 | tf_op jit(solution)/shard_map/ppermute | solution.py:29
  154.7 10.4 %collective-permute-start.33 = (bf16[32,64,256]{2,1,0:T(8,128)(2,1)S(1)}, bf16[32,64,256]{2,1,0:T(8,128)(2,1)S(1)}, u32[]{:S(2)}, u32[]{:S(2)}) collective-permute-start(bf16[32,64,256]{2,1,0:T(8,128)(2,1)S(1)} %collective-permute-done.32.rest_7_), channel_id=1, source_target_pairs={{0,8},{1,9},{2,10},{3,11},{4,12},{5,13},{6,14},{7,15},{8,0},{9,1},... | collective-permute-start | bytes 3145736 | tf_op jit(solution)/shard_map/ppermute | solution.py:29
  154.7 10.4 %collective-permute-start.35 = (bf16[32,64,256]{2,1,0:T(8,128)(2,1)S(1)}, bf16[32,64,256]{2,1,0:T(8,128)(2,1)S(1)}, u32[]{:S(2)}, u32[]{:S(2)}) collective-permute-start(bf16[32,64,256]{2,1,0:T(8,128)(2,1)S(1)} %collective-permute-done.34.rest_9_), channel_id=1, source_target_pairs={{0,8},{1,9},{2,10},{3,11},{4,12},{5,13},{6,14},{7,15},{8,0},{9,1},... | collective-permute-start | bytes 3145736 | tf_op jit(solution)/shard_map/ppermute | solution.py:29
  157.2 7.9 %collective-permute-start.37 = (bf16[32,64,256]{2,1,0:T(8,128)(2,1)S(1)}, bf16[32,64,256]{2,1,0:T(8,128)(2,1)S(1)}, u32[]{:S(2)}, u32[]{:S(2)}) collective-permute-start(bf16[32,64,256]{2,1,0:T(8,128)(2,1)S(1)} %collective-permute-done.36.rest_11_), channel_id=1, source_target_pairs={{0,8},{1,9},{2,10},{3,11},{4,12},{5,13},{6,14},{7,15},{8,0},{9,1},... | collective-permute-start | bytes 3145736 | tf_op jit(solution)/shard_map/ppermute | solution.py:29
  161.2 25.5 %collective-permute-start.45 = (bf16[32,64,256]{2,1,0:T(8,128)(2,1)S(1)}, bf16[32,64,256]{2,1,0:T(8,128)(2,1)S(1)}, u32[]{:S(2)}, u32[]{:S(2)}) collective-permute-start(bf16[32,64,256]{2,1,0:T(8,128)(2,1)S(1)} %pick.12.rest_5_), channel_id=1, source_target_pairs={{0,2},{1,3},{6,4},{7,5},{8,10},{9,11},{14,12},{15,13},{16,18},{17,... | collective-permute-start | bytes 3145736 | tf_op jit(solution)/shard_map/ppermute | solution.py:29
  164.2 22.5 %collective-permute-start.47 = (bf16[32,64,256]{2,1,0:T(8,128)(2,1)S(1)}, bf16[32,64,256]{2,1,0:T(8,128)(2,1)S(1)}, u32[]{:S(2)}, u32[]{:S(2)}) collective-permute-start(bf16[32,64,256]{2,1,0:T(8,128)(2,1)S(1)} %pick.12.rest_5_), channel_id=1, source_target_pairs={{2,4},{3,5},{4,2},{5,3},{10,12},{11,13},{12,10},{13,11},{18,20},{1... | collective-permute-start | bytes 3145736 | tf_op jit(solution)/shard_map/ppermute | solution.py:29
  169.8 8.6 %collective-permute-start.38 = (bf16[4,192,256]{2,1,0:T(8,128)(2,1)S(1)}, bf16[4,192,256]{2,1,0:T(8,128)(2,1)S(1)}, u32[]{:S(2)}, u32[]{:S(2)}) collective-permute-start(bf16[4,192,256]{2,1,0:T(8,128)(2,1)S(1)} %get-tuple-element.71.rest_0_), channel_id=1, source_target_pairs={{0,1},{1,0},{2,3},{3,2},{4,5},{5,4},{6,7},{7,6},{8,24},{9,25},{10,... | collective-permute-start | bytes 1179656 | tf_op jit(solution)/shard_map/ppermute | solution.py:29
  169.8 10.6 %collective-permute-start.39 = (bf16[4,192,256]{2,1,0:T(8,128)(2,1)S(1)}, bf16[4,192,256]{2,1,0:T(8,128)(2,1)S(1)}, u32[]{:S(2)}, u32[]{:S(2)}) collective-permute-start(bf16[4,192,256]{2,1,0:T(8,128)(2,1)S(1)} %get-tuple-element.71.rest_0_), channel_id=1, source_target_pairs={{0,16},{1,17},{2,18},{3,19},{4,20},{5,21},{6,22},{7,23},{8,9},{9,8... | collective-permute-start | bytes 1179656 | tf_op jit(solution)/shard_map/ppermute | solution.py:29
  180.4 6.9 %collective-permute-start.40 = (bf16[4,192,256]{2,1,0:T(8,128)(2,1)S(1)}, bf16[4,192,256]{2,1,0:T(8,128)(2,1)S(1)}, u32[]{:S(2)}, u32[]{:S(2)}) collective-permute-start(bf16[4,192,256]{2,1,0:T(8,128)(2,1)S(1)} %collective-permute-done.38.rest_1_), channel_id=1, source_target_pairs={{0,16},{1,17},{2,18},{3,19},{4,20},{5,21},{6,22},{7,23},{8,9},{9,8... | collective-permute-start | bytes 1179656 | tf_op jit(solution)/shard_map/ppermute | solution.py:29
  187.3 26.7 %collective-permute-start.49 = (bf16[32,64,256]{2,1,0:T(8,128)(2,1)S(1)}, bf16[32,64,256]{2,1,0:T(8,128)(2,1)S(1)}, u32[]{:S(2)}, u32[]{:S(2)}) collective-permute-start(bf16[32,64,256]{2,1,0:T(8,128)(2,1)S(1)} %pick.12.rest_5_), channel_id=1, source_target_pairs={{0,4},{1,5},{6,2},{7,3},{8,12},{9,13},{14,10},{15,11},{16,20},{17,... | collective-permute-start | bytes 3145736 | tf_op jit(solution)/shard_map/ppermute | solution.py:29
  194.7 8.1 %collective-permute-start.41 = (bf16[4,192,256]{2,1,0:T(8,128)(2,1)S(1)}, bf16[4,192,256]{2,1,0:T(8,128)(2,1)S(1)}, u32[]{:S(2)}, u32[]{:S(2)}) collective-permute-start(bf16[4,192,256]{2,1,0:T(8,128)(2,1)S(1)} %project_out.5.rest_0_.rest_4_), channel_id=1, source_target_pairs={{0,1},{1,0},{2,3},{3,2},{4,5},{5,4},{6,7},{7,6},{8,24},{9,25},{10,... | collective-permute-start | bytes 1179656 | tf_op jit(solution)/shard_map/ppermute | solution.py:29
  194.7 9.7 %collective-permute-start.42 = (bf16[4,192,256]{2,1,0:T(8,128)(2,1)S(1)}, bf16[4,192,256]{2,1,0:T(8,128)(2,1)S(1)}, u32[]{:S(2)}, u32[]{:S(2)}) collective-permute-start(bf16[4,192,256]{2,1,0:T(8,128)(2,1)S(1)} %project_out.5.rest_0_.rest_4_), channel_id=1, source_target_pairs={{0,16},{1,17},{2,18},{3,19},{4,20},{5,21},{6,22},{7,23},{8,9},{9,8... | collective-permute-start | bytes 1179656 | tf_op jit(solution)/shard_map/ppermute | solution.py:29
  204.4 6.9 %collective-permute-start.43 = (bf16[4,192,256]{2,1,0:T(8,128)(2,1)S(1)}, bf16[4,192,256]{2,1,0:T(8,128)(2,1)S(1)}, u32[]{:S(2)}, u32[]{:S(2)}) collective-permute-start(bf16[4,192,256]{2,1,0:T(8,128)(2,1)S(1)} %collective-permute-done.41.rest_1_), channel_id=1, source_target_pairs={{0,16},{1,17},{2,18},{3,19},{4,20},{5,21},{6,22},{7,23},{8,9},{9,8... | collective-permute-start | bytes 1179656 | tf_op jit(solution)/shard_map/ppermute | solution.py:29
  205.8 14.7 %collective-permute-start.44 = (bf16[32,64,256]{2,1,0:T(8,128)(2,1)S(1)}, bf16[32,64,256]{2,1,0:T(8,128)(2,1)S(1)}, u32[]{:S(2)}, u32[]{:S(2)}) collective-permute-start(bf16[32,64,256]{2,1,0:T(8,128)(2,1)S(1)} %pick.12.rest_5_), channel_id=1, source_target_pairs={{0,8},{1,9},{2,10},{3,11},{4,12},{5,13},{6,14},{7,15},{8,0},{9,1},... | collective-permute-start | bytes 3145736 | tf_op jit(solution)/shard_map/ppermute | solution.py:29
  207.5 14.7 %collective-permute-start.46 = (bf16[32,64,256]{2,1,0:T(8,128)(2,1)S(1)}, bf16[32,64,256]{2,1,0:T(8,128)(2,1)S(1)}, u32[]{:S(2)}, u32[]{:S(2)}) collective-permute-start(bf16[32,64,256]{2,1,0:T(8,128)(2,1)S(1)} %collective-permute-done.45.rest_7_), channel_id=1, source_target_pairs={{0,8},{1,9},{2,10},{3,11},{4,12},{5,13},{6,14},{7,15},{8,0},{9,1},... | collective-permute-start | bytes 3145736 | tf_op jit(solution)/shard_map/ppermute | solution.py:29
  207.5 14.7 %collective-permute-start.48 = (bf16[32,64,256]{2,1,0:T(8,128)(2,1)S(1)}, bf16[32,64,256]{2,1,0:T(8,128)(2,1)S(1)}, u32[]{:S(2)}, u32[]{:S(2)}) collective-permute-start(bf16[32,64,256]{2,1,0:T(8,128)(2,1)S(1)} %collective-permute-done.47.rest_9_), channel_id=1, source_target_pairs={{0,8},{1,9},{2,10},{3,11},{4,12},{5,13},{6,14},{7,15},{8,0},{9,1},... | collective-permute-start | bytes 3145736 | tf_op jit(solution)/shard_map/ppermute | solution.py:29
  214.0 8.2 %collective-permute-start.50 = (bf16[32,64,256]{2,1,0:T(8,128)(2,1)S(1)}, bf16[32,64,256]{2,1,0:T(8,128)(2,1)S(1)}, u32[]{:S(2)}, u32[]{:S(2)}) collective-permute-start(bf16[32,64,256]{2,1,0:T(8,128)(2,1)S(1)} %collective-permute-done.49.rest_11_), channel_id=1, source_target_pairs={{0,8},{1,9},{2,10},{3,11},{4,12},{5,13},{6,14},{7,15},{8,0},{9,1},... | collective-permute-start | bytes 3145736 | tf_op jit(solution)/shard_map/ppermute | solution.py:29
  215.7 27.3 %collective-permute-start.58 = (bf16[32,64,256]{2,1,0:T(8,128)(2,1)S(1)}, bf16[32,64,256]{2,1,0:T(8,128)(2,1)S(1)}, u32[]{:S(2)}, u32[]{:S(2)}) collective-permute-start(bf16[32,64,256]{2,1,0:T(8,128)(2,1)S(1)} %pick.13.rest_5_), channel_id=1, source_target_pairs={{0,2},{1,3},{6,4},{7,5},{8,10},{9,11},{14,12},{15,13},{16,18},{17,... | collective-permute-start | bytes 3145736 | tf_op jit(solution)/shard_map/ppermute | solution.py:29
  220.5 22.5 %collective-permute-start.60 = (bf16[32,64,256]{2,1,0:T(8,128)(2,1)S(1)}, bf16[32,64,256]{2,1,0:T(8,128)(2,1)}, u32[]{:S(2)}, u32[]{:S(2)}) collective-permute-start(bf16[32,64,256]{2,1,0:T(8,128)(2,1)S(1)} %pick.13.rest_5_), channel_id=1, source_target_pairs={{2,4},{3,5},{4,2},{5,3},{10,12},{11,13},{12,10},{13,11},{18,20},{1... | collective-permute-start | bytes 3145736 | tf_op jit(solution)/shard_map/ppermute | solution.py:29
  226.8 8.6 %collective-permute-start.51 = (bf16[4,192,256]{2,1,0:T(8,128)(2,1)S(1)}, bf16[4,192,256]{2,1,0:T(8,128)(2,1)S(1)}, u32[]{:S(2)}, u32[]{:S(2)}) collective-permute-start(bf16[4,192,256]{2,1,0:T(8,128)(2,1)S(1)} %get-tuple-element.77.rest_0_), channel_id=1, source_target_pairs={{0,1},{1,0},{2,3},{3,2},{4,5},{5,4},{6,7},{7,6},{8,24},{9,25},{10,... | collective-permute-start | bytes 1179656 | tf_op jit(solution)/shard_map/ppermute | solution.py:29
  226.9 10.6 %collective-permute-start.52 = (bf16[4,192,256]{2,1,0:T(8,128)(2,1)S(1)}, bf16[4,192,256]{2,1,0:T(8,128)(2,1)S(1)}, u32[]{:S(2)}, u32[]{:S(2)}) collective-permute-start(bf16[4,192,256]{2,1,0:T(8,128)(2,1)S(1)} %get-tuple-element.77.rest_0_), channel_id=1, source_target_pairs={{0,16},{1,17},{2,18},{3,19},{4,20},{5,21},{6,22},{7,23},{8,9},{9,8... | collective-permute-start | bytes 1179656 | tf_op jit(solution)/shard_map/ppermute | solution.py:29
  237.5 6.9 %collective-permute-start.53 = (bf16[4,192,256]{2,1,0:T(8,128)(2,1)S(1)}, bf16[4,192,256]{2,1,0:T(8,128)(2,1)S(1)}, u32[]{:S(2)}, u32[]{:S(2)}) collective-permute-start(bf16[4,192,256]{2,1,0:T(8,128)(2,1)S(1)} %collective-permute-done.51.rest_1_), channel_id=1, source_target_pairs={{0,16},{1,17},{2,18},{3,19},{4,20},{5,21},{6,22},{7,23},{8,9},{9,8... | collective-permute-start | bytes 1179656 | tf_op jit(solution)/shard_map/ppermute | solution.py:29
  244.4 26.1 %collective-permute-start.62 = (bf16[32,64,256]{2,1,0:T(8,128)(2,1)S(1)}, bf16[32,64,256]{2,1,0:T(8,128)(2,1)}, u32[]{:S(2)}, u32[]{:S(2)}) collective-permute-start(bf16[32,64,256]{2,1,0:T(8,128)(2,1)S(1)} %pick.13.rest_5_), channel_id=1, source_target_pairs={{0,4},{1,5},{6,2},{7,3},{8,12},{9,13},{14,10},{15,11},{16,20},{17,... | collective-permute-start | bytes 3145736 | tf_op jit(solution)/shard_map/ppermute | solution.py:29
  252.0 8.1 %collective-permute-start.54 = (bf16[4,192,256]{2,1,0:T(8,128)(2,1)S(1)}, bf16[4,192,256]{2,1,0:T(8,128)(2,1)S(1)}, u32[]{:S(2)}, u32[]{:S(2)}) collective-permute-start(bf16[4,192,256]{2,1,0:T(8,128)(2,1)S(1)} %project_out.6.rest_0_.rest_4_), channel_id=1, source_target_pairs={{0,1},{1,0},{2,3},{3,2},{4,5},{5,4},{6,7},{7,6},{8,24},{9,25},{10,... | collective-permute-start | bytes 1179656 | tf_op jit(solution)/shard_map/ppermute | solution.py:29
  252.1 9.7 %collective-permute-start.55 = (bf16[4,192,256]{2,1,0:T(8,128)(2,1)S(1)}, bf16[4,192,256]{2,1,0:T(8,128)(2,1)S(1)}, u32[]{:S(2)}, u32[]{:S(2)}) collective-permute-start(bf16[4,192,256]{2,1,0:T(8,128)(2,1)S(1)} %project_out.6.rest_0_.rest_4_), channel_id=1, source_target_pairs={{0,16},{1,17},{2,18},{3,19},{4,20},{5,21},{6,22},{7,23},{8,9},{9,8... | collective-permute-start | bytes 1179656 | tf_op jit(solution)/shard_map/ppermute | solution.py:29
  262.6 6.9 %collective-permute-start.56 = (bf16[4,192,256]{2,1,0:T(8,128)(2,1)S(1)}, bf16[4,192,256]{2,1,0:T(8,128)(2,1)S(1)}, u32[]{:S(2)}, u32[]{:S(2)}) collective-permute-start(bf16[4,192,256]{2,1,0:T(8,128)(2,1)S(1)} %collective-permute-done.54.rest_1_), channel_id=1, source_target_pairs={{0,16},{1,17},{2,18},{3,19},{4,20},{5,21},{6,22},{7,23},{8,9},{9,8... | collective-permute-start | bytes 1179656 | tf_op jit(solution)/shard_map/ppermute | solution.py:29
  263.9 10.8 %collective-permute-start.57 = (bf16[32,64,256]{2,1,0:T(8,128)(2,1)S(1)}, bf16[32,64,256]{2,1,0:T(8,128)(2,1)}, u32[]{:S(2)}, u32[]{:S(2)}) collective-permute-start(bf16[32,64,256]{2,1,0:T(8,128)(2,1)S(1)} %pick.13.rest_5_), channel_id=1, source_target_pairs={{0,8},{1,9},{2,10},{3,11},{4,12},{5,13},{6,14},{7,15},{8,0},{9,1},... | collective-permute-start | bytes 3145736 | tf_op jit(solution)/shard_map/ppermute | solution.py:29
  266.0 8.7 %collective-permute-start.59 = (bf16[32,64,256]{2,1,0:T(8,128)(2,1)S(1)}, bf16[32,64,256]{2,1,0:T(8,128)(2,1)}, u32[]{:S(2)}, u32[]{:S(2)}) collective-permute-start(bf16[32,64,256]{2,1,0:T(8,128)(2,1)S(1)} %collective-permute-done.58.rest_7_), channel_id=1, source_target_pairs={{0,8},{1,9},{2,10},{3,11},{4,12},{5,13},{6,14},{7,15},{8,0},{9,1},... | collective-permute-start | bytes 3145736 | tf_op jit(solution)/shard_map/ppermute | solution.py:29
  266.0 8.7 %collective-permute-start.61 = (bf16[32,64,256]{2,1,0:T(8,128)(2,1)}, bf16[32,64,256]{2,1,0:T(8,128)(2,1)}, u32[]{:S(2)}, u32[]{:S(2)}) collective-permute-start(bf16[32,64,256]{2,1,0:T(8,128)(2,1)} %collective-permute-done.60.rest_9_), channel_id=1, source_target_pairs={{0,8},{1,9},{2,10},{3,11},{4,12},{5,13},{6,14},{7,15},{8,0},{9,1},... | collective-permute-start | bytes 3145736 | tf_op jit(solution)/shard_map/ppermute | solution.py:29
  273.0 24.0 %collective-permute-start.65 = (bf16[192,2048]{1,0:T(8,128)(2,1)}, bf16[192,2048]{1,0:T(8,128)(2,1)S(1)}, u32[]{:S(2)}, u32[]{:S(2)}) collective-permute-start(bf16[192,2048]{1,0:T(8,128)(2,1)} %copy-done.24), channel_id=1, source_target_pairs={{2,10},{3,11},{4,12},{5,13},{10,8},{11,9},{12,14},{13,15},{18,26},... | collective-permute-start | bytes 2359304 | tf_op jit(solution)/shard_map/ppermute | solution.py:29
  283.8 8.7 %collective-permute-start.66 = (bf16[4,192,256]{2,1,0:T(8,128)(2,1)S(1)}, bf16[4,192,256]{2,1,0:T(8,128)(2,1)S(1)}, u32[]{:S(2)}, u32[]{:S(2)}) collective-permute-start(bf16[4,192,256]{2,1,0:T(8,128)(2,1)S(1)} %get-tuple-element.87.rest_0_), channel_id=1, source_target_pairs={{0,1},{1,0},{2,3},{3,2},{4,5},{5,4},{6,7},{7,6},{8,24},{9,25},{10,... | collective-permute-start | bytes 1179656 | tf_op jit(solution)/shard_map/ppermute | solution.py:29
  285.1 10.7 %collective-permute-start.67 = (bf16[4,192,256]{2,1,0:T(8,128)(2,1)S(1)}, bf16[4,192,256]{2,1,0:T(8,128)(2,1)S(1)}, u32[]{:S(2)}, u32[]{:S(2)}) collective-permute-start(bf16[4,192,256]{2,1,0:T(8,128)(2,1)S(1)} %get-tuple-element.87.rest_0_), channel_id=1, source_target_pairs={{0,16},{1,17},{2,18},{3,19},{4,20},{5,21},{6,22},{7,23},{8,9},{9,8... | collective-permute-start | bytes 1179656 | tf_op jit(solution)/shard_map/ppermute | solution.py:29
  286.5 10.6 %collective-permute-start.64 = (bf16[192,2048]{1,0:T(8,128)(2,1)S(1)}, bf16[192,2048]{1,0:T(8,128)(2,1)S(1)}, u32[]{:S(2)}, u32[]{:S(2)}) collective-permute-start(bf16[192,2048]{1,0:T(8,128)(2,1)S(1)} %broadcast_select_fusion), channel_id=1, source_target_pairs={{2,2},{3,3},{4,4},{5,5},{10,0},{11,1},{12,6},{13,7},{18,18},{19,19... | collective-permute-start | bytes 2359304 | tf_op jit(solution)/shard_map/ppermute | solution.py:29
  295.8 6.9 %collective-permute-start.68 = (bf16[4,192,256]{2,1,0:T(8,128)(2,1)S(1)}, bf16[4,192,256]{2,1,0:T(8,128)(2,1)S(1)}, u32[]{:S(2)}, u32[]{:S(2)}) collective-permute-start(bf16[4,192,256]{2,1,0:T(8,128)(2,1)S(1)} %collective-permute-done.66.rest_1_), channel_id=1, source_target_pairs={{0,16},{1,17},{2,18},{3,19},{4,20},{5,21},{6,22},{7,23},{8,9},{9,8... | collective-permute-start | bytes 1179656 | tf_op jit(solution)/shard_map/ppermute | solution.py:29
  305.4 9.4 %collective-permute-start.69 = (bf16[4,192,256]{2,1,0:T(8,128)(2,1)S(1)}, bf16[4,192,256]{2,1,0:T(8,128)(2,1)S(1)}, u32[]{:S(2)}, u32[]{:S(2)}) collective-permute-start(bf16[4,192,256]{2,1,0:T(8,128)(2,1)S(1)} %project_out.7), channel_id=1, source_target_pairs={{2,26},{3,27},{4,28},{5,29},{10,24},{11,25},{12,30},{13,31}} | collective-permute-start | bytes 1179656 | tf_op jit(solution)/shard_map/ppermute | solution.py:29
  306.7 8.5 %collective-permute-start.70 = (bf16[4,192,256]{2,1,0:T(8,128)(2,1)S(1)}, bf16[4,192,256]{2,1,0:T(8,128)(2,1)S(1)}, u32[]{:S(2)}, u32[]{:S(2)}) collective-permute-start(bf16[4,192,256]{2,1,0:T(8,128)(2,1)S(1)} %project_out.7), channel_id=1, source_target_pairs={{18,26},{19,27},{20,28},{21,29},{26,24},{27,25},{28,30},{29,31}} | collective-permute-start | bytes 1179656 | tf_op jit(solution)/shard_map/ppermute | solution.py:29
  (44 other events, 275.8 us)

commit v3 on v2

--- a/solution.py
+++ b/solution.py
@@ -13,7 +13,7 @@
 PROJECT_US = 1
 AXES = ("pipe", "fsdp", "tensor")
 VMEM_LIMIT = 32 * 1024 * 1024
-CUT_VMEM = 48 * 1024 * 1024
+CUT_VMEM = 56 * 1024 * 1024
 PICK_VMEM = 12 * 1024 * 1024
 
 
@@ -476,14 +476,15 @@
             results = [deliver(core) for core in range(2)]
         pieces = share(heads)
         if s + 1 < sections:
-            tie = pieces[1:]
+            tie = pieces[1:3] if s == 0 else pieces[1:]
             if s + 2 < sections:
                 coming = piece_of(s + 2, round_b if s == 0 else round_a)
                 tie = [*tie, coming]
             leg = second_leg(leg, *tie)
             most = with_core(leg[:-1])
         if s == sections - 1:
-            pieces[0] = after(pieces[0], *results)
+            result = jnp.where((p & 1) == 1, results[1], results[0])
+            pieces[0] = after(pieces[0], result)
         u = project_out(s, me, lists, lists_x, 3 * per * cols_half, pos, pieces, u, in_count, out_count, weights)
 
     final = u
@@ -504,7 +505,6 @@
     blocks = jnp.stack(halves).reshape(2, 2, cols, rows, width)
     blocks = jnp.where(made_by == 1, blocks[:, ::-1], blocks)
     last = jnp.transpose(blocks, (3, 0, 1, 2, 4)).reshape(rows, -1)
-    result = jnp.where((p & 1) == 1, results[1], results[0])
     return jnp.where(p == sections - 1, last, result)[None]
 
 

time: 320 us -> 319 us (level)
  waiting for transfers between devices: 129 us -> 141 us
  starting transfers between devices: 118 us -> 107 us
  Pallas kernels: 51.6 us -> 46.9 us
    ppermute x71, waiting for transfers between devices: 129 us -> 141 us  [hop(): return lax.ppermute(value, AXES, pairs)]
    ppermute x71, starting transfers between devices: 118 us -> 107 us  [hop(): return lax.ppermute(value, AXES, pairs)]
    unnamed x74 -> x86, local copies, waits for them, and re-layouts: 15.1 us -> 16.5 us
  transfers between devices with their start and end apart: 71 -> 71, of which waited for: 39 -> 35; matrix products, arithmetic and copies ran while one was open for 0% -> 1% of each run, Pallas kernels for 13% -> 12%
where the time goes in v3:
time: 319 us; the launch traced here: 317 us
  waiting for transfers between devices  141 us (44%)
  starting transfers between devices  107 us (34%)
  Pallas kernels  46.9 us (15%)
  local copies, waits for them, and re-layouts  19.2 us (6%)
    ppermute x71, waiting for transfers between devices, hop(): return lax.ppermute(value, AXES, pairs)  141 us
    ppermute x71, starting transfers between devices, hop(): return lax.ppermute(value, AXES, pairs)  107 us
    pallas_call x4, Pallas kernels, attend(): pl.pallas_call(functools.partial(attend_kernel, section, len(parts), rows...  21.5 us
    unnamed x86, local copies, waits for them, and re-layouts  16.5 us
    pallas_call x4, Pallas kernels, project_out(): pl.pallas_call(functools.partial(output_kernel, section, first, len(parts...  10 us
    pallas_call x7, Pallas kernels, pick(): pl.pallas_call(functools.partial(pick_kernel, choice, tuple((len(candidat...  8.61 us
  transfers between devices with their start and end apart: 71, of which 35 were waited for; matrix products, arithmetic and copies ran while one was open for 1% of the time, Pallas kernels for 12%

profile of v3, /device:TPU:5, one launch (start us, length us, event | category | flops | bytes accessed | tf_op | source)
XLA Modules:
  0.0 317.3 jit_solution(815623609317911694)
XLA Ops:
  0.6 5.1 %cut.1 = (bf16[28,64,256]{2,1,0:T(8,128)(2,1)}, bf16[28,64,256]{2,1,0:T(8,128)(2,1)}, bf16[28,64,256]{2,1,0:T(8,128)(2,1)}, bf16[28,64,256]{2,1,0:T(8,128)(2,1)}) custom-call(s32[2]{0:T(128)} %pad_add_fusion.me_ref, bf16[1,4,8,64,256]{4,3,2,1,0:T(8,128)(2,1)} %rest_0_.1, bf16[1,4,8,64,256]{4,3,2,1,0:T(8,128)(2,1)} %rest_1_.1, ...), custom_call_target="tpu_custom_call" | custom-call | flops 1000000000 | tf_op jit(solution)/shard_map/cut/pallas_call | solution.py:293
  9.3 3.2 %collective-permute-start.5 = (bf16[4,192,256]{2,1,0:T(8,128)(2,1)S(1)}, bf16[4,192,256]{2,1,0:T(8,128)(2,1)S(1)}, u32[]{:S(2)}, u32[]{:S(2)}) collective-permute-start(bf16[4,192,256]{2,1,0:T(8,128)(2,1)S(1)} %get-tuple-element.50.rest_0_), channel_id=1, source_target_pairs={{8,10},{9,11},{14,12},{15,13},{24,26},{25,27},{30,28},{31,29}} | collective-permute-start | bytes 1179656 | tf_op jit(solution)/shard_map/ppermute | solution.py:29
  12.6 2.2 collective-permute-start.6
  14.8 1.9 collective-permute-start.9
  16.7 3.0 collective-permute-start.4
  22.6 2.9 collective-permute-start.10
  26.8 10.2 %collective-permute-done.10.rest_3_ = bf16[4,64,256]{2,1,0:T(8,128)(2,1)S(1)} collective-permute-done((bf16[4,64,256]{2,1,0:T(8,128)(2,1)S(1)}, bf16[4,64,256]{2,1,0:T(8,128)(2,1)S(1)}, u32[]{:S(2)}, u32[]{:S(2)}) %collective-permute-start.10) | collective-permute-done | bytes 131104 | tf_op jit(solution)/shard_map/ppermute | solution.py:29
  37.9 2.0 collective-permute-start.11
  40.1 1.8 pick.8.rest_5_
  41.9 2.4 collective-permute-start.17
  44.3 1.6 collective-permute-start.19
  48.5 2.2 collective-permute-start.1
  51.4 1.9 collective-permute-start.2
  54.9 1.7 pick.10
  56.6 3.4 %collective-permute-done.13.rest_3_ = bf16[4,192,256]{2,1,0:T(8,128)(2,1)S(1)} collective-permute-done((bf16[4,192,256]{2,1,0:T(8,128)(2,1)S(1)}, bf16[4,192,256]{2,1,0:T(8,128)(2,1)S(1)}, u32[]{:S(2)}, u32[]{:S(2)}) %collective-permute-start.13) | collective-permute-done | bytes 393248 | tf_op jit(solution)/shard_map/ppermute | solution.py:29
  60.7 4.5 %collective-permute-done.17.rest_7_ = bf16[32,64,256]{2,1,0:T(8,128)(2,1)} collective-permute-done((bf16[32,64,256]{2,1,0:T(8,128)(2,1)S(1)}, bf16[32,64,256]{2,1,0:T(8,128)(2,1)}, u32[]{:S(2)}, u32[]{:S(2)}) %collective-permute-start.17) | collective-permute-done | bytes 1048608 | tf_op jit(solution)/shard_map/ppermute | solution.py:29
  65.2 7.5 %collective-permute-start.21 = (bf16[32,64,256]{2,1,0:T(8,128)(2,1)S(1)}, bf16[32,64,256]{2,1,0:T(8,128)(2,1)}, u32[]{:S(2)}, u32[]{:S(2)}) collective-permute-start(bf16[32,64,256]{2,1,0:T(8,128)(2,1)S(1)} %pick.8.rest_5_), channel_id=1, source_target_pairs={{0,4},{1,5},{6,2},{7,3},{8,12},{9,13},{14,10},{15,11},{16,20},{17,... | collective-permute-start | bytes 3145736 | tf_op jit(solution)/shard_map/ppermute | solution.py:29
  72.7 1.7 pick.9
  75.8 2.5 collective-permute-start.16
  78.8 13.9 %collective-permute-done.21.rest_11_ = bf16[32,64,256]{2,1,0:T(8,128)(2,1)} collective-permute-done((bf16[32,64,256]{2,1,0:T(8,128)(2,1)S(1)}, bf16[32,64,256]{2,1,0:T(8,128)(2,1)}, u32[]{:S(2)}, u32[]{:S(2)}) %collective-permute-start.21) | collective-permute-done | bytes 1048608 | tf_op jit(solution)/shard_map/ppermute | solution.py:29
  92.7 2.4 collective-permute-start.22
  96.1 5.1 %collective-permute-start.32 = (bf16[32,64,256]{2,1,0:T(8,128)(2,1)S(1)}, bf16[32,64,256]{2,1,0:T(8,128)(2,1)}, u32[]{:S(2)}, u32[]{:S(2)}) collective-permute-start(bf16[32,64,256]{2,1,0:T(8,128)(2,1)S(1)} %pick.11.rest_5_), channel_id=1, source_target_pairs={{0,2},{1,3},{6,4},{7,5},{8,10},{9,11},{14,12},{15,13},{16,18},{17,... | collective-permute-start | bytes 3145736 | tf_op jit(solution)/shard_map/ppermute | solution.py:29
  102.1 1.7 collective-permute-start.34
  111.0 5.9 %attend.4.rest_0_ = bf16[4,192,256]{2,1,0:T(8,128)(2,1)S(1)} custom-call(s32[2]{0:T(128)S(1)} %copy-done.31, f32[4,128]{1,0:T(4,128)S(1)} %slice.20.list_ref, s32[4]{0:T(128)S(1)} %broadcast_select_fusion.3.pos_ref, s32[3,4,4]{2,1,0:T(4,128)S(1)} %broadcast_select_fusion.2.mask_ref, bf16[4,192,256]{2,1,0:T(8,128)(2,1)S(1)} %copy-done.15, ...), custom_call_target="tpu_custom_call" | custom-call | flops 1000000000 | tf_op jit(solution)/shard_map/attend/pallas_call | solution.py:252
  117.9 8.3 %collective-permute-done.23.rest_1_ = bf16[4,192,256]{2,1,0:T(8,128)(2,1)S(1)} collective-permute-done((bf16[4,192,256]{2,1,0:T(8,128)(2,1)S(1)}, bf16[4,192,256]{2,1,0:T(8,128)(2,1)S(1)}, u32[]{:S(2)}, u32[]{:S(2)}) %collective-permute-start.23) | collective-permute-done | bytes 393248 | tf_op jit(solution)/shard_map/ppermute | solution.py:29
  129.4 1.9 collective-permute-start.36
  132.0 2.5 collective-permute-done.3.other_ref
  134.5 2.7 project_out.4.rest_0_.rest_4_
  138.2 6.8 %collective-permute-done.26.rest_1_ = bf16[4,192,256]{2,1,0:T(8,128)(2,1)S(1)} collective-permute-done((bf16[4,192,256]{2,1,0:T(8,128)(2,1)S(1)}, bf16[4,192,256]{2,1,0:T(8,128)(2,1)S(1)}, u32[]{:S(2)}, u32[]{:S(2)}) %collective-permute-start.26) | collective-permute-done | bytes 393248 | tf_op jit(solution)/shard_map/ppermute | solution.py:29
  147.0 3.5 %collective-permute-start.31 = (bf16[32,64,256]{2,1,0:T(8,128)(2,1)S(1)}, bf16[32,64,256]{2,1,0:T(8,128)(2,1)S(1)}, u32[]{:S(2)}, u32[]{:S(2)}) collective-permute-start(bf16[32,64,256]{2,1,0:T(8,128)(2,1)S(1)} %pick.11.rest_5_), channel_id=1, source_target_pairs={{0,8},{1,9},{2,10},{3,11},{4,12},{5,13},{6,14},{7,15},{8,0},{9,1},... | collective-permute-start | bytes 3145736 | tf_op jit(solution)/shard_map/ppermute | solution.py:29
  151.1 2.4 collective-permute-done.36.rest_11_
  153.5 3.2 %collective-permute-start.37 = (bf16[32,64,256]{2,1,0:T(8,128)(2,1)S(1)}, bf16[32,64,256]{2,1,0:T(8,128)(2,1)S(1)}, u32[]{:S(2)}, u32[]{:S(2)}) collective-permute-start(bf16[32,64,256]{2,1,0:T(8,128)(2,1)S(1)} %collective-permute-done.36.rest_11_), channel_id=1, source_target_pairs={{0,8},{1,9},{2,10},{3,11},{4,12},{5,13},{6,14},{7,15},{8,0},{9,1},... | collective-permute-start | bytes 3145736 | tf_op jit(solution)/shard_map/ppermute | solution.py:29
  156.7 3.1 collective-permute-start.45
  160.7 4.8 %attend.5 = (bf16[4,192,256]{2,1,0:T(8,128)(2,1)S(1)}, bf16[192,2048]{1,0:T(8,128)(2,1)S(1)}) custom-call(s32[2]{0:T(128)S(1)} %copy-done.31, f32[4,128]{1,0:T(4,128)S(1)} %slice.20.list_ref, s32[4]{0:T(128)S(1)} %broadcast_select_fusion.3.pos_ref, s32[3,4,4]{2,1,0:T(4,128)S(1)} %broadcast_select_fusion.2.mask_ref, ...), custom_call_target="tpu_custom_call" | custom-call | flops 1000000000 | tf_op jit(solution)/shard_map/attend/pallas_call | solution.py:252
  166.8 8.3 %collective-permute-done.38.rest_1_ = bf16[4,192,256]{2,1,0:T(8,128)(2,1)S(1)} collective-permute-done((bf16[4,192,256]{2,1,0:T(8,128)(2,1)S(1)}, bf16[4,192,256]{2,1,0:T(8,128)(2,1)S(1)}, u32[]{:S(2)}, u32[]{:S(2)}) %collective-permute-start.38) | collective-permute-done | bytes 393248 | tf_op jit(solution)/shard_map/ppermute | solution.py:29
  175.0 1.7 collective-permute-done.39.rest_2_
  178.7 3.6 %collective-permute-done.45.rest_7_ = bf16[32,64,256]{2,1,0:T(8,128)(2,1)S(1)} collective-permute-done((bf16[32,64,256]{2,1,0:T(8,128)(2,1)S(1)}, bf16[32,64,256]{2,1,0:T(8,128)(2,1)S(1)}, u32[]{:S(2)}, u32[]{:S(2)}) %collective-permute-start.45) | collective-permute-done | bytes 1048608 | tf_op jit(solution)/shard_map/ppermute | solution.py:29
  183.7 4.0 %collective-permute-start.49 = (bf16[32,64,256]{2,1,0:T(8,128)(2,1)S(1)}, bf16[32,64,256]{2,1,0:T(8,128)(2,1)S(1)}, u32[]{:S(2)}, u32[]{:S(2)}) collective-permute-start(bf16[32,64,256]{2,1,0:T(8,128)(2,1)S(1)} %pick.12.rest_5_), channel_id=1, source_target_pairs={{0,4},{1,5},{6,2},{7,3},{8,12},{9,13},{14,10},{15,11},{16,20},{17,... | collective-permute-start | bytes 3145736 | tf_op jit(solution)/shard_map/ppermute | solution.py:29
  187.6 2.4 project_out.5.rest_0_.rest_4_
  191.7 6.4 %collective-permute-done.41.rest_1_ = bf16[4,192,256]{2,1,0:T(8,128)(2,1)S(1)} collective-permute-done((bf16[4,192,256]{2,1,0:T(8,128)(2,1)S(1)}, bf16[4,192,256]{2,1,0:T(8,128)(2,1)S(1)}, u32[]{:S(2)}, u32[]{:S(2)}) %collective-permute-start.41) | collective-permute-done | bytes 393248 | tf_op jit(solution)/shard_map/ppermute | solution.py:29
  198.1 2.7 collective-permute-done.42.rest_2_
  201.6 1.8 collective-permute-start.44
  203.9 3.7 %collective-permute-done.43.rest_3_ = bf16[4,192,256]{2,1,0:T(8,128)(2,1)S(1)} collective-permute-done((bf16[4,192,256]{2,1,0:T(8,128)(2,1)S(1)}, bf16[4,192,256]{2,1,0:T(8,128)(2,1)S(1)}, u32[]{:S(2)}, u32[]{:S(2)}) %collective-permute-start.43) | collective-permute-done | bytes 393248 | tf_op jit(solution)/shard_map/ppermute | solution.py:29
  208.7 2.2 collective-permute-start.50
  210.9 5.2 %collective-permute-start.58 = (bf16[32,64,256]{2,1,0:T(8,128)(2,1)S(1)}, bf16[32,64,256]{2,1,0:T(8,128)(2,1)S(1)}, u32[]{:S(2)}, u32[]{:S(2)}) collective-permute-start(bf16[32,64,256]{2,1,0:T(8,128)(2,1)S(1)} %pick.13.rest_5_), channel_id=1, source_target_pairs={{0,2},{1,3},{6,4},{7,5},{8,10},{9,11},{14,12},{15,13},{16,18},{17,... | collective-permute-start | bytes 3145736 | tf_op jit(solution)/shard_map/ppermute | solution.py:29
  216.1 1.6 collective-permute-start.60
  217.8 4.7 %attend.6 = (bf16[4,192,256]{2,1,0:T(8,128)(2,1)S(1)}, bf16[192,2048]{1,0:T(8,128)(2,1)S(1)}) custom-call(s32[2]{0:T(128)S(1)} %copy-done.31, f32[4,128]{1,0:T(4,128)S(1)} %slice.20.list_ref, s32[4]{0:T(128)S(1)} %broadcast_select_fusion.3.pos_ref, s32[3,4,4]{2,1,0:T(4,128)S(1)} %broadcast_select_fusion.2.mask_ref, ...), custom_call_target="tpu_custom_call" | custom-call | flops 1000000000 | tf_op jit(solution)/shard_map/attend/pallas_call | solution.py:252
  224.5 8.3 %collective-permute-done.51.rest_1_ = bf16[4,192,256]{2,1,0:T(8,128)(2,1)S(1)} collective-permute-done((bf16[4,192,256]{2,1,0:T(8,128)(2,1)S(1)}, bf16[4,192,256]{2,1,0:T(8,128)(2,1)S(1)}, u32[]{:S(2)}, u32[]{:S(2)}) %collective-permute-start.51) | collective-permute-done | bytes 393248 | tf_op jit(solution)/shard_map/ppermute | solution.py:29
  232.8 1.7 collective-permute-done.52.rest_2_
  235.4 3.2 %collective-permute-done.58.rest_7_ = bf16[32,64,256]{2,1,0:T(8,128)(2,1)S(1)} collective-permute-done((bf16[32,64,256]{2,1,0:T(8,128)(2,1)S(1)}, bf16[32,64,256]{2,1,0:T(8,128)(2,1)S(1)}, u32[]{:S(2)}, u32[]{:S(2)}) %collective-permute-start.58) | collective-permute-done | bytes 1048608 | tf_op jit(solution)/shard_map/ppermute | solution.py:29
  238.6 2.8 collective-permute-done.53.rest_3_
  241.4 3.9 %collective-permute-start.62 = (bf16[32,64,256]{2,1,0:T(8,128)(2,1)S(1)}, bf16[32,64,256]{2,1,0:T(8,128)(2,1)}, u32[]{:S(2)}, u32[]{:S(2)}) collective-permute-start(bf16[32,64,256]{2,1,0:T(8,128)(2,1)S(1)} %pick.13.rest_5_), channel_id=1, source_target_pairs={{0,4},{1,5},{6,2},{7,3},{8,12},{9,13},{14,10},{15,11},{16,20},{17,... | collective-permute-start | bytes 3145736 | tf_op jit(solution)/shard_map/ppermute | solution.py:29
  245.3 2.2 project_out.6.rest_0_.rest_4_
  249.4 6.0 %collective-permute-done.54.rest_1_ = bf16[4,192,256]{2,1,0:T(8,128)(2,1)S(1)} collective-permute-done((bf16[4,192,256]{2,1,0:T(8,128)(2,1)S(1)}, bf16[4,192,256]{2,1,0:T(8,128)(2,1)S(1)}, u32[]{:S(2)}, u32[]{:S(2)}) %collective-permute-start.54) | collective-permute-done | bytes 393248 | tf_op jit(solution)/shard_map/ppermute | solution.py:29
  255.4 3.1 collective-permute-done.55.rest_2_
  263.0 3.3 %collective-permute-done.56.rest_3_ = bf16[4,192,256]{2,1,0:T(8,128)(2,1)S(1)} collective-permute-done((bf16[4,192,256]{2,1,0:T(8,128)(2,1)S(1)}, bf16[4,192,256]{2,1,0:T(8,128)(2,1)S(1)}, u32[]{:S(2)}, u32[]{:S(2)}) %collective-permute-start.56) | collective-permute-done | bytes 393248 | tf_op jit(solution)/shard_map/ppermute | solution.py:29
  267.0 2.4 collective-permute-start.63
  275.1 6.1 %attend.7 = (bf16[4,192,256]{2,1,0:T(8,128)(2,1)S(1)}, bf16[192,2048]{1,0:T(8,128)(2,1)S(1)}) custom-call(s32[2]{0:T(128)S(1)} %copy-done.31, f32[4,128]{1,0:T(4,128)S(1)} %slice.20.list_ref, s32[4]{0:T(128)S(1)} %broadcast_select_fusion.3.pos_ref, s32[3,4,4]{2,1,0:T(4,128)S(1)} %broadcast_select_fusion.2.mask_ref, ...), custom_call_target="tpu_custom_call" | custom-call | flops 1000000000 | tf_op jit(solution)/shard_map/attend/pallas_call | solution.py:252
  283.4 7.2 %collective-permute-done.66.rest_1_ = bf16[4,192,256]{2,1,0:T(8,128)(2,1)S(1)} collective-permute-done((bf16[4,192,256]{2,1,0:T(8,128)(2,1)S(1)}, bf16[4,192,256]{2,1,0:T(8,128)(2,1)S(1)}, u32[]{:S(2)}, u32[]{:S(2)}) %collective-permute-start.66) | collective-permute-done | bytes 393248 | tf_op jit(solution)/shard_map/ppermute | solution.py:29
  290.6 2.2 collective-permute-done.67.rest_2_
  294.6 5.1 %collective-permute-done.68.rest_3_ = bf16[4,192,256]{2,1,0:T(8,128)(2,1)S(1)} collective-permute-done((bf16[4,192,256]{2,1,0:T(8,128)(2,1)S(1)}, bf16[4,192,256]{2,1,0:T(8,128)(2,1)S(1)}, u32[]{:S(2)}, u32[]{:S(2)}) %collective-permute-start.68) | collective-permute-done | bytes 393248 | tf_op jit(solution)/shard_map/ppermute | solution.py:29
  299.7 2.7 project_out.7
  305.0 7.4 %collective-permute-done.69 = bf16[4,192,256]{2,1,0:T(8,128)(2,1)S(1)} collective-permute-done((bf16[4,192,256]{2,1,0:T(8,128)(2,1)S(1)}, bf16[4,192,256]{2,1,0:T(8,128)(2,1)S(1)}, u32[]{:S(2)}, u32[]{:S(2)}) %collective-permute-start.69) | collective-permute-done | bytes 393248 | tf_op jit(solution)/shard_map/ppermute | solution.py:29
  312.4 1.8 collective-permute-done.70
  (194 shorter events, 68.9 us)
Async XLA Ops:
  8.1 13.2 %collective-permute-start.7 = (bf16[16,64,256]{2,1,0:T(8,128)(2,1)S(1)}, bf16[16,64,256]{2,1,0:T(8,128)(2,1)}, u32[]{:S(2)}, u32[]{:S(2)}) collective-permute-start(bf16[16,64,256]{2,1,0:T(8,128)(2,1)S(1)} %get-tuple-element.51), channel_id=1, source_target_pairs={{0,1},{1,0},{2,3},{3,2},{4,5},{5,4},{6,7},{7,6},{8,9},{9,8},{10,11... | collective-permute-start | bytes 1572872 | tf_op jit(solution)/shard_map/ppermute | solution.py:29
  9.3 11.1 %collective-permute-start.5 = (bf16[4,192,256]{2,1,0:T(8,128)(2,1)S(1)}, bf16[4,192,256]{2,1,0:T(8,128)(2,1)S(1)}, u32[]{:S(2)}, u32[]{:S(2)}) collective-permute-start(bf16[4,192,256]{2,1,0:T(8,128)(2,1)S(1)} %get-tuple-element.50.rest_0_), channel_id=1, source_target_pairs={{8,10},{9,11},{14,12},{15,13},{24,26},{25,27},{30,28},{31,29}} | collective-permute-start | bytes 1179656 | tf_op jit(solution)/shard_map/ppermute | solution.py:29
  12.6 25.3 %collective-permute-start.6 = (bf16[28,64,256]{2,1,0:T(8,128)(2,1)}, bf16[28,64,256]{2,1,0:T(8,128)(2,1)S(1)}, u32[]{:S(2)}, u32[]{:S(2)}) collective-permute-start(bf16[28,64,256]{2,1,0:T(8,128)(2,1)} %get-tuple-element.64.rest_0_), channel_id=1, source_target_pairs={{0,16},{1,17},{2,18},{3,19},{4,20},{5,21},{6,22},{7,23},{24,8},{25... | collective-permute-start | bytes 2752520 | tf_op jit(solution)/shard_map/ppermute | solution.py:29
  14.8 23.1 %collective-permute-start.9 = (bf16[28,64,256]{2,1,0:T(8,128)(2,1)}, bf16[28,64,256]{2,1,0:T(8,128)(2,1)}, u32[]{:S(2)}, u32[]{:S(2)}) collective-permute-start(bf16[28,64,256]{2,1,0:T(8,128)(2,1)} %get-tuple-element.66.rest_0_), channel_id=1, source_target_pairs={{0,24},{1,25},{2,26},{3,27},{4,28},{5,29},{6,30},{7,31},{24,0},{25... | collective-permute-start | bytes 2752520 | tf_op jit(solution)/shard_map/ppermute | solution.py:29
  20.5 19.6 %collective-permute-start.14 = (bf16[28,64,256]{2,1,0:T(8,128)(2,1)}, bf16[28,64,256]{2,1,0:T(8,128)(2,1)S(1)}, u32[]{:S(2)}, u32[]{:S(2)}) collective-permute-start(bf16[28,64,256]{2,1,0:T(8,128)(2,1)} %get-tuple-element.57), channel_id=1, source_target_pairs={{0,8},{1,9},{2,10},{3,11},{4,12},{5,13},{6,14},{7,15},{8,0},{9,1},... | collective-permute-start | bytes 2752520 | tf_op jit(solution)/shard_map/ppermute | solution.py:29
  22.6 14.5 %collective-permute-start.10 = (bf16[4,64,256]{2,1,0:T(8,128)(2,1)S(1)}, bf16[4,64,256]{2,1,0:T(8,128)(2,1)S(1)}, u32[]{:S(2)}, u32[]{:S(2)}) collective-permute-start(bf16[4,64,256]{2,1,0:T(8,128)(2,1)S(1)} %get-tuple-element.54.rest_1_), channel_id=1, source_target_pairs={{0,24},{1,25},{2,26},{3,27},{4,28},{5,29},{6,30},{7,31},{24,0},{25... | collective-permute-start | bytes 393224 | tf_op jit(solution)/shard_map/ppermute | solution.py:29
  25.5 12.4 %collective-permute-start.8 = (bf16[4,64,256]{2,1,0:T(8,128)(2,1)S(1)}, bf16[4,64,256]{2,1,0:T(8,128)(2,1)S(1)}, u32[]{:S(2)}, u32[]{:S(2)}) collective-permute-start(bf16[4,64,256]{2,1,0:T(8,128)(2,1)S(1)} %get-tuple-element.52.rest_1_), channel_id=1, source_target_pairs={{0,16},{1,17},{2,18},{3,19},{4,20},{5,21},{6,22},{7,23},{24,8},{25... | collective-permute-start | bytes 393224 | tf_op jit(solution)/shard_map/ppermute | solution.py:29
  37.9 10.6 %collective-permute-start.11 = (bf16[4,192,256]{2,1,0:T(8,128)(2,1)S(1)}, bf16[4,192,256]{2,1,0:T(8,128)(2,1)S(1)}, u32[]{:S(2)}, u32[]{:S(2)}) collective-permute-start(bf16[4,192,256]{2,1,0:T(8,128)(2,1)S(1)} %pick.7.rest_0_.rest_4_), channel_id=1, source_target_pairs={{0,1},{1,0},{2,3},{3,2},{4,5},{5,4},{6,7},{7,6},{8,24},{9,25},{10,... | collective-permute-start | bytes 1179656 | tf_op jit(solution)/shard_map/ppermute | solution.py:29
  39.9 10.8 %collective-permute-start.12 = (bf16[4,192,256]{2,1,0:T(8,128)(2,1)S(1)}, bf16[4,192,256]{2,1,0:T(8,128)(2,1)S(1)}, u32[]{:S(2)}, u32[]{:S(2)}) collective-permute-start(bf16[4,192,256]{2,1,0:T(8,128)(2,1)S(1)} %pick.7.rest_0_.rest_4_), channel_id=1, source_target_pairs={{0,16},{1,17},{2,18},{3,19},{4,20},{5,21},{6,22},{7,23},{8,9},{9,8... | collective-permute-start | bytes 1179656 | tf_op jit(solution)/shard_map/ppermute | solution.py:29
  41.9 23.3 %collective-permute-start.17 = (bf16[32,64,256]{2,1,0:T(8,128)(2,1)S(1)}, bf16[32,64,256]{2,1,0:T(8,128)(2,1)}, u32[]{:S(2)}, u32[]{:S(2)}) collective-permute-start(bf16[32,64,256]{2,1,0:T(8,128)(2,1)S(1)} %pick.8.rest_5_), channel_id=1, source_target_pairs={{0,2},{1,3},{6,4},{7,5},{8,10},{9,11},{14,12},{15,13},{16,18},{17,... | collective-permute-start | bytes 3145736 | tf_op jit(solution)/shard_map/ppermute | solution.py:29
  44.3 20.9 %collective-permute-start.19 = (bf16[32,64,256]{2,1,0:T(8,128)(2,1)S(1)}, bf16[32,64,256]{2,1,0:T(8,128)(2,1)}, u32[]{:S(2)}, u32[]{:S(2)}) collective-permute-start(bf16[32,64,256]{2,1,0:T(8,128)(2,1)S(1)} %pick.8.rest_5_), channel_id=1, source_target_pairs={{2,4},{3,5},{4,2},{5,3},{10,12},{11,13},{12,10},{13,11},{18,20},{1... | collective-permute-start | bytes 3145736 | tf_op jit(solution)/shard_map/ppermute | solution.py:29
  46.0 7.4 %collective-permute-start = (f32[1,4224]{1,0:T(1,128)S(1)}, f32[1,4224]{1,0:T(1,128)S(1)}, u32[]{:S(2)}, u32[]{:S(2)}) collective-permute-start(f32[1,4224]{1,0:T(1,128)S(1)} %get-tuple-element.49), channel_id=1, source_target_pairs={{0,8},{1,9},{2,10},{3,11},{4,12},{5,13},{6,14},{7,15},{8,0},{9,1},... | collective-permute-start | bytes 50696 | tf_op jit(solution)/shard_map/ppermute | solution.py:29
  60.0 18.4 %collective-permute-start.30 = (bf16[32,64,256]{2,1,0:T(8,128)(2,1)S(1)}, bf16[32,64,256]{2,1,0:T(8,128)(2,1)S(1)}, u32[]{:S(2)}, u32[]{:S(2)}) collective-permute-start(bf16[32,64,256]{2,1,0:T(8,128)(2,1)S(1)} %pick.10), channel_id=1, source_target_pairs={{8,16},{9,17},{10,18},{11,19},{12,20},{13,21},{14,22},{15,23},{16,... | collective-permute-start | bytes 3145736 | tf_op jit(solution)/shard_map/ppermute | solution.py:29
  65.2 27.5 %collective-permute-start.21 = (bf16[32,64,256]{2,1,0:T(8,128)(2,1)S(1)}, bf16[32,64,256]{2,1,0:T(8,128)(2,1)}, u32[]{:S(2)}, u32[]{:S(2)}) collective-permute-start(bf16[32,64,256]{2,1,0:T(8,128)(2,1)S(1)} %pick.8.rest_5_), channel_id=1, source_target_pairs={{0,4},{1,5},{6,2},{7,3},{8,12},{9,13},{14,10},{15,11},{16,20},{17,... | collective-permute-start | bytes 3145736 | tf_op jit(solution)/shard_map/ppermute | solution.py:29
  74.5 20.6 %collective-permute-start.29 = (bf16[32,64,256]{2,1,0:T(8,128)(2,1)S(1)}, bf16[32,64,256]{2,1,0:T(8,128)(2,1)S(1)}, u32[]{:S(2)}, u32[]{:S(2)}) collective-permute-start(bf16[32,64,256]{2,1,0:T(8,128)(2,1)S(1)} %pick.9), channel_id=1, source_target_pairs={{8,24},{9,25},{10,26},{11,27},{12,28},{13,29},{14,30},{15,31},{16,... | collective-permute-start | bytes 3145736 | tf_op jit(solution)/shard_map/ppermute | solution.py:29
  75.8 25.4 %collective-permute-start.16 = (bf16[32,64,256]{2,1,0:T(8,128)(2,1)S(1)}, bf16[32,64,256]{2,1,0:T(8,128)(2,1)S(1)}, u32[]{:S(2)}, u32[]{:S(2)}) collective-permute-start(bf16[32,64,256]{2,1,0:T(8,128)(2,1)S(1)} %pick.8.rest_5_), channel_id=1, source_target_pairs={{0,8},{1,9},{2,10},{3,11},{4,12},{5,13},{6,14},{7,15},{8,0},{9,1},... | collective-permute-start | bytes 3145736 | tf_op jit(solution)/shard_map/ppermute | solution.py:29
  78.3 26.2 %collective-permute-start.18 = (bf16[32,64,256]{2,1,0:T(8,128)(2,1)}, bf16[32,64,256]{2,1,0:T(8,128)(2,1)}, u32[]{:S(2)}, u32[]{:S(2)}) collective-permute-start(bf16[32,64,256]{2,1,0:T(8,128)(2,1)} %collective-permute-done.17.rest_7_), channel_id=1, source_target_pairs={{0,8},{1,9},{2,10},{3,11},{4,12},{5,13},{6,14},{7,15},{8,0},{9,1},... | collective-permute-start | bytes 3145736 | tf_op jit(solution)/shard_map/ppermute | solution.py:29
  78.4 26.1 %collective-permute-start.20 = (bf16[32,64,256]{2,1,0:T(8,128)(2,1)}, bf16[32,64,256]{2,1,0:T(8,128)(2,1)}, u32[]{:S(2)}, u32[]{:S(2)}) collective-permute-start(bf16[32,64,256]{2,1,0:T(8,128)(2,1)} %collective-permute-done.19.rest_9_), channel_id=1, source_target_pairs={{0,8},{1,9},{2,10},{3,11},{4,12},{5,13},{6,14},{7,15},{8,0},{9,1},... | collective-permute-start | bytes 3145736 | tf_op jit(solution)/shard_map/ppermute | solution.py:29
  92.7 11.8 %collective-permute-start.22 = (bf16[32,64,256]{2,1,0:T(8,128)(2,1)}, bf16[32,64,256]{2,1,0:T(8,128)(2,1)}, u32[]{:S(2)}, u32[]{:S(2)}) collective-permute-start(bf16[32,64,256]{2,1,0:T(8,128)(2,1)} %collective-permute-done.21.rest_11_), channel_id=1, source_target_pairs={{0,8},{1,9},{2,10},{3,11},{4,12},{5,13},{6,14},{7,15},{8,0},{9,1},... | collective-permute-start | bytes 3145736 | tf_op jit(solution)/shard_map/ppermute | solution.py:29
  96.1 33.3 %collective-permute-start.32 = (bf16[32,64,256]{2,1,0:T(8,128)(2,1)S(1)}, bf16[32,64,256]{2,1,0:T(8,128)(2,1)}, u32[]{:S(2)}, u32[]{:S(2)}) collective-permute-start(bf16[32,64,256]{2,1,0:T(8,128)(2,1)S(1)} %pick.11.rest_5_), channel_id=1, source_target_pairs={{0,2},{1,3},{6,4},{7,5},{8,10},{9,11},{14,12},{15,13},{16,18},{17,... | collective-permute-start | bytes 3145736 | tf_op jit(solution)/shard_map/ppermute | solution.py:29
  102.1 27.2 %collective-permute-start.34 = (bf16[32,64,256]{2,1,0:T(8,128)(2,1)S(1)}, bf16[32,64,256]{2,1,0:T(8,128)(2,1)}, u32[]{:S(2)}, u32[]{:S(2)}) collective-permute-start(bf16[32,64,256]{2,1,0:T(8,128)(2,1)S(1)} %pick.11.rest_5_), channel_id=1, source_target_pairs={{2,4},{3,5},{4,2},{5,3},{10,12},{11,13},{12,10},{13,11},{18,20},{1... | collective-permute-start | bytes 3145736 | tf_op jit(solution)/shard_map/ppermute | solution.py:29
  116.9 9.3 %collective-permute-start.23 = (bf16[4,192,256]{2,1,0:T(8,128)(2,1)S(1)}, bf16[4,192,256]{2,1,0:T(8,128)(2,1)S(1)}, u32[]{:S(2)}, u32[]{:S(2)}) collective-permute-start(bf16[4,192,256]{2,1,0:T(8,128)(2,1)S(1)} %attend.4.rest_0_), channel_id=1, source_target_pairs={{0,1},{1,0},{2,3},{3,2},{4,5},{5,4},{6,7},{7,6},{8,24},{9,25},{10,... | collective-permute-start | bytes 1179656 | tf_op jit(solution)/shard_map/ppermute | solution.py:29
  117.0 10.6 %collective-permute-start.24 = (bf16[4,192,256]{2,1,0:T(8,128)(2,1)S(1)}, bf16[4,192,256]{2,1,0:T(8,128)(2,1)S(1)}, u32[]{:S(2)}, u32[]{:S(2)}) collective-permute-start(bf16[4,192,256]{2,1,0:T(8,128)(2,1)S(1)} %attend.4.rest_0_), channel_id=1, source_target_pairs={{0,16},{1,17},{2,18},{3,19},{4,20},{5,21},{6,22},{7,23},{8,9},{9,8... | collective-permute-start | bytes 1179656 | tf_op jit(solution)/shard_map/ppermute | solution.py:29
  127.6 6.9 %collective-permute-start.25 = (bf16[4,192,256]{2,1,0:T(8,128)(2,1)S(1)}, bf16[4,192,256]{2,1,0:T(8,128)(2,1)S(1)}, u32[]{:S(2)}, u32[]{:S(2)}) collective-permute-start(bf16[4,192,256]{2,1,0:T(8,128)(2,1)S(1)} %collective-permute-done.23.rest_1_), channel_id=1, source_target_pairs={{0,16},{1,17},{2,18},{3,19},{4,20},{5,21},{6,22},{7,23},{8,9},{9,8... | collective-permute-start | bytes 1179656 | tf_op jit(solution)/shard_map/ppermute | solution.py:29
  129.4 24.1 %collective-permute-start.36 = (bf16[32,64,256]{2,1,0:T(8,128)(2,1)S(1)}, bf16[32,64,256]{2,1,0:T(8,128)(2,1)S(1)}, u32[]{:S(2)}, u32[]{:S(2)}) collective-permute-start(bf16[32,64,256]{2,1,0:T(8,128)(2,1)S(1)} %pick.11.rest_5_), channel_id=1, source_target_pairs={{0,4},{1,5},{6,2},{7,3},{8,12},{9,13},{14,10},{15,11},{16,20},{17,... | collective-permute-start | bytes 3145736 | tf_op jit(solution)/shard_map/ppermute | solution.py:29
  137.2 7.7 %collective-permute-start.26 = (bf16[4,192,256]{2,1,0:T(8,128)(2,1)S(1)}, bf16[4,192,256]{2,1,0:T(8,128)(2,1)S(1)}, u32[]{:S(2)}, u32[]{:S(2)}) collective-permute-start(bf16[4,192,256]{2,1,0:T(8,128)(2,1)S(1)} %project_out.4.rest_0_.rest_4_), channel_id=1, source_target_pairs={{0,1},{1,0},{2,3},{3,2},{4,5},{5,4},{6,7},{7,6},{8,24},{9,25},{10,... | collective-permute-start | bytes 1179656 | tf_op jit(solution)/shard_map/ppermute | solution.py:29
  137.3 8.9 %collective-permute-start.27 = (bf16[4,192,256]{2,1,0:T(8,128)(2,1)S(1)}, bf16[4,192,256]{2,1,0:T(8,128)(2,1)S(1)}, u32[]{:S(2)}, u32[]{:S(2)}) collective-permute-start(bf16[4,192,256]{2,1,0:T(8,128)(2,1)S(1)} %project_out.4.rest_0_.rest_4_), channel_id=1, source_target_pairs={{0,16},{1,17},{2,18},{3,19},{4,20},{5,21},{6,22},{7,23},{8,9},{9,8... | collective-permute-start | bytes 1179656 | tf_op jit(solution)/shard_map/ppermute | solution.py:29
  146.2 7.2 %collective-permute-start.28 = (bf16[4,192,256]{2,1,0:T(8,128)(2,1)S(1)}, bf16[4,192,256]{2,1,0:T(8,128)(2,1)S(1)}, u32[]{:S(2)}, u32[]{:S(2)}) collective-permute-start(bf16[4,192,256]{2,1,0:T(8,128)(2,1)S(1)} %collective-permute-done.26.rest_1_), channel_id=1, source_target_pairs={{0,16},{1,17},{2,18},{3,19},{4,20},{5,21},{6,22},{7,23},{8,9},{9,8... | collective-permute-start | bytes 1179656 | tf_op jit(solution)/shard_map/ppermute | solution.py:29
  147.0 12.7 %collective-permute-start.31 = (bf16[32,64,256]{2,1,0:T(8,128)(2,1)S(1)}, bf16[32,64,256]{2,1,0:T(8,128)(2,1)S(1)}, u32[]{:S(2)}, u32[]{:S(2)}) collective-permute-start(bf16[32,64,256]{2,1,0:T(8,128)(2,1)S(1)} %pick.11.rest_5_), channel_id=1, source_target_pairs={{0,8},{1,9},{2,10},{3,11},{4,12},{5,13},{6,14},{7,15},{8,0},{9,1},... | collective-permute-start | bytes 3145736 | tf_op jit(solution)/shard_map/ppermute | solution.py:29
  150.6 10.1 %collective-permute-start.33 = (bf16[32,64,256]{2,1,0:T(8,128)(2,1)}, bf16[32,64,256]{2,1,0:T(8,128)(2,1)S(1)}, u32[]{:S(2)}, u32[]{:S(2)}) collective-permute-start(bf16[32,64,256]{2,1,0:T(8,128)(2,1)} %collective-permute-done.32.rest_7_), channel_id=1, source_target_pairs={{0,8},{1,9},{2,10},{3,11},{4,12},{5,13},{6,14},{7,15},{8,0},{9,1},... | collective-permute-start | bytes 3145736 | tf_op jit(solution)/shard_map/ppermute | solution.py:29
  150.6 10.1 %collective-permute-start.35 = (bf16[32,64,256]{2,1,0:T(8,128)(2,1)}, bf16[32,64,256]{2,1,0:T(8,128)(2,1)S(1)}, u32[]{:S(2)}, u32[]{:S(2)}) collective-permute-start(bf16[32,64,256]{2,1,0:T(8,128)(2,1)} %collective-permute-done.34.rest_9_), channel_id=1, source_target_pairs={{0,8},{1,9},{2,10},{3,11},{4,12},{5,13},{6,14},{7,15},{8,0},{9,1},... | collective-permute-start | bytes 3145736 | tf_op jit(solution)/shard_map/ppermute | solution.py:29
  153.5 7.3 %collective-permute-start.37 = (bf16[32,64,256]{2,1,0:T(8,128)(2,1)S(1)}, bf16[32,64,256]{2,1,0:T(8,128)(2,1)S(1)}, u32[]{:S(2)}, u32[]{:S(2)}) collective-permute-start(bf16[32,64,256]{2,1,0:T(8,128)(2,1)S(1)} %collective-permute-done.36.rest_11_), channel_id=1, source_target_pairs={{0,8},{1,9},{2,10},{3,11},{4,12},{5,13},{6,14},{7,15},{8,0},{9,1},... | collective-permute-start | bytes 3145736 | tf_op jit(solution)/shard_map/ppermute | solution.py:29
  156.7 25.6 %collective-permute-start.45 = (bf16[32,64,256]{2,1,0:T(8,128)(2,1)S(1)}, bf16[32,64,256]{2,1,0:T(8,128)(2,1)S(1)}, u32[]{:S(2)}, u32[]{:S(2)}) collective-permute-start(bf16[32,64,256]{2,1,0:T(8,128)(2,1)S(1)} %pick.12.rest_5_), channel_id=1, source_target_pairs={{0,2},{1,3},{6,4},{7,5},{8,10},{9,11},{14,12},{15,13},{16,18},{17,... | collective-permute-start | bytes 3145736 | tf_op jit(solution)/shard_map/ppermute | solution.py:29
  159.8 22.5 %collective-permute-start.47 = (bf16[32,64,256]{2,1,0:T(8,128)(2,1)S(1)}, bf16[32,64,256]{2,1,0:T(8,128)(2,1)S(1)}, u32[]{:S(2)}, u32[]{:S(2)}) collective-permute-start(bf16[32,64,256]{2,1,0:T(8,128)(2,1)S(1)} %pick.12.rest_5_), channel_id=1, source_target_pairs={{2,4},{3,5},{4,2},{5,3},{10,12},{11,13},{12,10},{13,11},{18,20},{1... | collective-permute-start | bytes 3145736 | tf_op jit(solution)/shard_map/ppermute | solution.py:29
  165.6 9.5 %collective-permute-start.38 = (bf16[4,192,256]{2,1,0:T(8,128)(2,1)S(1)}, bf16[4,192,256]{2,1,0:T(8,128)(2,1)S(1)}, u32[]{:S(2)}, u32[]{:S(2)}) collective-permute-start(bf16[4,192,256]{2,1,0:T(8,128)(2,1)S(1)} %get-tuple-element.71.rest_0_), channel_id=1, source_target_pairs={{0,1},{1,0},{2,3},{3,2},{4,5},{5,4},{6,7},{7,6},{8,24},{9,25},{10,... | collective-permute-start | bytes 1179656 | tf_op jit(solution)/shard_map/ppermute | solution.py:29
  165.9 10.8 %collective-permute-start.39 = (bf16[4,192,256]{2,1,0:T(8,128)(2,1)S(1)}, bf16[4,192,256]{2,1,0:T(8,128)(2,1)S(1)}, u32[]{:S(2)}, u32[]{:S(2)}) collective-permute-start(bf16[4,192,256]{2,1,0:T(8,128)(2,1)S(1)} %get-tuple-element.71.rest_0_), channel_id=1, source_target_pairs={{0,16},{1,17},{2,18},{3,19},{4,20},{5,21},{6,22},{7,23},{8,9},{9,8... | collective-permute-start | bytes 1179656 | tf_op jit(solution)/shard_map/ppermute | solution.py:29
  176.7 6.9 %collective-permute-start.40 = (bf16[4,192,256]{2,1,0:T(8,128)(2,1)S(1)}, bf16[4,192,256]{2,1,0:T(8,128)(2,1)S(1)}, u32[]{:S(2)}, u32[]{:S(2)}) collective-permute-start(bf16[4,192,256]{2,1,0:T(8,128)(2,1)S(1)} %collective-permute-done.38.rest_1_), channel_id=1, source_target_pairs={{0,16},{1,17},{2,18},{3,19},{4,20},{5,21},{6,22},{7,23},{8,9},{9,8... | collective-permute-start | bytes 1179656 | tf_op jit(solution)/shard_map/ppermute | solution.py:29
  183.7 25.1 %collective-permute-start.49 = (bf16[32,64,256]{2,1,0:T(8,128)(2,1)S(1)}, bf16[32,64,256]{2,1,0:T(8,128)(2,1)S(1)}, u32[]{:S(2)}, u32[]{:S(2)}) collective-permute-start(bf16[32,64,256]{2,1,0:T(8,128)(2,1)S(1)} %pick.12.rest_5_), channel_id=1, source_target_pairs={{0,4},{1,5},{6,2},{7,3},{8,12},{9,13},{14,10},{15,11},{16,20},{17,... | collective-permute-start | bytes 3145736 | tf_op jit(solution)/shard_map/ppermute | solution.py:29
  190.0 8.0 %collective-permute-start.41 = (bf16[4,192,256]{2,1,0:T(8,128)(2,1)S(1)}, bf16[4,192,256]{2,1,0:T(8,128)(2,1)S(1)}, u32[]{:S(2)}, u32[]{:S(2)}) collective-permute-start(bf16[4,192,256]{2,1,0:T(8,128)(2,1)S(1)} %project_out.5.rest_0_.rest_4_), channel_id=1, source_target_pairs={{0,1},{1,0},{2,3},{3,2},{4,5},{5,4},{6,7},{7,6},{8,24},{9,25},{10,... | collective-permute-start | bytes 1179656 | tf_op jit(solution)/shard_map/ppermute | solution.py:29
  190.9 9.8 %collective-permute-start.42 = (bf16[4,192,256]{2,1,0:T(8,128)(2,1)S(1)}, bf16[4,192,256]{2,1,0:T(8,128)(2,1)S(1)}, u32[]{:S(2)}, u32[]{:S(2)}) collective-permute-start(bf16[4,192,256]{2,1,0:T(8,128)(2,1)S(1)} %project_out.5.rest_0_.rest_4_), channel_id=1, source_target_pairs={{0,16},{1,17},{2,18},{3,19},{4,20},{5,21},{6,22},{7,23},{8,9},{9,8... | collective-permute-start | bytes 1179656 | tf_op jit(solution)/shard_map/ppermute | solution.py:29
  200.7 6.9 %collective-permute-start.43 = (bf16[4,192,256]{2,1,0:T(8,128)(2,1)S(1)}, bf16[4,192,256]{2,1,0:T(8,128)(2,1)S(1)}, u32[]{:S(2)}, u32[]{:S(2)}) collective-permute-start(bf16[4,192,256]{2,1,0:T(8,128)(2,1)S(1)} %collective-permute-done.41.rest_1_), channel_id=1, source_target_pairs={{0,16},{1,17},{2,18},{3,19},{4,20},{5,21},{6,22},{7,23},{8,9},{9,8... | collective-permute-start | bytes 1179656 | tf_op jit(solution)/shard_map/ppermute | solution.py:29
  201.6 14.6 %collective-permute-start.44 = (bf16[32,64,256]{2,1,0:T(8,128)(2,1)S(1)}, bf16[32,64,256]{2,1,0:T(8,128)(2,1)S(1)}, u32[]{:S(2)}, u32[]{:S(2)}) collective-permute-start(bf16[32,64,256]{2,1,0:T(8,128)(2,1)S(1)} %pick.12.rest_5_), channel_id=1, source_target_pairs={{0,8},{1,9},{2,10},{3,11},{4,12},{5,13},{6,14},{7,15},{8,0},{9,1},... | collective-permute-start | bytes 3145736 | tf_op jit(solution)/shard_map/ppermute | solution.py:29
  203.4 14.4 %collective-permute-start.46 = (bf16[32,64,256]{2,1,0:T(8,128)(2,1)S(1)}, bf16[32,64,256]{2,1,0:T(8,128)(2,1)S(1)}, u32[]{:S(2)}, u32[]{:S(2)}) collective-permute-start(bf16[32,64,256]{2,1,0:T(8,128)(2,1)S(1)} %collective-permute-done.45.rest_7_), channel_id=1, source_target_pairs={{0,8},{1,9},{2,10},{3,11},{4,12},{5,13},{6,14},{7,15},{8,0},{9,1},... | collective-permute-start | bytes 3145736 | tf_op jit(solution)/shard_map/ppermute | solution.py:29
  203.4 14.4 %collective-permute-start.48 = (bf16[32,64,256]{2,1,0:T(8,128)(2,1)S(1)}, bf16[32,64,256]{2,1,0:T(8,128)(2,1)S(1)}, u32[]{:S(2)}, u32[]{:S(2)}) collective-permute-start(bf16[32,64,256]{2,1,0:T(8,128)(2,1)S(1)} %collective-permute-done.47.rest_9_), channel_id=1, source_target_pairs={{0,8},{1,9},{2,10},{3,11},{4,12},{5,13},{6,14},{7,15},{8,0},{9,1},... | collective-permute-start | bytes 3145736 | tf_op jit(solution)/shard_map/ppermute | solution.py:29
  208.7 9.0 %collective-permute-start.50 = (bf16[32,64,256]{2,1,0:T(8,128)(2,1)S(1)}, bf16[32,64,256]{2,1,0:T(8,128)(2,1)S(1)}, u32[]{:S(2)}, u32[]{:S(2)}) collective-permute-start(bf16[32,64,256]{2,1,0:T(8,128)(2,1)S(1)} %collective-permute-done.49.rest_11_), channel_id=1, source_target_pairs={{0,8},{1,9},{2,10},{3,11},{4,12},{5,13},{6,14},{7,15},{8,0},{9,1},... | collective-permute-start | bytes 3145736 | tf_op jit(solution)/shard_map/ppermute | solution.py:29
  210.9 27.7 %collective-permute-start.58 = (bf16[32,64,256]{2,1,0:T(8,128)(2,1)S(1)}, bf16[32,64,256]{2,1,0:T(8,128)(2,1)S(1)}, u32[]{:S(2)}, u32[]{:S(2)}) collective-permute-start(bf16[32,64,256]{2,1,0:T(8,128)(2,1)S(1)} %pick.13.rest_5_), channel_id=1, source_target_pairs={{0,2},{1,3},{6,4},{7,5},{8,10},{9,11},{14,12},{15,13},{16,18},{17,... | collective-permute-start | bytes 3145736 | tf_op jit(solution)/shard_map/ppermute | solution.py:29
  216.1 22.5 %collective-permute-start.60 = (bf16[32,64,256]{2,1,0:T(8,128)(2,1)S(1)}, bf16[32,64,256]{2,1,0:T(8,128)(2,1)}, u32[]{:S(2)}, u32[]{:S(2)}) collective-permute-start(bf16[32,64,256]{2,1,0:T(8,128)(2,1)S(1)} %pick.13.rest_5_), channel_id=1, source_target_pairs={{2,4},{3,5},{4,2},{5,3},{10,12},{11,13},{12,10},{13,11},{18,20},{1... | collective-permute-start | bytes 3145736 | tf_op jit(solution)/shard_map/ppermute | solution.py:29
  223.4 9.4 %collective-permute-start.51 = (bf16[4,192,256]{2,1,0:T(8,128)(2,1)S(1)}, bf16[4,192,256]{2,1,0:T(8,128)(2,1)S(1)}, u32[]{:S(2)}, u32[]{:S(2)}) collective-permute-start(bf16[4,192,256]{2,1,0:T(8,128)(2,1)S(1)} %get-tuple-element.77.rest_0_), channel_id=1, source_target_pairs={{0,1},{1,0},{2,3},{3,2},{4,5},{5,4},{6,7},{7,6},{8,24},{9,25},{10,... | collective-permute-start | bytes 1179656 | tf_op jit(solution)/shard_map/ppermute | solution.py:29
  223.7 10.8 %collective-permute-start.52 = (bf16[4,192,256]{2,1,0:T(8,128)(2,1)S(1)}, bf16[4,192,256]{2,1,0:T(8,128)(2,1)S(1)}, u32[]{:S(2)}, u32[]{:S(2)}) collective-permute-start(bf16[4,192,256]{2,1,0:T(8,128)(2,1)S(1)} %get-tuple-element.77.rest_0_), channel_id=1, source_target_pairs={{0,16},{1,17},{2,18},{3,19},{4,20},{5,21},{6,22},{7,23},{8,9},{9,8... | collective-permute-start | bytes 1179656 | tf_op jit(solution)/shard_map/ppermute | solution.py:29
  234.5 6.9 %collective-permute-start.53 = (bf16[4,192,256]{2,1,0:T(8,128)(2,1)S(1)}, bf16[4,192,256]{2,1,0:T(8,128)(2,1)S(1)}, u32[]{:S(2)}, u32[]{:S(2)}) collective-permute-start(bf16[4,192,256]{2,1,0:T(8,128)(2,1)S(1)} %collective-permute-done.51.rest_1_), channel_id=1, source_target_pairs={{0,16},{1,17},{2,18},{3,19},{4,20},{5,21},{6,22},{7,23},{8,9},{9,8... | collective-permute-start | bytes 1179656 | tf_op jit(solution)/shard_map/ppermute | solution.py:29
  241.4 25.6 %collective-permute-start.62 = (bf16[32,64,256]{2,1,0:T(8,128)(2,1)S(1)}, bf16[32,64,256]{2,1,0:T(8,128)(2,1)}, u32[]{:S(2)}, u32[]{:S(2)}) collective-permute-start(bf16[32,64,256]{2,1,0:T(8,128)(2,1)S(1)} %pick.13.rest_5_), channel_id=1, source_target_pairs={{0,4},{1,5},{6,2},{7,3},{8,12},{9,13},{14,10},{15,11},{16,20},{17,... | collective-permute-start | bytes 3145736 | tf_op jit(solution)/shard_map/ppermute | solution.py:29
  247.5 7.9 %collective-permute-start.54 = (bf16[4,192,256]{2,1,0:T(8,128)(2,1)S(1)}, bf16[4,192,256]{2,1,0:T(8,128)(2,1)S(1)}, u32[]{:S(2)}, u32[]{:S(2)}) collective-permute-start(bf16[4,192,256]{2,1,0:T(8,128)(2,1)S(1)} %project_out.6.rest_0_.rest_4_), channel_id=1, source_target_pairs={{0,1},{1,0},{2,3},{3,2},{4,5},{5,4},{6,7},{7,6},{8,24},{9,25},{10,... | collective-permute-start | bytes 1179656 | tf_op jit(solution)/shard_map/ppermute | solution.py:29
  248.6 10.0 %collective-permute-start.55 = (bf16[4,192,256]{2,1,0:T(8,128)(2,1)S(1)}, bf16[4,192,256]{2,1,0:T(8,128)(2,1)S(1)}, u32[]{:S(2)}, u32[]{:S(2)}) collective-permute-start(bf16[4,192,256]{2,1,0:T(8,128)(2,1)S(1)} %project_out.6.rest_0_.rest_4_), channel_id=1, source_target_pairs={{0,16},{1,17},{2,18},{3,19},{4,20},{5,21},{6,22},{7,23},{8,9},{9,8... | collective-permute-start | bytes 1179656 | tf_op jit(solution)/shard_map/ppermute | solution.py:29
  259.4 6.9 %collective-permute-start.56 = (bf16[4,192,256]{2,1,0:T(8,128)(2,1)S(1)}, bf16[4,192,256]{2,1,0:T(8,128)(2,1)S(1)}, u32[]{:S(2)}, u32[]{:S(2)}) collective-permute-start(bf16[4,192,256]{2,1,0:T(8,128)(2,1)S(1)} %collective-permute-done.54.rest_1_), channel_id=1, source_target_pairs={{0,16},{1,17},{2,18},{3,19},{4,20},{5,21},{6,22},{7,23},{8,9},{9,8... | collective-permute-start | bytes 1179656 | tf_op jit(solution)/shard_map/ppermute | solution.py:29
  261.0 10.2 %collective-permute-start.57 = (bf16[32,64,256]{2,1,0:T(8,128)(2,1)S(1)}, bf16[32,64,256]{2,1,0:T(8,128)(2,1)}, u32[]{:S(2)}, u32[]{:S(2)}) collective-permute-start(bf16[32,64,256]{2,1,0:T(8,128)(2,1)S(1)} %pick.13.rest_5_), channel_id=1, source_target_pairs={{0,8},{1,9},{2,10},{3,11},{4,12},{5,13},{6,14},{7,15},{8,0},{9,1},... | collective-permute-start | bytes 3145736 | tf_op jit(solution)/shard_map/ppermute | solution.py:29
  262.5 8.7 %collective-permute-start.59 = (bf16[32,64,256]{2,1,0:T(8,128)(2,1)S(1)}, bf16[32,64,256]{2,1,0:T(8,128)(2,1)}, u32[]{:S(2)}, u32[]{:S(2)}) collective-permute-start(bf16[32,64,256]{2,1,0:T(8,128)(2,1)S(1)} %collective-permute-done.58.rest_7_), channel_id=1, source_target_pairs={{0,8},{1,9},{2,10},{3,11},{4,12},{5,13},{6,14},{7,15},{8,0},{9,1},... | collective-permute-start | bytes 3145736 | tf_op jit(solution)/shard_map/ppermute | solution.py:29
  262.5 8.7 %collective-permute-start.61 = (bf16[32,64,256]{2,1,0:T(8,128)(2,1)}, bf16[32,64,256]{2,1,0:T(8,128)(2,1)}, u32[]{:S(2)}, u32[]{:S(2)}) collective-permute-start(bf16[32,64,256]{2,1,0:T(8,128)(2,1)} %collective-permute-done.60.rest_9_), channel_id=1, source_target_pairs={{0,8},{1,9},{2,10},{3,11},{4,12},{5,13},{6,14},{7,15},{8,0},{9,1},... | collective-permute-start | bytes 3145736 | tf_op jit(solution)/shard_map/ppermute | solution.py:29
  269.5 24.2 %collective-permute-start.64 = (bf16[192,2048]{1,0:T(8,128)(2,1)}, bf16[192,2048]{1,0:T(8,128)(2,1)S(1)}, u32[]{:S(2)}, u32[]{:S(2)}) collective-permute-start(bf16[192,2048]{1,0:T(8,128)(2,1)} %copy-done.33), channel_id=1, source_target_pairs={{2,10},{3,11},{4,12},{5,13},{10,8},{11,9},{12,14},{13,15},{18,26},... | collective-permute-start | bytes 2359304 | tf_op jit(solution)/shard_map/ppermute | solution.py:29
  281.3 12.3 %collective-permute-start.65 = (bf16[192,2048]{1,0:T(8,128)(2,1)S(1)}, bf16[192,2048]{1,0:T(8,128)(2,1)S(1)}, u32[]{:S(2)}, u32[]{:S(2)}) collective-permute-start(bf16[192,2048]{1,0:T(8,128)(2,1)S(1)} %broadcast_select_fusion), channel_id=1, source_target_pairs={{2,2},{3,3},{4,4},{5,5},{10,0},{11,1},{12,6},{13,7},{18,18},{19,19... | collective-permute-start | bytes 2359304 | tf_op jit(solution)/shard_map/ppermute | solution.py:29
  282.0 8.6 %collective-permute-start.66 = (bf16[4,192,256]{2,1,0:T(8,128)(2,1)S(1)}, bf16[4,192,256]{2,1,0:T(8,128)(2,1)S(1)}, u32[]{:S(2)}, u32[]{:S(2)}) collective-permute-start(bf16[4,192,256]{2,1,0:T(8,128)(2,1)S(1)} %get-tuple-element.87.rest_0_), channel_id=1, source_target_pairs={{0,1},{1,0},{2,3},{3,2},{4,5},{5,4},{6,7},{7,6},{8,24},{9,25},{10,... | collective-permute-start | bytes 1179656 | tf_op jit(solution)/shard_map/ppermute | solution.py:29
  282.6 10.2 %collective-permute-start.67 = (bf16[4,192,256]{2,1,0:T(8,128)(2,1)S(1)}, bf16[4,192,256]{2,1,0:T(8,128)(2,1)S(1)}, u32[]{:S(2)}, u32[]{:S(2)}) collective-permute-start(bf16[4,192,256]{2,1,0:T(8,128)(2,1)S(1)} %get-tuple-element.87.rest_0_), channel_id=1, source_target_pairs={{0,16},{1,17},{2,18},{3,19},{4,20},{5,21},{6,22},{7,23},{8,9},{9,8... | collective-permute-start | bytes 1179656 | tf_op jit(solution)/shard_map/ppermute | solution.py:29
  292.8 6.9 %collective-permute-start.68 = (bf16[4,192,256]{2,1,0:T(8,128)(2,1)S(1)}, bf16[4,192,256]{2,1,0:T(8,128)(2,1)S(1)}, u32[]{:S(2)}, u32[]{:S(2)}) collective-permute-start(bf16[4,192,256]{2,1,0:T(8,128)(2,1)S(1)} %collective-permute-done.66.rest_1_), channel_id=1, source_target_pairs={{0,16},{1,17},{2,18},{3,19},{4,20},{5,21},{6,22},{7,23},{8,9},{9,8... | collective-permute-start | bytes 1179656 | tf_op jit(solution)/shard_map/ppermute | solution.py:29
  302.4 10.0 %collective-permute-start.69 = (bf16[4,192,256]{2,1,0:T(8,128)(2,1)S(1)}, bf16[4,192,256]{2,1,0:T(8,128)(2,1)S(1)}, u32[]{:S(2)}, u32[]{:S(2)}) collective-permute-start(bf16[4,192,256]{2,1,0:T(8,128)(2,1)S(1)} %project_out.7), channel_id=1, source_target_pairs={{2,26},{3,27},{4,28},{5,29},{10,24},{11,25},{12,30},{13,31}} | collective-permute-start | bytes 1179656 | tf_op jit(solution)/shard_map/ppermute | solution.py:29
  303.7 10.5 %collective-permute-start.70 = (bf16[4,192,256]{2,1,0:T(8,128)(2,1)S(1)}, bf16[4,192,256]{2,1,0:T(8,128)(2,1)S(1)}, u32[]{:S(2)}, u32[]{:S(2)}) collective-permute-start(bf16[4,192,256]{2,1,0:T(8,128)(2,1)S(1)} %project_out.7), channel_id=1, source_target_pairs={{18,26},{19,27},{20,28},{21,29},{26,24},{27,25},{28,30},{29,31}} | collective-permute-start | bytes 1179656 | tf_op jit(solution)/shard_map/ppermute | solution.py:29
  (50 other events, 410.7 us)

commit v4 on v3

--- a/solution.py
+++ b/solution.py
@@ -55,9 +55,14 @@
     pieces, gain_ref, parts = rest[:4], rest[4], rest[5 : 5 + n_parts]
     outs, (weights, normed, proj, sems) = rest[5 + n_parts : -4], rest[-4:]
     out_ref = outs[0]
-    copies = weight_copies(parts, 0, weights, sems, pos_ref)
-    for copy in copies:
-        copy.start()
+    each = weights.shape[1] // 3
+    copies = [
+        weight_copies(parts, kind * each, weights.at[:, pl.ds(kind * each, each)], sems.at[kind], pos_ref)
+        for kind in range(3)
+    ]
+    for of_kind in copies:
+        for copy in of_kind:
+            copy.start()
     cols, (per_piece, rows, width) = out_ref.shape[0] // 2, pieces[0].shape
     blocks = 4 * per_piece
     row = me_ref[0] ^ section
@@ -85,13 +90,13 @@
                 place = ((keeper_y ^ dy) * per_piece + (odd ^ (t // cols)) * cols + t % cols) * width
                 value = jnp.where(odd == 1, pieces[dy][t], pieces[2 * dy][t])
                 outs[1][:, pl.ds(pl.multiple_of(place, width), width)] = value
-    for copy in copies:
-        copy.wait()
     count = weights.shape[1]
     per = count // (3 * cols)
     wide = blocks // 2
-    for core in range(2):
-        for kind in range(3):
+    for kind in range(3):
+        for copy in copies[kind]:
+            copy.wait()
+        for core in range(2):
             for c in range(cols):
                 total = None
                 for i in range(per):
@@ -258,7 +263,7 @@
             pltpu.VMEM((2, count, depth, width), jnp.bfloat16),
             pltpu.VMEM((4 * cols, rows, width), jnp.bfloat16),
             pltpu.VMEM((3, cols, rows, width), jnp.bfloat16),
-            pltpu.SemaphoreType.DMA((len(parts),)),
+            pltpu.SemaphoreType.DMA((3, len(parts))),
         ],
         compiler_params=pltpu.CompilerParams(vmem_limit_bytes=VMEM_LIMIT),
         cost_estimate=hint(ATTEND_US),

time: 319 us -> 317 us (level)
  transfers between devices with their start and end apart: 71 -> 71, of which waited for: 35 -> 35; matrix products, arithmetic and copies ran while one was open for 1% -> 1% of each run, Pallas kernels for 12% -> 11%
where the time goes in v4:
time: 317 us; the launch traced here: 316 us
  waiting for transfers between devices  140 us (44%)
  starting transfers between devices  107 us (34%)
  Pallas kernels  45.5 us (14%)
  local copies, waits for them, and re-layouts  19.2 us (6%)
    ppermute x71, waiting for transfers between devices, hop(): return lax.ppermute(value, AXES, pairs)  140 us
    ppermute x71, starting transfers between devices, hop(): return lax.ppermute(value, AXES, pairs)  107 us
    pallas_call x4, Pallas kernels, attend(): pl.pallas_call(functools.partial(attend_kernel, section, len(parts), rows...  20.2 us
    unnamed x86, local copies, waits for them, and re-layouts  16.5 us
    pallas_call x4, Pallas kernels, project_out(): pl.pallas_call(functools.partial(output_kernel, section, first, len(parts...  10 us
    pallas_call x7, Pallas kernels, pick(): pl.pallas_call(functools.partial(pick_kernel, choice, tuple((len(candidat...  8.61 us
  transfers between devices with their start and end apart: 71, of which 35 were waited for; matrix products, arithmetic and copies ran while one was open for 1% of the time, Pallas kernels for 11%

profile of v4, /device:TPU:5, one launch (start us, length us, event | category | flops | bytes accessed | tf_op | source)
XLA Modules:
  0.0 315.8 jit_solution(8782766220397198467)
XLA Ops:
  0.6 5.1 %cut.1 = (bf16[28,64,256]{2,1,0:T(8,128)(2,1)}, bf16[28,64,256]{2,1,0:T(8,128)(2,1)}, bf16[28,64,256]{2,1,0:T(8,128)(2,1)}, bf16[28,64,256]{2,1,0:T(8,128)(2,1)}) custom-call(s32[2]{0:T(128)} %pad_add_fusion.me_ref, bf16[1,4,8,64,256]{4,3,2,1,0:T(8,128)(2,1)} %rest_0_.1, bf16[1,4,8,64,256]{4,3,2,1,0:T(8,128)(2,1)} %rest_1_.1, ...), custom_call_target="tpu_custom_call" | custom-call | flops 1000000000 | tf_op jit(solution)/shard_map/cut/pallas_call | solution.py:298
  9.3 3.2 %collective-permute-start.5 = (bf16[4,192,256]{2,1,0:T(8,128)(2,1)S(1)}, bf16[4,192,256]{2,1,0:T(8,128)(2,1)S(1)}, u32[]{:S(2)}, u32[]{:S(2)}) collective-permute-start(bf16[4,192,256]{2,1,0:T(8,128)(2,1)S(1)} %get-tuple-element.50.rest_0_), channel_id=1, source_target_pairs={{8,10},{9,11},{14,12},{15,13},{24,26},{25,27},{30,28},{31,29}} | collective-permute-start | bytes 1179656 | tf_op jit(solution)/shard_map/ppermute | solution.py:29
  12.6 2.2 collective-permute-start.6
  14.8 1.9 collective-permute-start.9
  16.7 3.0 collective-permute-start.4
  22.6 2.9 collective-permute-start.10
  26.8 10.2 %collective-permute-done.10.rest_3_ = bf16[4,64,256]{2,1,0:T(8,128)(2,1)S(1)} collective-permute-done((bf16[4,64,256]{2,1,0:T(8,128)(2,1)S(1)}, bf16[4,64,256]{2,1,0:T(8,128)(2,1)S(1)}, u32[]{:S(2)}, u32[]{:S(2)}) %collective-permute-start.10) | collective-permute-done | bytes 131104 | tf_op jit(solution)/shard_map/ppermute | solution.py:29
  37.9 2.0 collective-permute-start.11
  40.1 1.8 pick.8.rest_5_
  41.9 2.4 collective-permute-start.17
  44.3 1.6 collective-permute-start.19
  48.5 2.2 collective-permute-start.1
  51.4 1.9 collective-permute-start.2
  54.9 1.7 pick.10
  56.6 3.4 %collective-permute-done.13.rest_3_ = bf16[4,192,256]{2,1,0:T(8,128)(2,1)S(1)} collective-permute-done((bf16[4,192,256]{2,1,0:T(8,128)(2,1)S(1)}, bf16[4,192,256]{2,1,0:T(8,128)(2,1)S(1)}, u32[]{:S(2)}, u32[]{:S(2)}) %collective-permute-start.13) | collective-permute-done | bytes 393248 | tf_op jit(solution)/shard_map/ppermute | solution.py:29
  60.7 4.5 %collective-permute-done.17.rest_7_ = bf16[32,64,256]{2,1,0:T(8,128)(2,1)} collective-permute-done((bf16[32,64,256]{2,1,0:T(8,128)(2,1)S(1)}, bf16[32,64,256]{2,1,0:T(8,128)(2,1)}, u32[]{:S(2)}, u32[]{:S(2)}) %collective-permute-start.17) | collective-permute-done | bytes 1048608 | tf_op jit(solution)/shard_map/ppermute | solution.py:29
  65.2 7.5 %collective-permute-start.21 = (bf16[32,64,256]{2,1,0:T(8,128)(2,1)S(1)}, bf16[32,64,256]{2,1,0:T(8,128)(2,1)}, u32[]{:S(2)}, u32[]{:S(2)}) collective-permute-start(bf16[32,64,256]{2,1,0:T(8,128)(2,1)S(1)} %pick.8.rest_5_), channel_id=1, source_target_pairs={{0,4},{1,5},{6,2},{7,3},{8,12},{9,13},{14,10},{15,11},{16,20},{17,... | collective-permute-start | bytes 3145736 | tf_op jit(solution)/shard_map/ppermute | solution.py:29
  72.7 1.7 pick.9
  75.8 2.5 collective-permute-start.16
  78.8 13.9 %collective-permute-done.21.rest_11_ = bf16[32,64,256]{2,1,0:T(8,128)(2,1)} collective-permute-done((bf16[32,64,256]{2,1,0:T(8,128)(2,1)S(1)}, bf16[32,64,256]{2,1,0:T(8,128)(2,1)}, u32[]{:S(2)}, u32[]{:S(2)}) %collective-permute-start.21) | collective-permute-done | bytes 1048608 | tf_op jit(solution)/shard_map/ppermute | solution.py:29
  92.7 2.4 collective-permute-start.22
  96.1 5.1 %collective-permute-start.32 = (bf16[32,64,256]{2,1,0:T(8,128)(2,1)S(1)}, bf16[32,64,256]{2,1,0:T(8,128)(2,1)}, u32[]{:S(2)}, u32[]{:S(2)}) collective-permute-start(bf16[32,64,256]{2,1,0:T(8,128)(2,1)S(1)} %pick.11.rest_5_), channel_id=1, source_target_pairs={{0,2},{1,3},{6,4},{7,5},{8,10},{9,11},{14,12},{15,13},{16,18},{17,... | collective-permute-start | bytes 3145736 | tf_op jit(solution)/shard_map/ppermute | solution.py:29
  102.1 1.7 collective-permute-start.34
  111.0 5.1 %attend.4.rest_0_ = bf16[4,192,256]{2,1,0:T(8,128)(2,1)S(1)} custom-call(s32[2]{0:T(128)S(1)} %copy-done.31, f32[4,128]{1,0:T(4,128)S(1)} %slice.20.list_ref, s32[4]{0:T(128)S(1)} %broadcast_select_fusion.3.pos_ref, s32[3,4,4]{2,1,0:T(4,128)S(1)} %broadcast_select_fusion.2.mask_ref, bf16[4,192,256]{2,1,0:T(8,128)(2,1)S(1)} %copy-done.15, ...), custom_call_target="tpu_custom_call" | custom-call | flops 1000000000 | tf_op jit(solution)/shard_map/attend/pallas_call | solution.py:257
  117.1 8.3 %collective-permute-done.23.rest_1_ = bf16[4,192,256]{2,1,0:T(8,128)(2,1)S(1)} collective-permute-done((bf16[4,192,256]{2,1,0:T(8,128)(2,1)S(1)}, bf16[4,192,256]{2,1,0:T(8,128)(2,1)S(1)}, u32[]{:S(2)}, u32[]{:S(2)}) %collective-permute-start.23) | collective-permute-done | bytes 393248 | tf_op jit(solution)/shard_map/ppermute | solution.py:29
  128.6 1.9 collective-permute-start.36
  131.2 2.5 collective-permute-done.3.other_ref
  133.7 2.7 project_out.4.rest_0_.rest_4_
  137.4 6.8 %collective-permute-done.26.rest_1_ = bf16[4,192,256]{2,1,0:T(8,128)(2,1)S(1)} collective-permute-done((bf16[4,192,256]{2,1,0:T(8,128)(2,1)S(1)}, bf16[4,192,256]{2,1,0:T(8,128)(2,1)S(1)}, u32[]{:S(2)}, u32[]{:S(2)}) %collective-permute-start.26) | collective-permute-done | bytes 393248 | tf_op jit(solution)/shard_map/ppermute | solution.py:29
  146.3 3.5 %collective-permute-start.31 = (bf16[32,64,256]{2,1,0:T(8,128)(2,1)S(1)}, bf16[32,64,256]{2,1,0:T(8,128)(2,1)S(1)}, u32[]{:S(2)}, u32[]{:S(2)}) collective-permute-start(bf16[32,64,256]{2,1,0:T(8,128)(2,1)S(1)} %pick.11.rest_5_), channel_id=1, source_target_pairs={{0,8},{1,9},{2,10},{3,11},{4,12},{5,13},{6,14},{7,15},{8,0},{9,1},... | collective-permute-start | bytes 3145736 | tf_op jit(solution)/shard_map/ppermute | solution.py:29
  150.3 2.0 collective-permute-done.36.rest_11_
  152.4 3.5 %collective-permute-start.37 = (bf16[32,64,256]{2,1,0:T(8,128)(2,1)S(1)}, bf16[32,64,256]{2,1,0:T(8,128)(2,1)S(1)}, u32[]{:S(2)}, u32[]{:S(2)}) collective-permute-start(bf16[32,64,256]{2,1,0:T(8,128)(2,1)S(1)} %collective-permute-done.36.rest_11_), channel_id=1, source_target_pairs={{0,8},{1,9},{2,10},{3,11},{4,12},{5,13},{6,14},{7,15},{8,0},{9,1},... | collective-permute-start | bytes 3145736 | tf_op jit(solution)/shard_map/ppermute | solution.py:29
  155.9 3.1 collective-permute-start.45
  160.0 4.9 %attend.5 = (bf16[4,192,256]{2,1,0:T(8,128)(2,1)S(1)}, bf16[192,2048]{1,0:T(8,128)(2,1)S(1)}) custom-call(s32[2]{0:T(128)S(1)} %copy-done.31, f32[4,128]{1,0:T(4,128)S(1)} %slice.20.list_ref, s32[4]{0:T(128)S(1)} %broadcast_select_fusion.3.pos_ref, s32[3,4,4]{2,1,0:T(4,128)S(1)} %broadcast_select_fusion.2.mask_ref, ...), custom_call_target="tpu_custom_call" | custom-call | flops 1000000000 | tf_op jit(solution)/shard_map/attend/pallas_call | solution.py:257
  166.1 8.3 %collective-permute-done.38.rest_1_ = bf16[4,192,256]{2,1,0:T(8,128)(2,1)S(1)} collective-permute-done((bf16[4,192,256]{2,1,0:T(8,128)(2,1)S(1)}, bf16[4,192,256]{2,1,0:T(8,128)(2,1)S(1)}, u32[]{:S(2)}, u32[]{:S(2)}) %collective-permute-start.38) | collective-permute-done | bytes 393248 | tf_op jit(solution)/shard_map/ppermute | solution.py:29
  174.3 1.7 collective-permute-done.39.rest_2_
  178.0 3.5 %collective-permute-done.45.rest_7_ = bf16[32,64,256]{2,1,0:T(8,128)(2,1)S(1)} collective-permute-done((bf16[32,64,256]{2,1,0:T(8,128)(2,1)S(1)}, bf16[32,64,256]{2,1,0:T(8,128)(2,1)S(1)}, u32[]{:S(2)}, u32[]{:S(2)}) %collective-permute-start.45) | collective-permute-done | bytes 1048608 | tf_op jit(solution)/shard_map/ppermute | solution.py:29
  183.0 3.9 %collective-permute-start.49 = (bf16[32,64,256]{2,1,0:T(8,128)(2,1)S(1)}, bf16[32,64,256]{2,1,0:T(8,128)(2,1)S(1)}, u32[]{:S(2)}, u32[]{:S(2)}) collective-permute-start(bf16[32,64,256]{2,1,0:T(8,128)(2,1)S(1)} %pick.12.rest_5_), channel_id=1, source_target_pairs={{0,4},{1,5},{6,2},{7,3},{8,12},{9,13},{14,10},{15,11},{16,20},{17,... | collective-permute-start | bytes 3145736 | tf_op jit(solution)/shard_map/ppermute | solution.py:29
  186.9 2.4 project_out.5.rest_0_.rest_4_
  191.0 6.2 %collective-permute-done.41.rest_1_ = bf16[4,192,256]{2,1,0:T(8,128)(2,1)S(1)} collective-permute-done((bf16[4,192,256]{2,1,0:T(8,128)(2,1)S(1)}, bf16[4,192,256]{2,1,0:T(8,128)(2,1)S(1)}, u32[]{:S(2)}, u32[]{:S(2)}) %collective-permute-start.41) | collective-permute-done | bytes 393248 | tf_op jit(solution)/shard_map/ppermute | solution.py:29
  197.2 2.9 collective-permute-done.42.rest_2_
  200.9 1.7 collective-permute-start.44
  203.1 3.8 %collective-permute-done.43.rest_3_ = bf16[4,192,256]{2,1,0:T(8,128)(2,1)S(1)} collective-permute-done((bf16[4,192,256]{2,1,0:T(8,128)(2,1)S(1)}, bf16[4,192,256]{2,1,0:T(8,128)(2,1)S(1)}, u32[]{:S(2)}, u32[]{:S(2)}) %collective-permute-start.43) | collective-permute-done | bytes 393248 | tf_op jit(solution)/shard_map/ppermute | solution.py:29
  207.8 2.3 collective-permute-start.50
  210.1 5.2 %collective-permute-start.58 = (bf16[32,64,256]{2,1,0:T(8,128)(2,1)S(1)}, bf16[32,64,256]{2,1,0:T(8,128)(2,1)S(1)}, u32[]{:S(2)}, u32[]{:S(2)}) collective-permute-start(bf16[32,64,256]{2,1,0:T(8,128)(2,1)S(1)} %pick.13.rest_5_), channel_id=1, source_target_pairs={{0,2},{1,3},{6,4},{7,5},{8,10},{9,11},{14,12},{15,13},{16,18},{17,... | collective-permute-start | bytes 3145736 | tf_op jit(solution)/shard_map/ppermute | solution.py:29
  215.3 1.6 collective-permute-start.60
  217.0 5.0 %attend.6 = (bf16[4,192,256]{2,1,0:T(8,128)(2,1)S(1)}, bf16[192,2048]{1,0:T(8,128)(2,1)S(1)}) custom-call(s32[2]{0:T(128)S(1)} %copy-done.31, f32[4,128]{1,0:T(4,128)S(1)} %slice.20.list_ref, s32[4]{0:T(128)S(1)} %broadcast_select_fusion.3.pos_ref, s32[3,4,4]{2,1,0:T(4,128)S(1)} %broadcast_select_fusion.2.mask_ref, ...), custom_call_target="tpu_custom_call" | custom-call | flops 1000000000 | tf_op jit(solution)/shard_map/attend/pallas_call | solution.py:257
  224.1 8.2 %collective-permute-done.51.rest_1_ = bf16[4,192,256]{2,1,0:T(8,128)(2,1)S(1)} collective-permute-done((bf16[4,192,256]{2,1,0:T(8,128)(2,1)S(1)}, bf16[4,192,256]{2,1,0:T(8,128)(2,1)S(1)}, u32[]{:S(2)}, u32[]{:S(2)}) %collective-permute-start.51) | collective-permute-done | bytes 393248 | tf_op jit(solution)/shard_map/ppermute | solution.py:29
  232.3 1.7 collective-permute-done.52.rest_2_
  234.9 2.9 collective-permute-done.58.rest_7_
  237.8 3.1 collective-permute-done.53.rest_3_
  241.0 3.8 %collective-permute-start.62 = (bf16[32,64,256]{2,1,0:T(8,128)(2,1)S(1)}, bf16[32,64,256]{2,1,0:T(8,128)(2,1)}, u32[]{:S(2)}, u32[]{:S(2)}) collective-permute-start(bf16[32,64,256]{2,1,0:T(8,128)(2,1)S(1)} %pick.13.rest_5_), channel_id=1, source_target_pairs={{0,4},{1,5},{6,2},{7,3},{8,12},{9,13},{14,10},{15,11},{16,20},{17,... | collective-permute-start | bytes 3145736 | tf_op jit(solution)/shard_map/ppermute | solution.py:29
  244.7 2.2 project_out.6.rest_0_.rest_4_
  248.9 5.8 %collective-permute-done.54.rest_1_ = bf16[4,192,256]{2,1,0:T(8,128)(2,1)S(1)} collective-permute-done((bf16[4,192,256]{2,1,0:T(8,128)(2,1)S(1)}, bf16[4,192,256]{2,1,0:T(8,128)(2,1)S(1)}, u32[]{:S(2)}, u32[]{:S(2)}) %collective-permute-start.54) | collective-permute-done | bytes 393248 | tf_op jit(solution)/shard_map/ppermute | solution.py:29
  254.8 3.3 %collective-permute-done.55.rest_2_ = bf16[4,192,256]{2,1,0:T(8,128)(2,1)S(1)} collective-permute-done((bf16[4,192,256]{2,1,0:T(8,128)(2,1)S(1)}, bf16[4,192,256]{2,1,0:T(8,128)(2,1)S(1)}, u32[]{:S(2)}, u32[]{:S(2)}) %collective-permute-start.55) | collective-permute-done | bytes 393248 | tf_op jit(solution)/shard_map/ppermute | solution.py:29
  262.4 3.4 %collective-permute-done.56.rest_3_ = bf16[4,192,256]{2,1,0:T(8,128)(2,1)S(1)} collective-permute-done((bf16[4,192,256]{2,1,0:T(8,128)(2,1)S(1)}, bf16[4,192,256]{2,1,0:T(8,128)(2,1)S(1)}, u32[]{:S(2)}, u32[]{:S(2)}) %collective-permute-start.56) | collective-permute-done | bytes 393248 | tf_op jit(solution)/shard_map/ppermute | solution.py:29
  266.6 2.4 collective-permute-start.63
  274.6 5.1 %attend.7 = (bf16[4,192,256]{2,1,0:T(8,128)(2,1)S(1)}, bf16[192,2048]{1,0:T(8,128)(2,1)S(1)}) custom-call(s32[2]{0:T(128)S(1)} %copy-done.31, f32[4,128]{1,0:T(4,128)S(1)} %slice.20.list_ref, s32[4]{0:T(128)S(1)} %broadcast_select_fusion.3.pos_ref, s32[3,4,4]{2,1,0:T(4,128)S(1)} %broadcast_select_fusion.2.mask_ref, ...), custom_call_target="tpu_custom_call" | custom-call | flops 1000000000 | tf_op jit(solution)/shard_map/attend/pallas_call | solution.py:257
  281.9 7.2 %collective-permute-done.66.rest_1_ = bf16[4,192,256]{2,1,0:T(8,128)(2,1)S(1)} collective-permute-done((bf16[4,192,256]{2,1,0:T(8,128)(2,1)S(1)}, bf16[4,192,256]{2,1,0:T(8,128)(2,1)S(1)}, u32[]{:S(2)}, u32[]{:S(2)}) %collective-permute-start.66) | collective-permute-done | bytes 393248 | tf_op jit(solution)/shard_map/ppermute | solution.py:29
  289.2 1.9 collective-permute-done.67.rest_2_
  293.1 4.9 %collective-permute-done.68.rest_3_ = bf16[4,192,256]{2,1,0:T(8,128)(2,1)S(1)} collective-permute-done((bf16[4,192,256]{2,1,0:T(8,128)(2,1)S(1)}, bf16[4,192,256]{2,1,0:T(8,128)(2,1)S(1)}, u32[]{:S(2)}, u32[]{:S(2)}) %collective-permute-start.68) | collective-permute-done | bytes 393248 | tf_op jit(solution)/shard_map/ppermute | solution.py:29
  298.1 2.7 project_out.7
  303.4 7.4 %collective-permute-done.69 = bf16[4,192,256]{2,1,0:T(8,128)(2,1)S(1)} collective-permute-done((bf16[4,192,256]{2,1,0:T(8,128)(2,1)S(1)}, bf16[4,192,256]{2,1,0:T(8,128)(2,1)S(1)}, u32[]{:S(2)}, u32[]{:S(2)}) %collective-permute-start.69) | collective-permute-done | bytes 393248 | tf_op jit(solution)/shard_map/ppermute | solution.py:29
  310.8 1.9 collective-permute-done.70
  (194 shorter events, 69.0 us)
Async XLA Ops:
  8.1 13.2 %collective-permute-start.7 = (bf16[16,64,256]{2,1,0:T(8,128)(2,1)S(1)}, bf16[16,64,256]{2,1,0:T(8,128)(2,1)}, u32[]{:S(2)}, u32[]{:S(2)}) collective-permute-start(bf16[16,64,256]{2,1,0:T(8,128)(2,1)S(1)} %get-tuple-element.51), channel_id=1, source_target_pairs={{0,1},{1,0},{2,3},{3,2},{4,5},{5,4},{6,7},{7,6},{8,9},{9,8},{10,11... | collective-permute-start | bytes 1572872 | tf_op jit(solution)/shard_map/ppermute | solution.py:29
  9.3 11.1 %collective-permute-start.5 = (bf16[4,192,256]{2,1,0:T(8,128)(2,1)S(1)}, bf16[4,192,256]{2,1,0:T(8,128)(2,1)S(1)}, u32[]{:S(2)}, u32[]{:S(2)}) collective-permute-start(bf16[4,192,256]{2,1,0:T(8,128)(2,1)S(1)} %get-tuple-element.50.rest_0_), channel_id=1, source_target_pairs={{8,10},{9,11},{14,12},{15,13},{24,26},{25,27},{30,28},{31,29}} | collective-permute-start | bytes 1179656 | tf_op jit(solution)/shard_map/ppermute | solution.py:29
  12.6 25.3 %collective-permute-start.6 = (bf16[28,64,256]{2,1,0:T(8,128)(2,1)}, bf16[28,64,256]{2,1,0:T(8,128)(2,1)S(1)}, u32[]{:S(2)}, u32[]{:S(2)}) collective-permute-start(bf16[28,64,256]{2,1,0:T(8,128)(2,1)} %get-tuple-element.64.rest_0_), channel_id=1, source_target_pairs={{0,16},{1,17},{2,18},{3,19},{4,20},{5,21},{6,22},{7,23},{24,8},{25... | collective-permute-start | bytes 2752520 | tf_op jit(solution)/shard_map/ppermute | solution.py:29
  14.8 23.1 %collective-permute-start.9 = (bf16[28,64,256]{2,1,0:T(8,128)(2,1)}, bf16[28,64,256]{2,1,0:T(8,128)(2,1)}, u32[]{:S(2)}, u32[]{:S(2)}) collective-permute-start(bf16[28,64,256]{2,1,0:T(8,128)(2,1)} %get-tuple-element.66.rest_0_), channel_id=1, source_target_pairs={{0,24},{1,25},{2,26},{3,27},{4,28},{5,29},{6,30},{7,31},{24,0},{25... | collective-permute-start | bytes 2752520 | tf_op jit(solution)/shard_map/ppermute | solution.py:29
  20.5 19.6 %collective-permute-start.14 = (bf16[28,64,256]{2,1,0:T(8,128)(2,1)}, bf16[28,64,256]{2,1,0:T(8,128)(2,1)S(1)}, u32[]{:S(2)}, u32[]{:S(2)}) collective-permute-start(bf16[28,64,256]{2,1,0:T(8,128)(2,1)} %get-tuple-element.57), channel_id=1, source_target_pairs={{0,8},{1,9},{2,10},{3,11},{4,12},{5,13},{6,14},{7,15},{8,0},{9,1},... | collective-permute-start | bytes 2752520 | tf_op jit(solution)/shard_map/ppermute | solution.py:29
  22.6 14.5 %collective-permute-start.10 = (bf16[4,64,256]{2,1,0:T(8,128)(2,1)S(1)}, bf16[4,64,256]{2,1,0:T(8,128)(2,1)S(1)}, u32[]{:S(2)}, u32[]{:S(2)}) collective-permute-start(bf16[4,64,256]{2,1,0:T(8,128)(2,1)S(1)} %get-tuple-element.54.rest_1_), channel_id=1, source_target_pairs={{0,24},{1,25},{2,26},{3,27},{4,28},{5,29},{6,30},{7,31},{24,0},{25... | collective-permute-start | bytes 393224 | tf_op jit(solution)/shard_map/ppermute | solution.py:29
  25.5 12.4 %collective-permute-start.8 = (bf16[4,64,256]{2,1,0:T(8,128)(2,1)S(1)}, bf16[4,64,256]{2,1,0:T(8,128)(2,1)S(1)}, u32[]{:S(2)}, u32[]{:S(2)}) collective-permute-start(bf16[4,64,256]{2,1,0:T(8,128)(2,1)S(1)} %get-tuple-element.52.rest_1_), channel_id=1, source_target_pairs={{0,16},{1,17},{2,18},{3,19},{4,20},{5,21},{6,22},{7,23},{24,8},{25... | collective-permute-start | bytes 393224 | tf_op jit(solution)/shard_map/ppermute | solution.py:29
  37.9 10.6 %collective-permute-start.11 = (bf16[4,192,256]{2,1,0:T(8,128)(2,1)S(1)}, bf16[4,192,256]{2,1,0:T(8,128)(2,1)S(1)}, u32[]{:S(2)}, u32[]{:S(2)}) collective-permute-start(bf16[4,192,256]{2,1,0:T(8,128)(2,1)S(1)} %pick.7.rest_0_.rest_4_), channel_id=1, source_target_pairs={{0,1},{1,0},{2,3},{3,2},{4,5},{5,4},{6,7},{7,6},{8,24},{9,25},{10,... | collective-permute-start | bytes 1179656 | tf_op jit(solution)/shard_map/ppermute | solution.py:29
  39.9 10.8 %collective-permute-start.12 = (bf16[4,192,256]{2,1,0:T(8,128)(2,1)S(1)}, bf16[4,192,256]{2,1,0:T(8,128)(2,1)S(1)}, u32[]{:S(2)}, u32[]{:S(2)}) collective-permute-start(bf16[4,192,256]{2,1,0:T(8,128)(2,1)S(1)} %pick.7.rest_0_.rest_4_), channel_id=1, source_target_pairs={{0,16},{1,17},{2,18},{3,19},{4,20},{5,21},{6,22},{7,23},{8,9},{9,8... | collective-permute-start | bytes 1179656 | tf_op jit(solution)/shard_map/ppermute | solution.py:29
  41.9 23.3 %collective-permute-start.17 = (bf16[32,64,256]{2,1,0:T(8,128)(2,1)S(1)}, bf16[32,64,256]{2,1,0:T(8,128)(2,1)}, u32[]{:S(2)}, u32[]{:S(2)}) collective-permute-start(bf16[32,64,256]{2,1,0:T(8,128)(2,1)S(1)} %pick.8.rest_5_), channel_id=1, source_target_pairs={{0,2},{1,3},{6,4},{7,5},{8,10},{9,11},{14,12},{15,13},{16,18},{17,... | collective-permute-start | bytes 3145736 | tf_op jit(solution)/shard_map/ppermute | solution.py:29
  44.3 20.9 %collective-permute-start.19 = (bf16[32,64,256]{2,1,0:T(8,128)(2,1)S(1)}, bf16[32,64,256]{2,1,0:T(8,128)(2,1)}, u32[]{:S(2)}, u32[]{:S(2)}) collective-permute-start(bf16[32,64,256]{2,1,0:T(8,128)(2,1)S(1)} %pick.8.rest_5_), channel_id=1, source_target_pairs={{2,4},{3,5},{4,2},{5,3},{10,12},{11,13},{12,10},{13,11},{18,20},{1... | collective-permute-start | bytes 3145736 | tf_op jit(solution)/shard_map/ppermute | solution.py:29
  46.0 7.4 %collective-permute-start = (f32[1,4224]{1,0:T(1,128)S(1)}, f32[1,4224]{1,0:T(1,128)S(1)}, u32[]{:S(2)}, u32[]{:S(2)}) collective-permute-start(f32[1,4224]{1,0:T(1,128)S(1)} %get-tuple-element.49), channel_id=1, source_target_pairs={{0,8},{1,9},{2,10},{3,11},{4,12},{5,13},{6,14},{7,15},{8,0},{9,1},... | collective-permute-start | bytes 50696 | tf_op jit(solution)/shard_map/ppermute | solution.py:29
  60.0 18.4 %collective-permute-start.30 = (bf16[32,64,256]{2,1,0:T(8,128)(2,1)S(1)}, bf16[32,64,256]{2,1,0:T(8,128)(2,1)S(1)}, u32[]{:S(2)}, u32[]{:S(2)}) collective-permute-start(bf16[32,64,256]{2,1,0:T(8,128)(2,1)S(1)} %pick.10), channel_id=1, source_target_pairs={{8,16},{9,17},{10,18},{11,19},{12,20},{13,21},{14,22},{15,23},{16,... | collective-permute-start | bytes 3145736 | tf_op jit(solution)/shard_map/ppermute | solution.py:29
  65.2 27.5 %collective-permute-start.21 = (bf16[32,64,256]{2,1,0:T(8,128)(2,1)S(1)}, bf16[32,64,256]{2,1,0:T(8,128)(2,1)}, u32[]{:S(2)}, u32[]{:S(2)}) collective-permute-start(bf16[32,64,256]{2,1,0:T(8,128)(2,1)S(1)} %pick.8.rest_5_), channel_id=1, source_target_pairs={{0,4},{1,5},{6,2},{7,3},{8,12},{9,13},{14,10},{15,11},{16,20},{17,... | collective-permute-start | bytes 3145736 | tf_op jit(solution)/shard_map/ppermute | solution.py:29
  74.5 20.6 %collective-permute-start.29 = (bf16[32,64,256]{2,1,0:T(8,128)(2,1)S(1)}, bf16[32,64,256]{2,1,0:T(8,128)(2,1)S(1)}, u32[]{:S(2)}, u32[]{:S(2)}) collective-permute-start(bf16[32,64,256]{2,1,0:T(8,128)(2,1)S(1)} %pick.9), channel_id=1, source_target_pairs={{8,24},{9,25},{10,26},{11,27},{12,28},{13,29},{14,30},{15,31},{16,... | collective-permute-start | bytes 3145736 | tf_op jit(solution)/shard_map/ppermute | solution.py:29
  75.8 25.4 %collective-permute-start.16 = (bf16[32,64,256]{2,1,0:T(8,128)(2,1)S(1)}, bf16[32,64,256]{2,1,0:T(8,128)(2,1)S(1)}, u32[]{:S(2)}, u32[]{:S(2)}) collective-permute-start(bf16[32,64,256]{2,1,0:T(8,128)(2,1)S(1)} %pick.8.rest_5_), channel_id=1, source_target_pairs={{0,8},{1,9},{2,10},{3,11},{4,12},{5,13},{6,14},{7,15},{8,0},{9,1},... | collective-permute-start | bytes 3145736 | tf_op jit(solution)/shard_map/ppermute | solution.py:29
  78.3 26.2 %collective-permute-start.18 = (bf16[32,64,256]{2,1,0:T(8,128)(2,1)}, bf16[32,64,256]{2,1,0:T(8,128)(2,1)}, u32[]{:S(2)}, u32[]{:S(2)}) collective-permute-start(bf16[32,64,256]{2,1,0:T(8,128)(2,1)} %collective-permute-done.17.rest_7_), channel_id=1, source_target_pairs={{0,8},{1,9},{2,10},{3,11},{4,12},{5,13},{6,14},{7,15},{8,0},{9,1},... | collective-permute-start | bytes 3145736 | tf_op jit(solution)/shard_map/ppermute | solution.py:29
  78.4 26.1 %collective-permute-start.20 = (bf16[32,64,256]{2,1,0:T(8,128)(2,1)}, bf16[32,64,256]{2,1,0:T(8,128)(2,1)}, u32[]{:S(2)}, u32[]{:S(2)}) collective-permute-start(bf16[32,64,256]{2,1,0:T(8,128)(2,1)} %collective-permute-done.19.rest_9_), channel_id=1, source_target_pairs={{0,8},{1,9},{2,10},{3,11},{4,12},{5,13},{6,14},{7,15},{8,0},{9,1},... | collective-permute-start | bytes 3145736 | tf_op jit(solution)/shard_map/ppermute | solution.py:29
  92.7 11.8 %collective-permute-start.22 = (bf16[32,64,256]{2,1,0:T(8,128)(2,1)}, bf16[32,64,256]{2,1,0:T(8,128)(2,1)}, u32[]{:S(2)}, u32[]{:S(2)}) collective-permute-start(bf16[32,64,256]{2,1,0:T(8,128)(2,1)} %collective-permute-done.21.rest_11_), channel_id=1, source_target_pairs={{0,8},{1,9},{2,10},{3,11},{4,12},{5,13},{6,14},{7,15},{8,0},{9,1},... | collective-permute-start | bytes 3145736 | tf_op jit(solution)/shard_map/ppermute | solution.py:29
  96.1 32.5 %collective-permute-start.32 = (bf16[32,64,256]{2,1,0:T(8,128)(2,1)S(1)}, bf16[32,64,256]{2,1,0:T(8,128)(2,1)}, u32[]{:S(2)}, u32[]{:S(2)}) collective-permute-start(bf16[32,64,256]{2,1,0:T(8,128)(2,1)S(1)} %pick.11.rest_5_), channel_id=1, source_target_pairs={{0,2},{1,3},{6,4},{7,5},{8,10},{9,11},{14,12},{15,13},{16,18},{17,... | collective-permute-start | bytes 3145736 | tf_op jit(solution)/shard_map/ppermute | solution.py:29
  102.1 26.5 %collective-permute-start.34 = (bf16[32,64,256]{2,1,0:T(8,128)(2,1)S(1)}, bf16[32,64,256]{2,1,0:T(8,128)(2,1)}, u32[]{:S(2)}, u32[]{:S(2)}) collective-permute-start(bf16[32,64,256]{2,1,0:T(8,128)(2,1)S(1)} %pick.11.rest_5_), channel_id=1, source_target_pairs={{2,4},{3,5},{4,2},{5,3},{10,12},{11,13},{12,10},{13,11},{18,20},{1... | collective-permute-start | bytes 3145736 | tf_op jit(solution)/shard_map/ppermute | solution.py:29
  116.1 9.3 %collective-permute-start.23 = (bf16[4,192,256]{2,1,0:T(8,128)(2,1)S(1)}, bf16[4,192,256]{2,1,0:T(8,128)(2,1)S(1)}, u32[]{:S(2)}, u32[]{:S(2)}) collective-permute-start(bf16[4,192,256]{2,1,0:T(8,128)(2,1)S(1)} %attend.4.rest_0_), channel_id=1, source_target_pairs={{0,1},{1,0},{2,3},{3,2},{4,5},{5,4},{6,7},{7,6},{8,24},{9,25},{10,... | collective-permute-start | bytes 1179656 | tf_op jit(solution)/shard_map/ppermute | solution.py:29
  116.2 10.6 %collective-permute-start.24 = (bf16[4,192,256]{2,1,0:T(8,128)(2,1)S(1)}, bf16[4,192,256]{2,1,0:T(8,128)(2,1)S(1)}, u32[]{:S(2)}, u32[]{:S(2)}) collective-permute-start(bf16[4,192,256]{2,1,0:T(8,128)(2,1)S(1)} %attend.4.rest_0_), channel_id=1, source_target_pairs={{0,16},{1,17},{2,18},{3,19},{4,20},{5,21},{6,22},{7,23},{8,9},{9,8... | collective-permute-start | bytes 1179656 | tf_op jit(solution)/shard_map/ppermute | solution.py:29
  126.8 6.9 %collective-permute-start.25 = (bf16[4,192,256]{2,1,0:T(8,128)(2,1)S(1)}, bf16[4,192,256]{2,1,0:T(8,128)(2,1)S(1)}, u32[]{:S(2)}, u32[]{:S(2)}) collective-permute-start(bf16[4,192,256]{2,1,0:T(8,128)(2,1)S(1)} %collective-permute-done.23.rest_1_), channel_id=1, source_target_pairs={{0,16},{1,17},{2,18},{3,19},{4,20},{5,21},{6,22},{7,23},{8,9},{9,8... | collective-permute-start | bytes 1179656 | tf_op jit(solution)/shard_map/ppermute | solution.py:29
  128.6 23.7 %collective-permute-start.36 = (bf16[32,64,256]{2,1,0:T(8,128)(2,1)S(1)}, bf16[32,64,256]{2,1,0:T(8,128)(2,1)S(1)}, u32[]{:S(2)}, u32[]{:S(2)}) collective-permute-start(bf16[32,64,256]{2,1,0:T(8,128)(2,1)S(1)} %pick.11.rest_5_), channel_id=1, source_target_pairs={{0,4},{1,5},{6,2},{7,3},{8,12},{9,13},{14,10},{15,11},{16,20},{17,... | collective-permute-start | bytes 3145736 | tf_op jit(solution)/shard_map/ppermute | solution.py:29
  136.5 7.7 %collective-permute-start.26 = (bf16[4,192,256]{2,1,0:T(8,128)(2,1)S(1)}, bf16[4,192,256]{2,1,0:T(8,128)(2,1)S(1)}, u32[]{:S(2)}, u32[]{:S(2)}) collective-permute-start(bf16[4,192,256]{2,1,0:T(8,128)(2,1)S(1)} %project_out.4.rest_0_.rest_4_), channel_id=1, source_target_pairs={{0,1},{1,0},{2,3},{3,2},{4,5},{5,4},{6,7},{7,6},{8,24},{9,25},{10,... | collective-permute-start | bytes 1179656 | tf_op jit(solution)/shard_map/ppermute | solution.py:29
  136.5 8.9 %collective-permute-start.27 = (bf16[4,192,256]{2,1,0:T(8,128)(2,1)S(1)}, bf16[4,192,256]{2,1,0:T(8,128)(2,1)S(1)}, u32[]{:S(2)}, u32[]{:S(2)}) collective-permute-start(bf16[4,192,256]{2,1,0:T(8,128)(2,1)S(1)} %project_out.4.rest_0_.rest_4_), channel_id=1, source_target_pairs={{0,16},{1,17},{2,18},{3,19},{4,20},{5,21},{6,22},{7,23},{8,9},{9,8... | collective-permute-start | bytes 1179656 | tf_op jit(solution)/shard_map/ppermute | solution.py:29
  145.4 6.9 %collective-permute-start.28 = (bf16[4,192,256]{2,1,0:T(8,128)(2,1)S(1)}, bf16[4,192,256]{2,1,0:T(8,128)(2,1)S(1)}, u32[]{:S(2)}, u32[]{:S(2)}) collective-permute-start(bf16[4,192,256]{2,1,0:T(8,128)(2,1)S(1)} %collective-permute-done.26.rest_1_), channel_id=1, source_target_pairs={{0,16},{1,17},{2,18},{3,19},{4,20},{5,21},{6,22},{7,23},{8,9},{9,8... | collective-permute-start | bytes 1179656 | tf_op jit(solution)/shard_map/ppermute | solution.py:29
  146.3 12.7 %collective-permute-start.31 = (bf16[32,64,256]{2,1,0:T(8,128)(2,1)S(1)}, bf16[32,64,256]{2,1,0:T(8,128)(2,1)S(1)}, u32[]{:S(2)}, u32[]{:S(2)}) collective-permute-start(bf16[32,64,256]{2,1,0:T(8,128)(2,1)S(1)} %pick.11.rest_5_), channel_id=1, source_target_pairs={{0,8},{1,9},{2,10},{3,11},{4,12},{5,13},{6,14},{7,15},{8,0},{9,1},... | collective-permute-start | bytes 3145736 | tf_op jit(solution)/shard_map/ppermute | solution.py:29
  149.8 10.1 %collective-permute-start.33 = (bf16[32,64,256]{2,1,0:T(8,128)(2,1)}, bf16[32,64,256]{2,1,0:T(8,128)(2,1)S(1)}, u32[]{:S(2)}, u32[]{:S(2)}) collective-permute-start(bf16[32,64,256]{2,1,0:T(8,128)(2,1)} %collective-permute-done.32.rest_7_), channel_id=1, source_target_pairs={{0,8},{1,9},{2,10},{3,11},{4,12},{5,13},{6,14},{7,15},{8,0},{9,1},... | collective-permute-start | bytes 3145736 | tf_op jit(solution)/shard_map/ppermute | solution.py:29
  149.8 10.1 %collective-permute-start.35 = (bf16[32,64,256]{2,1,0:T(8,128)(2,1)}, bf16[32,64,256]{2,1,0:T(8,128)(2,1)S(1)}, u32[]{:S(2)}, u32[]{:S(2)}) collective-permute-start(bf16[32,64,256]{2,1,0:T(8,128)(2,1)} %collective-permute-done.34.rest_9_), channel_id=1, source_target_pairs={{0,8},{1,9},{2,10},{3,11},{4,12},{5,13},{6,14},{7,15},{8,0},{9,1},... | collective-permute-start | bytes 3145736 | tf_op jit(solution)/shard_map/ppermute | solution.py:29
  152.4 7.6 %collective-permute-start.37 = (bf16[32,64,256]{2,1,0:T(8,128)(2,1)S(1)}, bf16[32,64,256]{2,1,0:T(8,128)(2,1)S(1)}, u32[]{:S(2)}, u32[]{:S(2)}) collective-permute-start(bf16[32,64,256]{2,1,0:T(8,128)(2,1)S(1)} %collective-permute-done.36.rest_11_), channel_id=1, source_target_pairs={{0,8},{1,9},{2,10},{3,11},{4,12},{5,13},{6,14},{7,15},{8,0},{9,1},... | collective-permute-start | bytes 3145736 | tf_op jit(solution)/shard_map/ppermute | solution.py:29
  155.9 25.6 %collective-permute-start.45 = (bf16[32,64,256]{2,1,0:T(8,128)(2,1)S(1)}, bf16[32,64,256]{2,1,0:T(8,128)(2,1)S(1)}, u32[]{:S(2)}, u32[]{:S(2)}) collective-permute-start(bf16[32,64,256]{2,1,0:T(8,128)(2,1)S(1)} %pick.12.rest_5_), channel_id=1, source_target_pairs={{0,2},{1,3},{6,4},{7,5},{8,10},{9,11},{14,12},{15,13},{16,18},{17,... | collective-permute-start | bytes 3145736 | tf_op jit(solution)/shard_map/ppermute | solution.py:29
  159.0 22.5 %collective-permute-start.47 = (bf16[32,64,256]{2,1,0:T(8,128)(2,1)S(1)}, bf16[32,64,256]{2,1,0:T(8,128)(2,1)S(1)}, u32[]{:S(2)}, u32[]{:S(2)}) collective-permute-start(bf16[32,64,256]{2,1,0:T(8,128)(2,1)S(1)} %pick.12.rest_5_), channel_id=1, source_target_pairs={{2,4},{3,5},{4,2},{5,3},{10,12},{11,13},{12,10},{13,11},{18,20},{1... | collective-permute-start | bytes 3145736 | tf_op jit(solution)/shard_map/ppermute | solution.py:29
  164.9 9.5 %collective-permute-start.38 = (bf16[4,192,256]{2,1,0:T(8,128)(2,1)S(1)}, bf16[4,192,256]{2,1,0:T(8,128)(2,1)S(1)}, u32[]{:S(2)}, u32[]{:S(2)}) collective-permute-start(bf16[4,192,256]{2,1,0:T(8,128)(2,1)S(1)} %get-tuple-element.71.rest_0_), channel_id=1, source_target_pairs={{0,1},{1,0},{2,3},{3,2},{4,5},{5,4},{6,7},{7,6},{8,24},{9,25},{10,... | collective-permute-start | bytes 1179656 | tf_op jit(solution)/shard_map/ppermute | solution.py:29
  165.3 10.8 %collective-permute-start.39 = (bf16[4,192,256]{2,1,0:T(8,128)(2,1)S(1)}, bf16[4,192,256]{2,1,0:T(8,128)(2,1)S(1)}, u32[]{:S(2)}, u32[]{:S(2)}) collective-permute-start(bf16[4,192,256]{2,1,0:T(8,128)(2,1)S(1)} %get-tuple-element.71.rest_0_), channel_id=1, source_target_pairs={{0,16},{1,17},{2,18},{3,19},{4,20},{5,21},{6,22},{7,23},{8,9},{9,8... | collective-permute-start | bytes 1179656 | tf_op jit(solution)/shard_map/ppermute | solution.py:29
  176.1 6.9 %collective-permute-start.40 = (bf16[4,192,256]{2,1,0:T(8,128)(2,1)S(1)}, bf16[4,192,256]{2,1,0:T(8,128)(2,1)S(1)}, u32[]{:S(2)}, u32[]{:S(2)}) collective-permute-start(bf16[4,192,256]{2,1,0:T(8,128)(2,1)S(1)} %collective-permute-done.38.rest_1_), channel_id=1, source_target_pairs={{0,16},{1,17},{2,18},{3,19},{4,20},{5,21},{6,22},{7,23},{8,9},{9,8... | collective-permute-start | bytes 1179656 | tf_op jit(solution)/shard_map/ppermute | solution.py:29
  183.0 24.9 %collective-permute-start.49 = (bf16[32,64,256]{2,1,0:T(8,128)(2,1)S(1)}, bf16[32,64,256]{2,1,0:T(8,128)(2,1)S(1)}, u32[]{:S(2)}, u32[]{:S(2)}) collective-permute-start(bf16[32,64,256]{2,1,0:T(8,128)(2,1)S(1)} %pick.12.rest_5_), channel_id=1, source_target_pairs={{0,4},{1,5},{6,2},{7,3},{8,12},{9,13},{14,10},{15,11},{16,20},{17,... | collective-permute-start | bytes 3145736 | tf_op jit(solution)/shard_map/ppermute | solution.py:29
  189.3 7.9 %collective-permute-start.41 = (bf16[4,192,256]{2,1,0:T(8,128)(2,1)S(1)}, bf16[4,192,256]{2,1,0:T(8,128)(2,1)S(1)}, u32[]{:S(2)}, u32[]{:S(2)}) collective-permute-start(bf16[4,192,256]{2,1,0:T(8,128)(2,1)S(1)} %project_out.5.rest_0_.rest_4_), channel_id=1, source_target_pairs={{0,1},{1,0},{2,3},{3,2},{4,5},{5,4},{6,7},{7,6},{8,24},{9,25},{10,... | collective-permute-start | bytes 1179656 | tf_op jit(solution)/shard_map/ppermute | solution.py:29
  190.2 9.8 %collective-permute-start.42 = (bf16[4,192,256]{2,1,0:T(8,128)(2,1)S(1)}, bf16[4,192,256]{2,1,0:T(8,128)(2,1)S(1)}, u32[]{:S(2)}, u32[]{:S(2)}) collective-permute-start(bf16[4,192,256]{2,1,0:T(8,128)(2,1)S(1)} %project_out.5.rest_0_.rest_4_), channel_id=1, source_target_pairs={{0,16},{1,17},{2,18},{3,19},{4,20},{5,21},{6,22},{7,23},{8,9},{9,8... | collective-permute-start | bytes 1179656 | tf_op jit(solution)/shard_map/ppermute | solution.py:29
  200.1 6.9 %collective-permute-start.43 = (bf16[4,192,256]{2,1,0:T(8,128)(2,1)S(1)}, bf16[4,192,256]{2,1,0:T(8,128)(2,1)S(1)}, u32[]{:S(2)}, u32[]{:S(2)}) collective-permute-start(bf16[4,192,256]{2,1,0:T(8,128)(2,1)S(1)} %collective-permute-done.41.rest_1_), channel_id=1, source_target_pairs={{0,16},{1,17},{2,18},{3,19},{4,20},{5,21},{6,22},{7,23},{8,9},{9,8... | collective-permute-start | bytes 1179656 | tf_op jit(solution)/shard_map/ppermute | solution.py:29
  200.9 14.4 %collective-permute-start.44 = (bf16[32,64,256]{2,1,0:T(8,128)(2,1)S(1)}, bf16[32,64,256]{2,1,0:T(8,128)(2,1)S(1)}, u32[]{:S(2)}, u32[]{:S(2)}) collective-permute-start(bf16[32,64,256]{2,1,0:T(8,128)(2,1)S(1)} %pick.12.rest_5_), channel_id=1, source_target_pairs={{0,8},{1,9},{2,10},{3,11},{4,12},{5,13},{6,14},{7,15},{8,0},{9,1},... | collective-permute-start | bytes 3145736 | tf_op jit(solution)/shard_map/ppermute | solution.py:29
  202.6 14.4 %collective-permute-start.46 = (bf16[32,64,256]{2,1,0:T(8,128)(2,1)S(1)}, bf16[32,64,256]{2,1,0:T(8,128)(2,1)S(1)}, u32[]{:S(2)}, u32[]{:S(2)}) collective-permute-start(bf16[32,64,256]{2,1,0:T(8,128)(2,1)S(1)} %collective-permute-done.45.rest_7_), channel_id=1, source_target_pairs={{0,8},{1,9},{2,10},{3,11},{4,12},{5,13},{6,14},{7,15},{8,0},{9,1},... | collective-permute-start | bytes 3145736 | tf_op jit(solution)/shard_map/ppermute | solution.py:29
  202.6 14.4 %collective-permute-start.48 = (bf16[32,64,256]{2,1,0:T(8,128)(2,1)S(1)}, bf16[32,64,256]{2,1,0:T(8,128)(2,1)S(1)}, u32[]{:S(2)}, u32[]{:S(2)}) collective-permute-start(bf16[32,64,256]{2,1,0:T(8,128)(2,1)S(1)} %collective-permute-done.47.rest_9_), channel_id=1, source_target_pairs={{0,8},{1,9},{2,10},{3,11},{4,12},{5,13},{6,14},{7,15},{8,0},{9,1},... | collective-permute-start | bytes 3145736 | tf_op jit(solution)/shard_map/ppermute | solution.py:29
  207.8 9.1 %collective-permute-start.50 = (bf16[32,64,256]{2,1,0:T(8,128)(2,1)S(1)}, bf16[32,64,256]{2,1,0:T(8,128)(2,1)S(1)}, u32[]{:S(2)}, u32[]{:S(2)}) collective-permute-start(bf16[32,64,256]{2,1,0:T(8,128)(2,1)S(1)} %collective-permute-done.49.rest_11_), channel_id=1, source_target_pairs={{0,8},{1,9},{2,10},{3,11},{4,12},{5,13},{6,14},{7,15},{8,0},{9,1},... | collective-permute-start | bytes 3145736 | tf_op jit(solution)/shard_map/ppermute | solution.py:29
  210.1 27.7 %collective-permute-start.58 = (bf16[32,64,256]{2,1,0:T(8,128)(2,1)S(1)}, bf16[32,64,256]{2,1,0:T(8,128)(2,1)S(1)}, u32[]{:S(2)}, u32[]{:S(2)}) collective-permute-start(bf16[32,64,256]{2,1,0:T(8,128)(2,1)S(1)} %pick.13.rest_5_), channel_id=1, source_target_pairs={{0,2},{1,3},{6,4},{7,5},{8,10},{9,11},{14,12},{15,13},{16,18},{17,... | collective-permute-start | bytes 3145736 | tf_op jit(solution)/shard_map/ppermute | solution.py:29
  215.3 22.5 %collective-permute-start.60 = (bf16[32,64,256]{2,1,0:T(8,128)(2,1)S(1)}, bf16[32,64,256]{2,1,0:T(8,128)(2,1)}, u32[]{:S(2)}, u32[]{:S(2)}) collective-permute-start(bf16[32,64,256]{2,1,0:T(8,128)(2,1)S(1)} %pick.13.rest_5_), channel_id=1, source_target_pairs={{2,4},{3,5},{4,2},{5,3},{10,12},{11,13},{12,10},{13,11},{18,20},{1... | collective-permute-start | bytes 3145736 | tf_op jit(solution)/shard_map/ppermute | solution.py:29
  222.9 9.4 %collective-permute-start.51 = (bf16[4,192,256]{2,1,0:T(8,128)(2,1)S(1)}, bf16[4,192,256]{2,1,0:T(8,128)(2,1)S(1)}, u32[]{:S(2)}, u32[]{:S(2)}) collective-permute-start(bf16[4,192,256]{2,1,0:T(8,128)(2,1)S(1)} %get-tuple-element.77.rest_0_), channel_id=1, source_target_pairs={{0,1},{1,0},{2,3},{3,2},{4,5},{5,4},{6,7},{7,6},{8,24},{9,25},{10,... | collective-permute-start | bytes 1179656 | tf_op jit(solution)/shard_map/ppermute | solution.py:29
  223.2 10.8 %collective-permute-start.52 = (bf16[4,192,256]{2,1,0:T(8,128)(2,1)S(1)}, bf16[4,192,256]{2,1,0:T(8,128)(2,1)S(1)}, u32[]{:S(2)}, u32[]{:S(2)}) collective-permute-start(bf16[4,192,256]{2,1,0:T(8,128)(2,1)S(1)} %get-tuple-element.77.rest_0_), channel_id=1, source_target_pairs={{0,16},{1,17},{2,18},{3,19},{4,20},{5,21},{6,22},{7,23},{8,9},{9,8... | collective-permute-start | bytes 1179656 | tf_op jit(solution)/shard_map/ppermute | solution.py:29
  234.0 6.9 %collective-permute-start.53 = (bf16[4,192,256]{2,1,0:T(8,128)(2,1)S(1)}, bf16[4,192,256]{2,1,0:T(8,128)(2,1)S(1)}, u32[]{:S(2)}, u32[]{:S(2)}) collective-permute-start(bf16[4,192,256]{2,1,0:T(8,128)(2,1)S(1)} %collective-permute-done.51.rest_1_), channel_id=1, source_target_pairs={{0,16},{1,17},{2,18},{3,19},{4,20},{5,21},{6,22},{7,23},{8,9},{9,8... | collective-permute-start | bytes 1179656 | tf_op jit(solution)/shard_map/ppermute | solution.py:29
  241.0 25.6 %collective-permute-start.62 = (bf16[32,64,256]{2,1,0:T(8,128)(2,1)S(1)}, bf16[32,64,256]{2,1,0:T(8,128)(2,1)}, u32[]{:S(2)}, u32[]{:S(2)}) collective-permute-start(bf16[32,64,256]{2,1,0:T(8,128)(2,1)S(1)} %pick.13.rest_5_), channel_id=1, source_target_pairs={{0,4},{1,5},{6,2},{7,3},{8,12},{9,13},{14,10},{15,11},{16,20},{17,... | collective-permute-start | bytes 3145736 | tf_op jit(solution)/shard_map/ppermute | solution.py:29
  247.0 7.8 %collective-permute-start.54 = (bf16[4,192,256]{2,1,0:T(8,128)(2,1)S(1)}, bf16[4,192,256]{2,1,0:T(8,128)(2,1)S(1)}, u32[]{:S(2)}, u32[]{:S(2)}) collective-permute-start(bf16[4,192,256]{2,1,0:T(8,128)(2,1)S(1)} %project_out.6.rest_0_.rest_4_), channel_id=1, source_target_pairs={{0,1},{1,0},{2,3},{3,2},{4,5},{5,4},{6,7},{7,6},{8,24},{9,25},{10,... | collective-permute-start | bytes 1179656 | tf_op jit(solution)/shard_map/ppermute | solution.py:29
  248.1 10.0 %collective-permute-start.55 = (bf16[4,192,256]{2,1,0:T(8,128)(2,1)S(1)}, bf16[4,192,256]{2,1,0:T(8,128)(2,1)S(1)}, u32[]{:S(2)}, u32[]{:S(2)}) collective-permute-start(bf16[4,192,256]{2,1,0:T(8,128)(2,1)S(1)} %project_out.6.rest_0_.rest_4_), channel_id=1, source_target_pairs={{0,16},{1,17},{2,18},{3,19},{4,20},{5,21},{6,22},{7,23},{8,9},{9,8... | collective-permute-start | bytes 1179656 | tf_op jit(solution)/shard_map/ppermute | solution.py:29
  258.9 6.9 %collective-permute-start.56 = (bf16[4,192,256]{2,1,0:T(8,128)(2,1)S(1)}, bf16[4,192,256]{2,1,0:T(8,128)(2,1)S(1)}, u32[]{:S(2)}, u32[]{:S(2)}) collective-permute-start(bf16[4,192,256]{2,1,0:T(8,128)(2,1)S(1)} %collective-permute-done.54.rest_1_), channel_id=1, source_target_pairs={{0,16},{1,17},{2,18},{3,19},{4,20},{5,21},{6,22},{7,23},{8,9},{9,8... | collective-permute-start | bytes 1179656 | tf_op jit(solution)/shard_map/ppermute | solution.py:29
  260.5 10.2 %collective-permute-start.57 = (bf16[32,64,256]{2,1,0:T(8,128)(2,1)S(1)}, bf16[32,64,256]{2,1,0:T(8,128)(2,1)}, u32[]{:S(2)}, u32[]{:S(2)}) collective-permute-start(bf16[32,64,256]{2,1,0:T(8,128)(2,1)S(1)} %pick.13.rest_5_), channel_id=1, source_target_pairs={{0,8},{1,9},{2,10},{3,11},{4,12},{5,13},{6,14},{7,15},{8,0},{9,1},... | collective-permute-start | bytes 3145736 | tf_op jit(solution)/shard_map/ppermute | solution.py:29
  261.9 8.8 %collective-permute-start.59 = (bf16[32,64,256]{2,1,0:T(8,128)(2,1)S(1)}, bf16[32,64,256]{2,1,0:T(8,128)(2,1)}, u32[]{:S(2)}, u32[]{:S(2)}) collective-permute-start(bf16[32,64,256]{2,1,0:T(8,128)(2,1)S(1)} %collective-permute-done.58.rest_7_), channel_id=1, source_target_pairs={{0,8},{1,9},{2,10},{3,11},{4,12},{5,13},{6,14},{7,15},{8,0},{9,1},... | collective-permute-start | bytes 3145736 | tf_op jit(solution)/shard_map/ppermute | solution.py:29
  261.9 8.8 %collective-permute-start.61 = (bf16[32,64,256]{2,1,0:T(8,128)(2,1)}, bf16[32,64,256]{2,1,0:T(8,128)(2,1)}, u32[]{:S(2)}, u32[]{:S(2)}) collective-permute-start(bf16[32,64,256]{2,1,0:T(8,128)(2,1)} %collective-permute-done.60.rest_9_), channel_id=1, source_target_pairs={{0,8},{1,9},{2,10},{3,11},{4,12},{5,13},{6,14},{7,15},{8,0},{9,1},... | collective-permute-start | bytes 3145736 | tf_op jit(solution)/shard_map/ppermute | solution.py:29
  269.0 23.1 %collective-permute-start.64 = (bf16[192,2048]{1,0:T(8,128)(2,1)}, bf16[192,2048]{1,0:T(8,128)(2,1)S(1)}, u32[]{:S(2)}, u32[]{:S(2)}) collective-permute-start(bf16[192,2048]{1,0:T(8,128)(2,1)} %copy-done.33), channel_id=1, source_target_pairs={{2,10},{3,11},{4,12},{5,13},{10,8},{11,9},{12,14},{13,15},{18,26},... | collective-permute-start | bytes 2359304 | tf_op jit(solution)/shard_map/ppermute | solution.py:29
  279.8 12.3 %collective-permute-start.65 = (bf16[192,2048]{1,0:T(8,128)(2,1)S(1)}, bf16[192,2048]{1,0:T(8,128)(2,1)S(1)}, u32[]{:S(2)}, u32[]{:S(2)}) collective-permute-start(bf16[192,2048]{1,0:T(8,128)(2,1)S(1)} %broadcast_select_fusion), channel_id=1, source_target_pairs={{2,2},{3,3},{4,4},{5,5},{10,0},{11,1},{12,6},{13,7},{18,18},{19,19... | collective-permute-start | bytes 2359304 | tf_op jit(solution)/shard_map/ppermute | solution.py:29
  280.6 8.6 %collective-permute-start.66 = (bf16[4,192,256]{2,1,0:T(8,128)(2,1)S(1)}, bf16[4,192,256]{2,1,0:T(8,128)(2,1)S(1)}, u32[]{:S(2)}, u32[]{:S(2)}) collective-permute-start(bf16[4,192,256]{2,1,0:T(8,128)(2,1)S(1)} %get-tuple-element.87.rest_0_), channel_id=1, source_target_pairs={{0,1},{1,0},{2,3},{3,2},{4,5},{5,4},{6,7},{7,6},{8,24},{9,25},{10,... | collective-permute-start | bytes 1179656 | tf_op jit(solution)/shard_map/ppermute | solution.py:29
  281.0 10.1 %collective-permute-start.67 = (bf16[4,192,256]{2,1,0:T(8,128)(2,1)S(1)}, bf16[4,192,256]{2,1,0:T(8,128)(2,1)S(1)}, u32[]{:S(2)}, u32[]{:S(2)}) collective-permute-start(bf16[4,192,256]{2,1,0:T(8,128)(2,1)S(1)} %get-tuple-element.87.rest_0_), channel_id=1, source_target_pairs={{0,16},{1,17},{2,18},{3,19},{4,20},{5,21},{6,22},{7,23},{8,9},{9,8... | collective-permute-start | bytes 1179656 | tf_op jit(solution)/shard_map/ppermute | solution.py:29
  291.1 6.9 %collective-permute-start.68 = (bf16[4,192,256]{2,1,0:T(8,128)(2,1)S(1)}, bf16[4,192,256]{2,1,0:T(8,128)(2,1)S(1)}, u32[]{:S(2)}, u32[]{:S(2)}) collective-permute-start(bf16[4,192,256]{2,1,0:T(8,128)(2,1)S(1)} %collective-permute-done.66.rest_1_), channel_id=1, source_target_pairs={{0,16},{1,17},{2,18},{3,19},{4,20},{5,21},{6,22},{7,23},{8,9},{9,8... | collective-permute-start | bytes 1179656 | tf_op jit(solution)/shard_map/ppermute | solution.py:29
  300.7 10.0 %collective-permute-start.69 = (bf16[4,192,256]{2,1,0:T(8,128)(2,1)S(1)}, bf16[4,192,256]{2,1,0:T(8,128)(2,1)S(1)}, u32[]{:S(2)}, u32[]{:S(2)}) collective-permute-start(bf16[4,192,256]{2,1,0:T(8,128)(2,1)S(1)} %project_out.7), channel_id=1, source_target_pairs={{2,26},{3,27},{4,28},{5,29},{10,24},{11,25},{12,30},{13,31}} | collective-permute-start | bytes 1179656 | tf_op jit(solution)/shard_map/ppermute | solution.py:29
  302.0 10.6 %collective-permute-start.70 = (bf16[4,192,256]{2,1,0:T(8,128)(2,1)S(1)}, bf16[4,192,256]{2,1,0:T(8,128)(2,1)S(1)}, u32[]{:S(2)}, u32[]{:S(2)}) collective-permute-start(bf16[4,192,256]{2,1,0:T(8,128)(2,1)S(1)} %project_out.7), channel_id=1, source_target_pairs={{18,26},{19,27},{20,28},{21,29},{26,24},{27,25},{28,30},{29,31}} | collective-permute-start | bytes 1179656 | tf_op jit(solution)/shard_map/ppermute | solution.py:29
  (50 other events, 407.3 us)
